TPU v7x, 32 devices: a whole 2x2x4 slice. The times are simulated.
32 devices in a mesh: gx: 4 (over y, x), gy: 8 (over z, core).
Axes of the slice: x: 2, y: 2, z: 4, core: 2. Of those that a mesh axis runs over, the one named last changes fastest.
Arguments:
- positions: bfloat16 [4, 8, 3, 128], P('gx', 'gy'), may hold values from -0.5 to 0.5
- features: bfloat16 [4, 8, 128, 128], P('gx', 'gy'), may hold values from -6 to 6
- senders: int32 [4, 8, 1, 8], P('gx', 'gy'), may hold values from 0 to 8, as said below
- counts: int32 [4, 8, 1], P('gx', 'gy'), may hold values from 1 to 5, as said below
- radial_w: float32 [2, 8, 128], replicated, may hold values from -0.36 to 0.36
- mix_w: bfloat16 [128, 128], replicated, may hold values from -0.5 to 0.5
- square_w: bfloat16 [128, 128], replicated, may hold values from -0.5 to 0.5
- cotangent: bfloat16 [4, 8, 128, 128], P('gx', 'gy'), may hold values from -6 to 6
Outputs:
- updated: bfloat16 [4, 8, 128, 128], P('gx', 'gy')
- grad_features: float32 [4, 8, 128, 128], P('gx', 'gy')
Inputs may be any that keep to these rules, and one draw needn't show every extreme that they name: `senders`: an entry g names ghost block g of the receiver's cell (see the steps); the 8 entries of one receiver block differ. Over the 1 receiver blocks of one cell the counts sum to at most 5, and some cell reaches 5 in every draw.
All inputs are finite; a program needn't handle non-finite values.
Results may differ from a plain program's by a relative error of at most 0.005.
The roundings to bfloat16 on the way count: a program that leaves them out, or rounds other values in their place, can miss the bound.
Values may be sent and summed in bfloat16 or wider, within the bound.
No kernel may reach another device: no remote copies, remote signals or barrier semaphores. Data moves between devices by JAX's collectives and lax.ppermute only.
A program may use at most 64 MiB of HBM per device.

v0:
```python
import functools

import jax
import jax.numpy as jnp
from jax import lax
from jax.experimental import pallas as pl
from jax.experimental.pallas import tpu as pltpu
from jax.sharding import PartitionSpec as P

LIVE = 5
SINE = (
    3.1415927410125732,
    -5.167712688446045,
    2.5501632690429688,
    -0.5992522239685059,
    0.08205040544271469,
    -0.00702838646247983,
)
NT = (((1,), (1,)), ((), ()))
f32 = jnp.float32
bf16 = jnp.bfloat16


def swap(block, axis, kind):
    n = lax.axis_size(axis)
    if n % 2 == 0:
        pairs = []
        for i in range(kind, n, 2):
            j = (i + 1) % n
            pairs += [(i, j), (j, i)]
    else:
        step = -1 if kind == 0 else 1
        pairs = [(i, (i + step) % n) for i in range(n)]
    return lax.ppermute(block, axis, pairs)


def swap_back(block, axis, kind):
    n = lax.axis_size(axis)
    return swap(block, axis, kind if n % 2 == 0 else 1 - kind)


def ahead(axis):
    n = lax.axis_size(axis)
    return 1 - lax.axis_index(axis) % 2 if n % 2 == 0 else jnp.int32(1)


def layer_kernel(
    meta, own_row, near_row, far_row, cot_ref, radial_ref, mix_ref, square_ref,
    updated_ref, own_out, near_out, far_out,
    basis, stacked, grads, sums, wide,
):
    rows, channels = cot_ref.shape
    degrees = radial_ref.shape[1]
    x_ahead, y_ahead = meta[0], meta[1]
    count = meta[2]

    sums[...] = jnp.zeros(sums.shape, f32)
    own_pos = own_row[1, rows:, :].astype(f32)
    own_cols = own_pos[:8].T
    recv = [jnp.broadcast_to(own_cols[:, m : m + 1], (rows, rows)) for m in range(3)]
    eye = (
        lax.broadcasted_iota(jnp.int32, (rows, rows), 0)
        == lax.broadcasted_iota(jnp.int32, (rows, rows), 1)
    ).astype(f32)

    slots, places = [], []
    for t in range(LIVE):
        ghost = meta[3 + t]
        dx, dy = ghost // 3 - 1, ghost % 3 - 1
        column = jnp.where(dx == 0, 1, jnp.where((dx == 1) == (x_ahead == 1), 0, 2))
        line = jnp.where(dy == 0, 0, jnp.where((dy == 1) == (y_ahead == 1), 1, 2))

        def fetch(ref, column=column):
            wide[...] = ref[column]

        pl.when(line == 0)(lambda: fetch(own_row))
        pl.when(line == 1)(lambda: fetch(near_row))
        pl.when(line == 2)(lambda: fetch(far_row))
        tail = wide[rows:, :].astype(f32)
        place = [
            tail[0:1] + dx.astype(f32),
            tail[1:2] + dy.astype(f32),
            tail[2:3],
        ]
        slots.append(line * 3 + column)
        places.append(place)
        feat = wide[:rows, :]
        wide_feat = feat.astype(f32)
        block = pl.ds(t * rows, rows)
        stacked[block, 0:channels] = feat
        for m in range(3):
            column_pos = jnp.broadcast_to(place[m], (rows, rows)).T
            stacked[block, (m + 1) * channels : (m + 2) * channels] = (
                column_pos[:, :channels] * wide_feat
            ).astype(bf16)

        squares = [(place[m] - recv[m]) * (place[m] - recv[m]) for m in range(3)]
        scaled = jnp.minimum(jnp.sqrt(squares[0] + squares[1] + squares[2]), 1.0)
        live = (t < count).astype(f32)
        own = (ghost == 4).astype(f32)
        envelope = (1.0 - scaled) * (1.0 - scaled) * (live - (live * own) * eye)
        shifted = scaled - 0.5
        power = shifted * shifted
        sine = jnp.full_like(power, SINE[-1])
        for factor in SINE[-2::-1]:
            sine = sine * power + factor
        cosine = -(shifted * sine)
        twice = cosine + cosine
        before, now = envelope, envelope * cosine
        for k in range(degrees):
            basis[k * rows : (k + 1) * rows, t * rows : (t + 1) * rows] = before.astype(bf16)
            before, now = now, twice * now - before

    moved = jnp.dot(basis[...], stacked[...], preferred_element_type=f32)
    sum_zero = jnp.zeros((rows, channels), f32)
    sum_one = jnp.zeros((rows, channels), f32)
    moments = [jnp.zeros((rows, channels), f32) for _ in range(3)]
    for k in range(degrees):
        part = moved[k * rows : (k + 1) * rows]
        zero, one = radial_ref[0, k : k + 1, :], radial_ref[1, k : k + 1, :]
        sum_zero += zero * part[:, :channels]
        sum_one += one * part[:, :channels]
        for m in range(3):
            moments[m] += one * part[:, (m + 1) * channels : (m + 2) * channels]

    cot = cot_ref[...]
    wide_cot = cot.astype(f32)
    cot_t = wide_cot.T
    mix, square = mix_ref[...], square_ref[...]
    square_t = square.astype(f32).T.astype(bf16)
    first = sum_zero.astype(bf16)
    second = jnp.concatenate(
        [(moments[m] - recv[m][:, :channels] * sum_one).astype(bf16) for m in range(3)], axis=0
    )
    wide_second = second.astype(f32)
    quadratic = jnp.dot(second, square, preferred_element_type=f32)
    linear = jnp.dot(first, mix, preferred_element_type=f32)
    product = quadratic * wide_second
    updated_ref[...] = (
        linear + (product[:rows] + product[rows : 2 * rows] + product[2 * rows :])
    ).astype(bf16)

    first_t = lax.dot_general(mix, cot, NT, preferred_element_type=f32)
    quadratic_t = lax.dot_general(square_t, second, NT, preferred_element_type=f32)
    weighted = jnp.concatenate(
        [(wide_cot * wide_second[m * rows : (m + 1) * rows]).astype(bf16) for m in range(3)], axis=0
    )
    pulled_t = lax.dot_general(square, weighted, NT, preferred_element_type=f32)
    second_t = [
        cot_t * quadratic_t[:, m * rows : (m + 1) * rows] + pulled_t[:, m * rows : (m + 1) * rows]
        for m in range(3)
    ]
    one_t = -(
        own_pos[0:1] * second_t[0] + own_pos[1:2] * second_t[1] + own_pos[2:3] * second_t[2]
    )
    radial_t = [radial_ref[path].T for path in range(2)]
    for k in range(degrees):
        zero, one = radial_t[0][:, k : k + 1], radial_t[1][:, k : k + 1]
        span = slice(k * rows, (k + 1) * rows)
        grads[0:channels, span] = (zero * first_t + one * one_t).astype(bf16)
        for m in range(3):
            grads[(m + 1) * channels : (m + 2) * channels, span] = (one * second_t[m]).astype(bf16)

    pulled = jnp.dot(grads[...], basis[...], preferred_element_type=f32)
    for t in range(LIVE):
        part = pulled[:, t * rows : (t + 1) * rows]
        total = part[:channels]
        for m in range(3):
            total = total + places[t][m] * part[(m + 1) * channels : (m + 2) * channels]
        sums[slots[t]] = total
    own_out[...] = sums[0:3]
    near_out[...] = sums[3:6].astype(bf16)
    far_out[...] = sums[6:9].astype(bf16)


def layer(meta, own_row, near_row, far_row, cotangent, radial_w, mix_w, square_w):
    rows, channels = cotangent.shape
    degrees = radial_w.shape[1]
    vmem = pl.BlockSpec(memory_space=pltpu.VMEM)
    packed = own_row.shape[1]
    return pl.pallas_call(
        layer_kernel,
        out_shape=(
            jax.ShapeDtypeStruct((rows, channels), bf16),
            jax.ShapeDtypeStruct((3, channels, rows), f32),
            jax.ShapeDtypeStruct((3, channels, rows), bf16),
            jax.ShapeDtypeStruct((3, channels, rows), bf16),
        ),
        in_specs=[pl.BlockSpec(memory_space=pltpu.SMEM)] + [vmem] * 7,
        out_specs=[vmem] * 4,
        scratch_shapes=[
            pltpu.VMEM((degrees * rows, LIVE * rows), bf16),
            pltpu.VMEM((LIVE * rows, 4 * channels), bf16),
            pltpu.VMEM((4 * channels, degrees * rows), bf16),
            pltpu.VMEM((9, channels, rows), f32),
            pltpu.VMEM((packed, channels), bf16),
        ],
        compiler_params=pltpu.CompilerParams(vmem_limit_bytes=40 * 2**20),
        name="layer",
    )(meta, own_row, near_row, far_row, cotangent, radial_w, mix_w, square_w)


def body(positions, features, senders, counts, radial_w, mix_w, square_w, cotangent):
    rows, channels = features.shape[2:]
    assert senders.shape[2] == 1 and rows == channels
    meta = jnp.concatenate(
        [jnp.stack([ahead("gx"), ahead("gy")]), counts.reshape(-1), senders.reshape(-1)]
    )
    packed = jnp.concatenate(
        [features[0, 0], jnp.pad(positions[0, 0], ((0, 13), (0, 0)))], axis=0
    )[None]
    own_row = jnp.concatenate([swap(packed, "gx", 0), packed, swap(packed, "gx", 1)], axis=0)
    near_row, far_row = swap(own_row, "gy", 0), swap(own_row, "gy", 1)
    updated, own_out, near_out, far_out = layer(
        meta, own_row, near_row, far_row, cotangent[0, 0], radial_w, mix_w, square_w
    )
    near_in, far_in = swap_back(near_out, "gy", 0), swap_back(far_out, "gy", 1)
    line = own_out + (near_in.astype(f32) + far_in.astype(f32))
    sent = line.astype(bf16)
    first_in, last_in = swap_back(sent[0], "gx", 0), swap_back(sent[2], "gx", 1)
    collected = (line[1] + (first_in.astype(f32) + last_in.astype(f32))).T
    return (updated[None, None], collected[None, None])


def solution(mesh):
    cell = P("gx", "gy", None, None)
    placed = (cell, cell, cell, P("gx", "gy", None), P(), P(), P(), cell)
    return jax.shard_map(
        body, mesh=mesh, in_specs=placed, out_specs=(cell, cell), check_vma=False
    )
```

profile of v0, /device:TPU:0, one launch (start us, length us, event | category | flops | bytes accessed | tf_op | source)
XLA Modules:
  0.0 33.8 jit_solution(1792654800261175928)
XLA Ops:
  0.6 0.0 copy-start.4
  0.6 0.7 %copy-done.4 = bf16[1,1,3,128]{3,2,1,0:T(4,128)(2,1)S(1)} copy-done((bf16[1,1,3,128]{3,2,1,0:T(4,128)(2,1)S(1)}, bf16[1,1,3,128]{3,2,1,0:T(4,128)(2,1)}, u32[]{:S(2)}) %copy-start.4) | copy-done | bytes 792
  1.3 0.8 %fusion.4 = bf16[1,144,128]{2,1,0:T(8,128)(2,1)S(1)} fusion(bf16[3,128]{1,0:T(4,128)(2,1)S(1)} %bitcast.27, bf16[128,128]{1,0:T(8,128)(2,1)} %bitcast.26), kind=kLoop, calls=%fused_computation.8 | loop fusion | flops 110592 | bytes 70400 | tf_op jit(solution)/shard_map/broadcast_in_dim | solution.py:209
  2.1 3.9 %collective-permute-start.1 = (bf16[1,144,128]{2,1,0:T(8,128)(2,1)S(1)}, bf16[1,144,128]{2,1,0:T(8,128)(2,1)S(1)}, u32[]{:S(2)}, u32[]{:S(2)}) collective-permute-start(bf16[1,144,128]{2,1,0:T(8,128)(2,1)S(1)} %fusion.4), channel_id=1, source_target_pairs={{8,16},{16,8},{24,0},{0,24},{9,17},{17,9},{25,1},{1,25},{10,18},{1... | collective-permute-start | bytes 110600 | tf_op jit(solution)/shard_map/ppermute | solution.py:34
  6.0 0.5 %collective-permute-start = (bf16[1,144,128]{2,1,0:T(8,128)(2,1)S(1)}, bf16[1,144,128]{2,1,0:T(8,128)(2,1)S(1)}, u32[]{:S(2)}, u32[]{:S(2)}) collective-permute-start(bf16[1,144,128]{2,1,0:T(8,128)(2,1)S(1)} %fusion.4), channel_id=1, source_target_pairs={{0,8},{8,0},{16,24},{24,16},{1,9},{9,1},{17,25},{25,17},{2,10},{10... | collective-permute-start | bytes 110600 | tf_op jit(solution)/shard_map/ppermute | solution.py:34
  7.2 0.7 %collective-permute-done.1 = bf16[1,144,128]{2,1,0:T(8,128)(2,1)S(1)} collective-permute-done((bf16[1,144,128]{2,1,0:T(8,128)(2,1)S(1)}, bf16[1,144,128]{2,1,0:T(8,128)(2,1)S(1)}, u32[]{:S(2)}, u32[]{:S(2)}) %collective-permute-start.1) | collective-permute-done | bytes 36896 | tf_op jit(solution)/shard_map/ppermute | solution.py:34
  7.9 2.0 %collective-permute-done = bf16[1,144,128]{2,1,0:T(8,128)(2,1)S(1)} collective-permute-done((bf16[1,144,128]{2,1,0:T(8,128)(2,1)S(1)}, bf16[1,144,128]{2,1,0:T(8,128)(2,1)S(1)}, u32[]{:S(2)}, u32[]{:S(2)}) %collective-permute-start) | collective-permute-done | bytes 36896 | tf_op jit(solution)/shard_map/ppermute | solution.py:34
  9.9 0.0 copy-start.5
  9.9 0.0 copy-start
  9.9 0.0 copy-start.1
  9.9 0.0 copy-start.2
  10.0 0.0 copy-start.3
  10.0 2.2 %collective-permute-start.3 = (bf16[3,144,128]{2,1,0:T(8,128)(2,1)S(1)}, bf16[3,144,128]{2,1,0:T(8,128)(2,1)S(1)}, u32[]{:S(2)}, u32[]{:S(2)}) collective-permute-start(bf16[3,144,128]{2,1,0:T(8,128)(2,1)S(1)} %pad_maximum_fusion.own_row), channel_id=1, source_target_pairs={{1,2},{2,1},{3,4},{4,3},{5,6},{6,5},{7,0},{0,7},{9,10},{10,9},{11,... | collective-permute-start | bytes 331784 | tf_op jit(solution)/shard_map/ppermute | solution.py:34
  12.1 0.0 collective-permute-start.2
  12.1 0.0 copy-done.5
  12.1 0.1 pad_add_fusion.meta
  12.2 4.7 %collective-permute-done.3.far_row = bf16[3,144,128]{2,1,0:T(8,128)(2,1)S(1)} collective-permute-done((bf16[3,144,128]{2,1,0:T(8,128)(2,1)S(1)}, bf16[3,144,128]{2,1,0:T(8,128)(2,1)S(1)}, u32[]{:S(2)}, u32[]{:S(2)}) %collective-permute-start.3) | collective-permute-done | bytes 110624 | tf_op jit(solution)/shard_map/ppermute | solution.py:34
  16.9 0.0 collective-permute-done.2.near_row
  16.9 0.0 copy-done
  16.9 0.0 copy-done.1
  16.9 0.0 copy-done.2
  16.9 0.0 copy-done.3
  17.0 4.3 %layer.1 = (bf16[128,128]{1,0:T(8,128)(2,1)}, f32[3,128,128]{2,1,0:T(8,128)S(1)}, bf16[3,128,128]{2,1,0:T(8,128)(2,1)S(1)}, bf16[3,128,128]{2,1,0:T(8,128)(2,1)S(1)}) custom-call(s32[11]{0:T(128)S(1)} %pad_add_fusion.meta, bf16[3,144,128]{2,1,0:T(8,128)(2,1)S(1)} %pad_maximum_fusion.own_row, bf16[3,144,128]{2,1,0:T(8,128)(2,1)S(1)} %collective-permute-done.2.near_row, ...), custom_call_target="tpu_custom_call" | custom-call | tf_op jit(solution)/shard_map/layer/pallas_call | solution.py:181
  21.3 0.1 collective-permute-start.4
  21.4 2.2 %collective-permute-start.5 = (bf16[3,128,128]{2,1,0:T(8,128)(2,1)S(1)}, bf16[3,128,128]{2,1,0:T(8,128)(2,1)S(1)}, u32[]{:S(2)}, u32[]{:S(2)}) collective-permute-start(bf16[3,128,128]{2,1,0:T(8,128)(2,1)S(1)} %get-tuple-element.9), channel_id=1, source_target_pairs={{1,2},{2,1},{3,4},{4,3},{5,6},{6,5},{7,0},{0,7},{9,10},{10,9},{11,... | collective-permute-start | bytes 294920 | tf_op jit(solution)/shard_map/ppermute | solution.py:34
  23.5 0.0 collective-permute-done.4
  23.5 4.1 %collective-permute-done.5 = bf16[3,128,128]{2,1,0:T(8,128)(2,1)S(1)} collective-permute-done((bf16[3,128,128]{2,1,0:T(8,128)(2,1)S(1)}, bf16[3,128,128]{2,1,0:T(8,128)(2,1)S(1)}, u32[]{:S(2)}, u32[]{:S(2)}) %collective-permute-start.5) | collective-permute-done | bytes 98336 | tf_op jit(solution)/shard_map/ppermute | solution.py:34
  27.7 0.6 %collective-permute-start.6 = (bf16[128,128]{1,0:T(8,128)(2,1)S(1)}, bf16[128,128]{1,0:T(8,128)(2,1)S(1)}, u32[]{:S(2)}, u32[]{:S(2)}) collective-permute-start(bf16[128,128]{1,0:T(8,128)(2,1)S(1)} %get-tuple-element.14), channel_id=1, source_target_pairs={{0,8},{8,0},{16,24},{24,16},{1,9},{9,1},{17,25},{25,17},{2,10},{10... | collective-permute-start | bytes 98312 | tf_op jit(solution)/shard_map/ppermute | solution.py:34
  28.3 1.4 %collective-permute-start.7 = (bf16[128,128]{1,0:T(8,128)(2,1)S(1)}, bf16[128,128]{1,0:T(8,128)(2,1)S(1)}, u32[]{:S(2)}, u32[]{:S(2)}) collective-permute-start(bf16[128,128]{1,0:T(8,128)(2,1)S(1)} %get-tuple-element.15), channel_id=1, source_target_pairs={{8,16},{16,8},{24,0},{0,24},{9,17},{17,9},{25,1},{1,25},{10,18},{1... | collective-permute-start | bytes 98312 | tf_op jit(solution)/shard_map/ppermute | solution.py:34
  29.7 1.9 %collective-permute-done.6 = bf16[128,128]{1,0:T(8,128)(2,1)S(1)} collective-permute-done((bf16[128,128]{1,0:T(8,128)(2,1)S(1)}, bf16[128,128]{1,0:T(8,128)(2,1)S(1)}, u32[]{:S(2)}, u32[]{:S(2)}) %collective-permute-start.6) | collective-permute-done | bytes 32800 | tf_op jit(solution)/shard_map/ppermute | solution.py:34
  31.7 1.4 %collective-permute-done.7 = bf16[128,128]{1,0:T(8,128)(2,1)S(1)} collective-permute-done((bf16[128,128]{1,0:T(8,128)(2,1)S(1)}, bf16[128,128]{1,0:T(8,128)(2,1)S(1)}, u32[]{:S(2)}, u32[]{:S(2)}) %collective-permute-start.7) | collective-permute-done | bytes 32800 | tf_op jit(solution)/shard_map/ppermute | solution.py:34
  33.1 0.7 %copy.10 = f32[1,1,128,128]{3,2,1,0:T(8,128)} copy(f32[1,1,128,128]{2,3,1,0:T(8,128)S(1)} %fusion.2) | data formatting | bytes 131072
  (4 shorter events, 0.1 us)
Async XLA Ops:
  0.6 0.7 %copy-start.4 = (bf16[1,1,3,128]{3,2,1,0:T(4,128)(2,1)S(1)}, bf16[1,1,3,128]{3,2,1,0:T(4,128)(2,1)}, u32[]{:S(2)}) copy-start(bf16[1,1,3,128]{3,2,1,0:T(4,128)(2,1)} %param.8) | copy-start | bytes 2308
  2.1 5.8 %collective-permute-start.1 = (bf16[1,144,128]{2,1,0:T(8,128)(2,1)S(1)}, bf16[1,144,128]{2,1,0:T(8,128)(2,1)S(1)}, u32[]{:S(2)}, u32[]{:S(2)}) collective-permute-start(bf16[1,144,128]{2,1,0:T(8,128)(2,1)S(1)} %fusion.4), channel_id=1, source_target_pairs={{8,16},{16,8},{24,0},{0,24},{9,17},{17,9},{25,1},{1,25},{10,18},{1... | collective-permute-start | bytes 110600 | tf_op jit(solution)/shard_map/ppermute | solution.py:34
  6.0 4.0 %collective-permute-start = (bf16[1,144,128]{2,1,0:T(8,128)(2,1)S(1)}, bf16[1,144,128]{2,1,0:T(8,128)(2,1)S(1)}, u32[]{:S(2)}, u32[]{:S(2)}) collective-permute-start(bf16[1,144,128]{2,1,0:T(8,128)(2,1)S(1)} %fusion.4), channel_id=1, source_target_pairs={{0,8},{8,0},{16,24},{24,16},{1,9},{9,1},{17,25},{25,17},{2,10},{10... | collective-permute-start | bytes 110600 | tf_op jit(solution)/shard_map/ppermute | solution.py:34
  9.9 2.2 %copy-start.5 = (s32[1,1,1,8]{3,2,1,0:T(1,128)S(1)}, s32[1,1,1,8]{3,2,1,0:T(1,128)}, u32[]{:S(2)}) copy-start(s32[1,1,1,8]{3,2,1,0:T(1,128)} %param.10) | copy-start | bytes 100
  9.9 7.0 %copy-start = (bf16[1,1,128,128]{3,2,1,0:T(8,128)(2,1)S(1)}, bf16[1,1,128,128]{3,2,1,0:T(8,128)(2,1)}, u32[]{:S(2)}) copy-start(bf16[1,1,128,128]{3,2,1,0:T(8,128)(2,1)} %param.15) | copy-start | bytes 98308
  9.9 7.0 %copy-start.1 = (bf16[128,128]{1,0:T(8,128)(2,1)S(1)}, bf16[128,128]{1,0:T(8,128)(2,1)}, u32[]{:S(2)}) copy-start(bf16[128,128]{1,0:T(8,128)(2,1)} %mix_ref.1) | copy-start | bytes 98308
  9.9 7.0 %copy-start.2 = (bf16[128,128]{1,0:T(8,128)(2,1)S(1)}, bf16[128,128]{1,0:T(8,128)(2,1)}, u32[]{:S(2)}) copy-start(bf16[128,128]{1,0:T(8,128)(2,1)} %square_ref.1) | copy-start | bytes 98308
  10.0 7.0 %copy-start.3 = (f32[2,8,128]{2,1,0:T(8,128)S(1)}, f32[2,8,128]{2,1,0:T(8,128)}, u32[]{:S(2)}) copy-start(f32[2,8,128]{2,1,0:T(8,128)} %radial_ref.1) | copy-start | bytes 24580
  10.0 7.0 %collective-permute-start.3 = (bf16[3,144,128]{2,1,0:T(8,128)(2,1)S(1)}, bf16[3,144,128]{2,1,0:T(8,128)(2,1)S(1)}, u32[]{:S(2)}, u32[]{:S(2)}) collective-permute-start(bf16[3,144,128]{2,1,0:T(8,128)(2,1)S(1)} %pad_maximum_fusion.own_row), channel_id=1, source_target_pairs={{1,2},{2,1},{3,4},{4,3},{5,6},{6,5},{7,0},{0,7},{9,10},{10,9},{11,... | collective-permute-start | bytes 331784 | tf_op jit(solution)/shard_map/ppermute | solution.py:34
  12.1 4.8 %collective-permute-start.2 = (bf16[3,144,128]{2,1,0:T(8,128)(2,1)S(1)}, bf16[3,144,128]{2,1,0:T(8,128)(2,1)S(1)}, u32[]{:S(2)}, u32[]{:S(2)}) collective-permute-start(bf16[3,144,128]{2,1,0:T(8,128)(2,1)S(1)} %pad_maximum_fusion.own_row), channel_id=1, source_target_pairs={{0,1},{1,0},{2,3},{3,2},{4,5},{5,4},{6,7},{7,6},{8,9},{9,8},{10,11... | collective-permute-start | bytes 331784 | tf_op jit(solution)/shard_map/ppermute | solution.py:34
  21.3 2.3 %collective-permute-start.4 = (bf16[3,128,128]{2,1,0:T(8,128)(2,1)S(1)}, bf16[3,128,128]{2,1,0:T(8,128)(2,1)S(1)}, u32[]{:S(2)}, u32[]{:S(2)}) collective-permute-start(bf16[3,128,128]{2,1,0:T(8,128)(2,1)S(1)} %get-tuple-element.8), channel_id=1, source_target_pairs={{0,1},{1,0},{2,3},{3,2},{4,5},{5,4},{6,7},{7,6},{8,9},{9,8},{10,11... | collective-permute-start | bytes 294920 | tf_op jit(solution)/shard_map/ppermute | solution.py:34
  21.4 6.3 %collective-permute-start.5 = (bf16[3,128,128]{2,1,0:T(8,128)(2,1)S(1)}, bf16[3,128,128]{2,1,0:T(8,128)(2,1)S(1)}, u32[]{:S(2)}, u32[]{:S(2)}) collective-permute-start(bf16[3,128,128]{2,1,0:T(8,128)(2,1)S(1)} %get-tuple-element.9), channel_id=1, source_target_pairs={{1,2},{2,1},{3,4},{4,3},{5,6},{6,5},{7,0},{0,7},{9,10},{10,9},{11,... | collective-permute-start | bytes 294920 | tf_op jit(solution)/shard_map/ppermute | solution.py:34
  27.7 4.0 %collective-permute-start.6 = (bf16[128,128]{1,0:T(8,128)(2,1)S(1)}, bf16[128,128]{1,0:T(8,128)(2,1)S(1)}, u32[]{:S(2)}, u32[]{:S(2)}) collective-permute-start(bf16[128,128]{1,0:T(8,128)(2,1)S(1)} %get-tuple-element.14), channel_id=1, source_target_pairs={{0,8},{8,0},{16,24},{24,16},{1,9},{9,1},{17,25},{25,17},{2,10},{10... | collective-permute-start | bytes 98312 | tf_op jit(solution)/shard_map/ppermute | solution.py:34
  28.3 4.8 %collective-permute-start.7 = (bf16[128,128]{1,0:T(8,128)(2,1)S(1)}, bf16[128,128]{1,0:T(8,128)(2,1)S(1)}, u32[]{:S(2)}, u32[]{:S(2)}) collective-permute-start(bf16[128,128]{1,0:T(8,128)(2,1)S(1)} %get-tuple-element.15), channel_id=1, source_target_pairs={{8,16},{16,8},{24,0},{0,24},{9,17},{17,9},{25,1},{1,25},{10,18},{1... | collective-permute-start | bytes 98312 | tf_op jit(solution)/shard_map/ppermute | solution.py:34
where the time goes:
time: 34.1 us; the launch traced here: 33.8 us
  waiting for transfers between devices  15 us (44%)
  starting transfers between devices  10.9 us (32%)
  Pallas kernels  4.32 us (13%)
  local copies, waits for them, and re-layouts  1.43 us (4%)
  between operations  1.37 us (4%)
  other arithmetic  0.91 us (3%)
    ppermute x8, waiting for transfers between devices, swap(): return lax.ppermute(block, axis, pairs)  15 us
    ppermute x8, starting transfers between devices, swap(): return lax.ppermute(block, axis, pairs)  10.9 us
    pallas_call x1, Pallas kernels, layer(): pl.pallas_call(layer_kernel, out_shape=(jax.ShapeDtypeStruct((rows, chann...  4.32 us
    unnamed x13, local copies, waits for them, and re-layouts  1.42 us
    broadcast_in_dim x1, other arithmetic, body(): jnp.concatenate([features[0, 0], jnp.pad(positions[0, 0], ((0, 13), (0, 0...  0.76 us
  transfers between devices with their start and end apart: 8, of which 6 were waited for; matrix products, arithmetic and copies ran while one was open for 0% of the time, Pallas kernels for 0%

commit v1 on v0

v1 whole, which is shorter than its diff:
```python
import functools

import jax
import jax.numpy as jnp
from jax import lax
from jax.experimental import pallas as pl
from jax.experimental.pallas import tpu as pltpu
from jax.sharding import PartitionSpec as P

SINE = (
    3.1415927410125732,
    -5.167712688446045,
    2.5501632690429688,
    -0.5992522239685059,
    0.08205040544271469,
    -0.00702838646247983,
)
NT = (((1,), (1,)), ((), ()))
f32 = jnp.float32
bf16 = jnp.bfloat16


def swap(block, axis, kind):
    n = lax.axis_size(axis)
    if n % 2 == 0:
        pairs = []
        for i in range(kind, n, 2):
            j = (i + 1) % n
            pairs += [(i, j), (j, i)]
    else:
        step = -1 if kind == 0 else 1
        pairs = [(i, (i + step) % n) for i in range(n)]
    return lax.ppermute(block, axis, pairs)


def swap_back(block, axis, kind):
    n = lax.axis_size(axis)
    return swap(block, axis, kind if n % 2 == 0 else 1 - kind)


def ahead(axis):
    n = lax.axis_size(axis)
    return 1 - lax.axis_index(axis) % 2 if n % 2 == 0 else jnp.int32(1)


def pack_kernel(feat_ref, pos_ref, out_ref, pos, sems):
    rows = feat_ref.shape[2]
    copies = [
        pltpu.make_async_copy(pos_ref, pos, sems.at[0]),
        pltpu.make_async_copy(feat_ref.at[0, 0], out_ref.at[0, :rows], sems.at[1]),
    ]
    for copy in copies:
        copy.start()
    copies[0].wait()
    tail = jnp.zeros((13, out_ref.shape[2]), f32)
    out_ref[0, rows:, :] = jnp.concatenate([pos[0, 0].astype(f32), tail], axis=0).astype(bf16)
    copies[1].wait()


def own_place(row, rows):
    pos = row[1, rows:, :].astype(f32)
    columns = pos[:8].T
    lines = [pos[m : m + 1] for m in range(3)]
    return lines, [jnp.broadcast_to(columns[:, m : m + 1], (rows, rows)) for m in range(3)]


def ghost_place(meta, row, line, column, rows):
    tail = row[column, rows:, :].astype(f32)
    along_x = (meta[0] * (1 - column)).astype(f32)
    along_y = (meta[1] * (0, 1, -1)[line]).astype(f32)
    return [tail[0:1] + along_x, tail[1:2] + along_y, tail[2:3]]


def add_tile(row, column, place, recv, weight, basis, stacked, at, degrees):
    rows, channels = recv[0].shape[0], row.shape[2]
    feat = row[column, :rows, :]
    wide = feat.astype(f32)
    block = slice(at * rows, (at + 1) * rows)
    stacked[block, 0:channels] = feat
    for m in range(3):
        along = jnp.broadcast_to(place[m], (rows, rows)).T
        stacked[block, (m + 1) * channels : (m + 2) * channels] = (along * wide).astype(bf16)
    squares = [(place[m] - recv[m]) * (place[m] - recv[m]) for m in range(3)]
    scaled = jnp.minimum(jnp.sqrt(squares[0] + squares[1] + squares[2]), 1.0)
    envelope = (1.0 - scaled) * (1.0 - scaled) * weight
    shifted = scaled - 0.5
    power = shifted * shifted
    sine = jnp.full_like(power, SINE[-1])
    for factor in SINE[-2::-1]:
        sine = sine * power + factor
    cosine = -(shifted * sine)
    twice = cosine + cosine
    before, now = envelope, envelope * cosine
    for k in range(degrees):
        basis[k * rows : (k + 1) * rows, block] = before.astype(bf16)
        before, now = now, twice * now - before


def gather(basis, stacked, radial_ref, sums):
    degrees = radial_ref.shape[1]
    channels = stacked.shape[1] // 4
    moved = jnp.dot(basis[...], stacked[...], preferred_element_type=f32)
    rows = moved.shape[0] // degrees
    for k in range(degrees):
        part = moved[k * rows : (k + 1) * rows]
        zero, one = radial_ref[0, k : k + 1, :], radial_ref[1, k : k + 1, :]
        lead = part[:, :channels]
        parts = [zero * lead, one * lead]
        for m in range(3):
            parts.append(one * part[:, (m + 1) * channels : (m + 2) * channels])
        sums = parts if sums is None else [a + b for a, b in zip(sums, parts)]
    return sums


def spread(grads, basis, places, outs):
    channels, rows = outs[0].shape
    pulled = jnp.dot(grads[...], basis[...], preferred_element_type=f32)
    for at, (place, out) in enumerate(zip(places, outs)):
        part = pulled[:, at * rows : (at + 1) * rows]
        total = part[:channels]
        for m in range(3):
            total = total + place[m] * part[(m + 1) * channels : (m + 2) * channels]
        out[...] = total.astype(out.dtype)


def prepare_kernel(
    cot_ref, radial_ref, mix_ref, square_ref,
    cot_out, radial_out, mix_out, square_out, cot_t_ref, square_t_ref, first_t_ref, radial_t_ref,
    sems,
):
    held = (cot_out, radial_out, mix_out, square_out)
    copies = [
        pltpu.make_async_copy(source, target, sems.at[at])
        for at, (source, target) in enumerate(
            zip((cot_ref.at[0, 0], radial_ref, mix_ref, square_ref), held)
        )
    ]
    for copy in copies:
        copy.start()
    for copy in copies:
        copy.wait()
    cot_t_ref[...] = cot_out[...].astype(f32).T
    square_t_ref[...] = square_out[...].astype(f32).T.astype(bf16)
    first_t_ref[...] = lax.dot_general(
        mix_out[...], cot_out[...], NT, preferred_element_type=f32
    )
    for path in range(2):
        radial_t_ref[path] = radial_out[path].T


def early_kernel(meta, own_row, near_row, radial_ref, basis, sums_ref, stacked):
    rows, channels = sums_ref.shape[1:]
    degrees = radial_ref.shape[1]
    _, recv = own_place(own_row, rows)
    others = (
        lax.broadcasted_iota(jnp.int32, (rows, rows), 0)
        != lax.broadcasted_iota(jnp.int32, (rows, rows), 1)
    ).astype(f32)
    for line, row in enumerate((own_row, near_row)):
        for column in range(3):
            at = line * 3 + column
            live = meta[2 + at]

            @pl.when(live == 1)
            def _(line=line, row=row, column=column, at=at):
                place = ghost_place(meta, row, line, column, rows)
                weight = others if (line, column) == (0, 1) else 1.0
                add_tile(row, column, place, recv, weight, basis, stacked, at, degrees)

            @pl.when(live == 0)
            def _(at=at):
                block = slice(at * rows, (at + 1) * rows)
                stacked[block, :] = jnp.zeros((rows, 4 * channels), bf16)
                basis[:, block] = jnp.zeros((degrees * rows, rows), bf16)

    for at, total in enumerate(gather(basis, stacked, radial_ref, None)):
        sums_ref[at] = total


def middle_kernel(
    meta, far_row, own_row, sums_ref, cot_ref, cot_t_ref, square_ref, square_t_ref, first_t_ref,
    radial_ref, radial_t_ref,
    far_out, grads, first_ref, second_ref,
    basis, stacked,
):
    rows, channels = cot_ref.shape
    degrees = radial_ref.shape[1]
    lines, recv = own_place(own_row, rows)
    places = []
    for column in range(3):
        place = ghost_place(meta, far_row, 2, column, rows)
        places.append(place)
        weight = meta[8 + column].astype(f32)
        add_tile(far_row, column, place, recv, weight, basis, stacked, column, degrees)
    totals = gather(basis, stacked, radial_ref, [sums_ref[at] for at in range(5)])
    sum_zero, sum_one, moments = totals[0], totals[1], totals[2:]
    first_ref[...] = sum_zero.astype(bf16)
    second = jnp.concatenate(
        [(moments[m] - recv[m] * sum_one).astype(bf16) for m in range(3)], axis=0
    )
    second_ref[...] = second
    wide_second = second.astype(f32)
    wide_cot, cot_t = cot_ref[...].astype(f32), cot_t_ref[...]
    quadratic_t = lax.dot_general(square_t_ref[...], second, NT, preferred_element_type=f32)
    weighted = jnp.concatenate(
        [(wide_cot * wide_second[m * rows : (m + 1) * rows]).astype(bf16) for m in range(3)], axis=0
    )
    pulled_t = lax.dot_general(square_ref[...], weighted, NT, preferred_element_type=f32)
    second_t = [
        cot_t * quadratic_t[:, m * rows : (m + 1) * rows] + pulled_t[:, m * rows : (m + 1) * rows]
        for m in range(3)
    ]
    one_t = -(lines[0] * second_t[0] + lines[1] * second_t[1] + lines[2] * second_t[2])
    first_t = first_t_ref[...]
    for k in range(degrees):
        zero, one = radial_t_ref[0, :, k : k + 1], radial_t_ref[1, :, k : k + 1]
        span = slice(k * rows, (k + 1) * rows)
        grads[0:channels, span] = (zero * first_t + one * one_t).astype(bf16)
        for m in range(3):
            grads[(m + 1) * channels : (m + 2) * channels, span] = (one * second_t[m]).astype(bf16)
    spread(grads, basis, places, [far_out.at[column] for column in range(3)])


def late_kernel(
    meta, own_row, near_row, basis, grads, first_ref, second_ref, mix_ref, square_ref,
    near_out, own_out, updated_ref,
):
    rows = first_ref.shape[0]
    places, outs = [], []
    for line, (row, out) in enumerate(((own_row, own_out), (near_row, near_out))):
        for column in range(3):
            places.append(ghost_place(meta, row, line, column, rows))
            outs.append(out.at[column])
    spread(grads, basis, places, outs)
    second = second_ref[...]
    quadratic = jnp.dot(second, square_ref[...], preferred_element_type=f32)
    linear = jnp.dot(first_ref[...], mix_ref[...], preferred_element_type=f32)
    product = quadratic * second.astype(f32)
    updated_ref[...] = (
        linear + (product[:rows] + product[rows : 2 * rows] + product[2 * rows :])
    ).astype(bf16)


def local(kernel, name, outs, scratch, meta, *args, flops=0, copies=0):
    vmem = pl.BlockSpec(memory_space=pltpu.VMEM)
    smem = pl.BlockSpec(memory_space=pltpu.SMEM)
    given = pl.BlockSpec(memory_space=pltpu.HBM) if copies else vmem
    return pl.pallas_call(
        kernel,
        out_shape=tuple(jax.ShapeDtypeStruct(*out) for out in outs),
        in_specs=([] if meta is None else [smem]) + [given] * len(args),
        out_specs=(vmem,) * len(outs),
        scratch_shapes=[pltpu.VMEM(*buffer) for buffer in scratch]
        + ([pltpu.SemaphoreType.DMA((copies,))] if copies else []),
        compiler_params=pltpu.CompilerParams(vmem_limit_bytes=32 * 2**20),
        cost_estimate=pl.CostEstimate(flops=flops, bytes_accessed=2**20, transcendentals=0),
        name=name,
    )(*(() if meta is None else (meta,)), *args)


def slot_list(senders, counts):
    dx = 2 * ahead("gx") - 1
    dy = 2 * ahead("gy") - 1
    lines = jnp.stack([jnp.zeros_like(dy), dy, -dy])
    columns = jnp.stack([dx, jnp.zeros_like(dx), -dx])
    ghosts = (3 * (columns[None, :] + 1) + lines[:, None] + 1).reshape(9, 1)
    taken = (senders == ghosts) & (jnp.arange(senders.shape[1]) < counts)
    live = jnp.any(taken, axis=1).astype(jnp.int32)
    return jnp.concatenate([jnp.stack([dx, dy]), live])


def body(positions, features, senders, counts, radial_w, mix_w, square_w, cotangent):
    rows, channels = features.shape[2:]
    degrees = radial_w.shape[1]
    assert senders.shape[2] == 1 and rows == channels
    meta = slot_list(senders[0, 0], counts[0, 0])
    square = (rows, channels)
    (packed,) = local(
        pack_kernel,
        "pack",
        [((1, rows + 16, channels), bf16)],
        [(positions.shape, bf16)],
        None, features, positions,
        copies=2,
    )
    last, first = swap(packed, "gx", 1), swap(packed, "gx", 0)
    prepared = local(
        prepare_kernel,
        "prepare",
        [
            (square, bf16),
            (radial_w.shape, f32),
            (square, bf16),
            (square, bf16),
            (square, f32),
            (square, bf16),
            (square, f32),
            ((2, channels, degrees), f32),
        ],
        [],
        None, cotangent, radial_w, mix_w, square_w,
        flops=10**8,
        copies=4,
    )
    last, first, prepared = lax.optimization_barrier((last, first, prepared))
    cot, radial_w, mix_w, square_w, cot_t, square_t, first_t, radial_t = prepared
    own_row = jnp.concatenate([first, packed, last], axis=0)
    far_row, near_row = swap(own_row, "gy", 1), swap(own_row, "gy", 0)
    basis, sums = local(
        early_kernel,
        "early",
        [((degrees * rows, 6 * rows), bf16), ((5, rows, channels), f32)],
        [((6 * rows, 4 * channels), bf16)],
        meta, own_row, near_row, radial_w,
        flops=10**9,
    )
    far_out, grads, first_bf, second_bf = local(
        middle_kernel,
        "middle",
        [
            ((3, channels, rows), bf16),
            ((4 * channels, degrees * rows), bf16),
            (square, bf16),
            ((3 * rows, channels), bf16),
        ],
        [((degrees * rows, 3 * rows), bf16), ((3 * rows, 4 * channels), bf16)],
        meta, far_row, own_row, sums, cot, cot_t, square_w, square_t, first_t, radial_w, radial_t,
        flops=10**9,
    )
    far_in = swap_back(far_out, "gy", 1)
    near_out, own_out, updated = local(
        late_kernel,
        "late",
        [((3, channels, rows), bf16), ((3, channels, rows), f32), (square, bf16)],
        [],
        meta, own_row, near_row, basis, grads, first_bf, second_bf, mix_w, square_w,
        flops=10**9,
    )
    near_in = swap_back(near_out, "gy", 0)
    far_in = lax.optimization_barrier(far_in.astype(f32))
    line = own_out + (near_in.astype(f32) + far_in)
    sent = line.astype(bf16)
    last_in, first_in = swap_back(sent[2], "gx", 1), swap_back(sent[0], "gx", 0)
    collected = (line[1] + (first_in.astype(f32) + last_in.astype(f32))).T
    return (updated[None, None], collected[None, None])


def solution(mesh):
    cell = P("gx", "gy", None, None)
    placed = (cell, cell, cell, P("gx", "gy", None), P(), P(), P(), cell)
    return jax.shard_map(
        body, mesh=mesh, in_specs=placed, out_specs=(cell, cell), check_vma=False
    )
```

time: 34.1 us -> 34.8 us (1.021)
  waiting for transfers between devices: 15 us -> 9 us
  local copies, waits for them, and re-layouts: 1.43 us -> 5.21 us
  Pallas kernels: 4.32 us -> 7.22 us
  starting transfers between devices: 10.9 us -> 10.4 us
    ppermute x8, waiting for transfers between devices: 15 us -> 9 us  [swap(): return lax.ppermute(block, axis, pairs)]
    unnamed x13, local copies, waits for them, and re-layouts: 1.42 us -> 5.12 us
    pallas_call x1 -> x5, Pallas kernels: 4.32 us -> 7.22 us  [local(): pl.pallas_call(kernel, out_shape=tuple((jax.ShapeDtypeStruct(*out) for ou...]
    broadcast_in_dim x1 -> x0, other arithmetic: 0.76 us -> none  [body(): jnp.concatenate([features[0, 0], jnp.pad(positions[0, 0], ((0, 13), (0, 0...]
    reduce_or x0 -> x1, other arithmetic: none -> 0.75 us  [slot_list(): live = jnp.any(taken, axis=1).astype(jnp.int32)]
    ppermute x8, starting transfers between devices: 10.9 us -> 10.4 us  [swap(): return lax.ppermute(block, axis, pairs)]
  transfers between devices with their start and end apart: 8 -> 8, of which waited for: 6 -> 5; matrix products, arithmetic and copies ran while one was open for 0% -> 3% of each run, Pallas kernels for 0% -> 13%
where the time goes in v1:
time: 34.8 us; the launch traced here: 34.3 us
  starting transfers between devices  10.4 us (30%)
  waiting for transfers between devices  9 us (26%)
  Pallas kernels  7.22 us (21%)
  local copies, waits for them, and re-layouts  5.21 us (15%)
  between operations  1.4 us (4%)
  other arithmetic  1.07 us (3%)
    ppermute x8, starting transfers between devices, swap(): return lax.ppermute(block, axis, pairs)  10.4 us
    ppermute x8, waiting for transfers between devices, swap(): return lax.ppermute(block, axis, pairs)  9 us
    pallas_call x5, Pallas kernels, local(): pl.pallas_call(kernel, out_shape=tuple((jax.ShapeDtypeStruct(*out) for ou...  7.22 us
    unnamed x13, local copies, waits for them, and re-layouts  5.12 us
    reduce_or x1, other arithmetic, slot_list(): live = jnp.any(taken, axis=1).astype(jnp.int32)  0.75 us
  transfers between devices with their start and end apart: 8, of which 5 were waited for; matrix products, arithmetic and copies ran while one was open for 3% of the time, Pallas kernels for 13%

profile of v1, /device:TPU:0, one launch (start us, length us, event | category | flops | bytes accessed | tf_op | source)
XLA Modules:
  0.0 34.3 jit_solution(12958280644592700782)
XLA Ops:
  0.6 0.7 %copy-done = bf16[1,1,128,128]{3,2,1,0:T(8,128)(2,1)S(1)} copy-done((bf16[1,1,128,128]{3,2,1,0:T(8,128)(2,1)S(1)}, bf16[1,1,128,128]{3,2,1,0:T(8,128)(2,1)}, u32[]{:S(2)}) %copy-start) | copy-done | bytes 32792
  1.4 0.7 %copy-done.1 = bf16[1,1,3,128]{3,2,1,0:T(4,128)(2,1)S(1)} copy-done((bf16[1,1,3,128]{3,2,1,0:T(4,128)(2,1)S(1)}, bf16[1,1,3,128]{3,2,1,0:T(4,128)(2,1)}, u32[]{:S(2)}) %copy-start.1) | copy-done | bytes 792
  2.1 3.0 %collective-permute-start.1 = (bf16[1,144,128]{2,1,0:T(8,128)(2,1)S(1)}, bf16[1,144,128]{2,1,0:T(8,128)(2,1)S(1)}, u32[]{:S(2)}, u32[]{:S(2)}) collective-permute-start(bf16[1,144,128]{2,1,0:T(8,128)(2,1)S(1)} %pack.1), channel_id=1, source_target_pairs={{0,8},{8,0},{16,24},{24,16},{1,9},{9,1},{17,25},{25,17},{2,10},{10... | collective-permute-start | bytes 110600 | tf_op jit(solution)/shard_map/ppermute | solution.py:33
  5.1 1.5 %collective-permute-start = (bf16[1,144,128]{2,1,0:T(8,128)(2,1)S(1)}, bf16[1,144,128]{2,1,0:T(8,128)(2,1)S(1)}, u32[]{:S(2)}, u32[]{:S(2)}) collective-permute-start(bf16[1,144,128]{2,1,0:T(8,128)(2,1)S(1)} %pack.1), channel_id=1, source_target_pairs={{8,16},{16,8},{24,0},{0,24},{9,17},{17,9},{25,1},{1,25},{10,18},{1... | collective-permute-start | bytes 110600 | tf_op jit(solution)/shard_map/ppermute | solution.py:33
  7.3 0.1 fusion.2
  7.4 0.1 add_add_fusion.1
  7.4 0.1 add.64
  7.5 0.7 %and_reduce_fusion = pred[9]{0:T(512)(128)(4,1)S(1)} fusion(s32[9]{0:T(128)S(1)} %add.64, s32[8]{0:T(128)} %bitcast.22, pred[8]{0:T(512)(128)(4,1)S(1)} %iota_compare_fusion), kind=kLoop, calls=%fused_computation.7 | loop fusion | flops 207 | bytes 85 | tf_op jit(solution)/shard_map/reduce_or | solution.py:268
  8.3 0.7 %copy-done.2 = bf16[1,1,128,128]{3,2,1,0:T(8,128)(2,1)S(1)} copy-done((bf16[1,1,128,128]{3,2,1,0:T(8,128)(2,1)S(1)}, bf16[1,1,128,128]{3,2,1,0:T(8,128)(2,1)}, u32[]{:S(2)}) %copy-start.2) | copy-done | bytes 32792
  9.0 0.8 %copy-done.3 = bf16[128,128]{1,0:T(8,128)(2,1)S(1)} copy-done((bf16[128,128]{1,0:T(8,128)(2,1)S(1)}, bf16[128,128]{1,0:T(8,128)(2,1)}, u32[]{:S(2)}) %copy-start.3) | copy-done | bytes 32792
  9.8 0.8 %copy-done.4 = bf16[128,128]{1,0:T(8,128)(2,1)S(1)} copy-done((bf16[128,128]{1,0:T(8,128)(2,1)S(1)}, bf16[128,128]{1,0:T(8,128)(2,1)}, u32[]{:S(2)}) %copy-start.4) | copy-done | bytes 32792
  10.6 0.7 %copy-done.5 = f32[2,8,128]{2,1,0:T(8,128)S(1)} copy-done((f32[2,8,128]{2,1,0:T(8,128)S(1)}, f32[2,8,128]{2,1,0:T(8,128)}, u32[]{:S(2)}) %copy-start.5) | copy-done | bytes 8216
  11.2 0.3 prepare.1
  11.6 0.0 collective-permute-done.1
  11.6 0.0 collective-permute-done
  11.6 2.5 %collective-permute-start.3 = (bf16[3,144,128]{2,1,0:T(8,128)(2,1)S(1)}, bf16[3,144,128]{2,1,0:T(8,128)(2,1)S(1)}, u32[]{:S(2)}, u32[]{:S(2)}) collective-permute-start(bf16[3,144,128]{2,1,0:T(8,128)(2,1)S(1)} %pad_maximum_fusion.own_row), channel_id=1, source_target_pairs={{1,2},{2,1},{3,4},{4,3},{5,6},{6,5},{7,0},{0,7},{9,10},{10,9},{11,... | collective-permute-start | bytes 331784 | tf_op jit(solution)/shard_map/ppermute | solution.py:33
  14.1 0.0 collective-permute-start.2
  14.1 0.1 pad_add_fusion.1.meta
  14.2 1.2 %collective-permute-done.2.near_row = bf16[3,144,128]{2,1,0:T(8,128)(2,1)S(1)} collective-permute-done((bf16[3,144,128]{2,1,0:T(8,128)(2,1)S(1)}, bf16[3,144,128]{2,1,0:T(8,128)(2,1)S(1)}, u32[]{:S(2)}, u32[]{:S(2)}) %collective-permute-start.2) | collective-permute-done | bytes 110624 | tf_op jit(solution)/shard_map/ppermute | solution.py:33
  15.5 2.0 %early.1 = (bf16[1024,768]{1,0:T(8,128)(2,1)S(1)}, f32[5,128,128]{2,1,0:T(8,128)S(1)}) custom-call(s32[11]{0:T(128)S(1)} %pad_add_fusion.1.meta, bf16[3,144,128]{2,1,0:T(8,128)(2,1)S(1)} %pad_maximum_fusion.own_row, bf16[3,144,128]{2,1,0:T(8,128)(2,1)S(1)} %collective-permute-done.2.near_row, f32[2,8,128]{2,1,0:T(8,128)S(1)} %get-tuple-element.39.radial_ref), custom_call_target="tpu_custom_call" | custom-call | flops 1000000000 | bytes 1048576 | tf_op jit(solution)/shard_map/early/pallas_call | solution.py:248
  17.5 1.1 %collective-permute-done.3.far_row = bf16[3,144,128]{2,1,0:T(8,128)(2,1)S(1)} collective-permute-done((bf16[3,144,128]{2,1,0:T(8,128)(2,1)S(1)}, bf16[3,144,128]{2,1,0:T(8,128)(2,1)S(1)}, u32[]{:S(2)}, u32[]{:S(2)}) %collective-permute-start.3) | collective-permute-done | bytes 110624 | tf_op jit(solution)/shard_map/ppermute | solution.py:33
  18.6 2.7 %middle.1 = (bf16[3,128,128]{2,1,0:T(8,128)(2,1)S(1)}, bf16[512,1024]{1,0:T(8,128)(2,1)S(1)}, bf16[128,128]{1,0:T(8,128)(2,1)S(1)}, bf16[384,128]{1,0:T(8,128)(2,1)S(1)}) custom-call(s32[11]{0:T(128)S(1)} %pad_add_fusion.1.meta, bf16[3,144,128]{2,1,0:T(8,128)(2,1)S(1)} %collective-permute-done.3.far_row, bf16[3,144,128]{2,1,0:T(8,128)(2,1)S(1)} %pad_maximum_fusion.own_row, ...), custom_call_target="tpu_custom_call" | custom-call | flops 1000000000 | bytes 1048576 | tf_op jit(solution)/shard_map/middle/pallas_call | solution.py:248
  21.2 1.6 %collective-permute-start.5 = (bf16[3,128,128]{2,1,0:T(8,128)(2,1)S(1)}, bf16[3,128,128]{2,1,0:T(8,128)(2,1)S(1)}, u32[]{:S(2)}, u32[]{:S(2)}) collective-permute-start(bf16[3,128,128]{2,1,0:T(8,128)(2,1)S(1)} %get-tuple-element.55), channel_id=1, source_target_pairs={{1,2},{2,1},{3,4},{4,3},{5,6},{6,5},{7,0},{0,7},{9,10},{10,9},{11,... | collective-permute-start | bytes 294920 | tf_op jit(solution)/shard_map/ppermute | solution.py:33
  22.9 2.2 %late.1 = (bf16[3,128,128]{2,1,0:T(8,128)(2,1)S(1)}, f32[3,128,128]{2,1,0:T(8,128)S(1)}, bf16[128,128]{1,0:T(8,128)(2,1)}) custom-call(s32[11]{0:T(128)S(1)} %pad_add_fusion.1.meta, bf16[3,144,128]{2,1,0:T(8,128)(2,1)S(1)} %pad_maximum_fusion.own_row, bf16[3,144,128]{2,1,0:T(8,128)(2,1)S(1)} %collective-permute-done.2.near_row, ...), custom_call_target="tpu_custom_call" | custom-call | flops 1000000000 | bytes 1048576 | tf_op jit(solution)/shard_map/late/pallas_call | solution.py:248
  25.1 0.0 collective-permute-start.4
  25.1 2.1 %collective-permute-done.5 = bf16[3,128,128]{2,1,0:T(8,128)(2,1)S(1)} collective-permute-done((bf16[3,128,128]{2,1,0:T(8,128)(2,1)S(1)}, bf16[3,128,128]{2,1,0:T(8,128)(2,1)S(1)}, u32[]{:S(2)}, u32[]{:S(2)}) %collective-permute-start.5) | collective-permute-done | bytes 98336 | tf_op jit(solution)/shard_map/ppermute | solution.py:33
  27.2 0.0 collective-permute-done.4
  27.2 1.6 %collective-permute-start.6 = (bf16[128,128]{1,0:T(8,128)(2,1)S(1)}, bf16[128,128]{1,0:T(8,128)(2,1)S(1)}, u32[]{:S(2)}, u32[]{:S(2)}) collective-permute-start(bf16[128,128]{1,0:T(8,128)(2,1)S(1)} %get-tuple-element.62), channel_id=1, source_target_pairs={{0,8},{8,0},{16,24},{24,16},{1,9},{9,1},{17,25},{25,17},{2,10},{10... | collective-permute-start | bytes 98312 | tf_op jit(solution)/shard_map/ppermute | solution.py:33
  28.8 0.2 collective-permute-start.7
  29.0 2.2 %collective-permute-done.6 = bf16[128,128]{1,0:T(8,128)(2,1)S(1)} collective-permute-done((bf16[128,128]{1,0:T(8,128)(2,1)S(1)}, bf16[128,128]{1,0:T(8,128)(2,1)S(1)}, u32[]{:S(2)}, u32[]{:S(2)}) %collective-permute-start.6) | collective-permute-done | bytes 32800 | tf_op jit(solution)/shard_map/ppermute | solution.py:33
  31.2 2.4 %collective-permute-done.7 = bf16[128,128]{1,0:T(8,128)(2,1)S(1)} collective-permute-done((bf16[128,128]{1,0:T(8,128)(2,1)S(1)}, bf16[128,128]{1,0:T(8,128)(2,1)S(1)}, u32[]{:S(2)}, u32[]{:S(2)}) %collective-permute-start.7) | collective-permute-done | bytes 32800 | tf_op jit(solution)/shard_map/ppermute | solution.py:33
  33.6 0.7 %copy.11 = f32[1,1,128,128]{3,2,1,0:T(8,128)} copy(f32[1,1,128,128]{2,3,1,0:T(8,128)S(1)} %fusion.1) | data formatting | bytes 131072
  (14 shorter events, 0.2 us)
Async XLA Ops:
  0.6 0.8 %copy-start = (bf16[1,1,128,128]{3,2,1,0:T(8,128)(2,1)S(1)}, bf16[1,1,128,128]{3,2,1,0:T(8,128)(2,1)}, u32[]{:S(2)}) copy-start(bf16[1,1,128,128]{3,2,1,0:T(8,128)(2,1)} %feat_ref.1) | copy-start | bytes 98308
  1.4 0.7 %copy-start.1 = (bf16[1,1,3,128]{3,2,1,0:T(4,128)(2,1)S(1)}, bf16[1,1,3,128]{3,2,1,0:T(4,128)(2,1)}, u32[]{:S(2)}) copy-start(bf16[1,1,3,128]{3,2,1,0:T(4,128)(2,1)} %pos_ref.1) | copy-start | bytes 2308
  2.1 9.4 %collective-permute-start.1 = (bf16[1,144,128]{2,1,0:T(8,128)(2,1)S(1)}, bf16[1,144,128]{2,1,0:T(8,128)(2,1)S(1)}, u32[]{:S(2)}, u32[]{:S(2)}) collective-permute-start(bf16[1,144,128]{2,1,0:T(8,128)(2,1)S(1)} %pack.1), channel_id=1, source_target_pairs={{0,8},{8,0},{16,24},{24,16},{1,9},{9,1},{17,25},{25,17},{2,10},{10... | collective-permute-start | bytes 110600 | tf_op jit(solution)/shard_map/ppermute | solution.py:33
  5.1 6.4 %collective-permute-start = (bf16[1,144,128]{2,1,0:T(8,128)(2,1)S(1)}, bf16[1,144,128]{2,1,0:T(8,128)(2,1)S(1)}, u32[]{:S(2)}, u32[]{:S(2)}) collective-permute-start(bf16[1,144,128]{2,1,0:T(8,128)(2,1)S(1)} %pack.1), channel_id=1, source_target_pairs={{8,16},{16,8},{24,0},{0,24},{9,17},{17,9},{25,1},{1,25},{10,18},{1... | collective-permute-start | bytes 110600 | tf_op jit(solution)/shard_map/ppermute | solution.py:33
  8.3 0.8 %copy-start.2 = (bf16[1,1,128,128]{3,2,1,0:T(8,128)(2,1)S(1)}, bf16[1,1,128,128]{3,2,1,0:T(8,128)(2,1)}, u32[]{:S(2)}) copy-start(bf16[1,1,128,128]{3,2,1,0:T(8,128)(2,1)} %cot_ref.1) | copy-start | bytes 98308
  9.0 0.8 %copy-start.3 = (bf16[128,128]{1,0:T(8,128)(2,1)S(1)}, bf16[128,128]{1,0:T(8,128)(2,1)}, u32[]{:S(2)}) copy-start(bf16[128,128]{1,0:T(8,128)(2,1)} %mix_ref.1) | copy-start | bytes 98308
  9.8 0.8 %copy-start.4 = (bf16[128,128]{1,0:T(8,128)(2,1)S(1)}, bf16[128,128]{1,0:T(8,128)(2,1)}, u32[]{:S(2)}) copy-start(bf16[128,128]{1,0:T(8,128)(2,1)} %square_ref.1) | copy-start | bytes 98308
  10.5 0.7 %copy-start.5 = (f32[2,8,128]{2,1,0:T(8,128)S(1)}, f32[2,8,128]{2,1,0:T(8,128)}, u32[]{:S(2)}) copy-start(f32[2,8,128]{2,1,0:T(8,128)} %radial_ref.1) | copy-start | bytes 24580
  11.6 7.0 %collective-permute-start.3 = (bf16[3,144,128]{2,1,0:T(8,128)(2,1)S(1)}, bf16[3,144,128]{2,1,0:T(8,128)(2,1)S(1)}, u32[]{:S(2)}, u32[]{:S(2)}) collective-permute-start(bf16[3,144,128]{2,1,0:T(8,128)(2,1)S(1)} %pad_maximum_fusion.own_row), channel_id=1, source_target_pairs={{1,2},{2,1},{3,4},{4,3},{5,6},{6,5},{7,0},{0,7},{9,10},{10,9},{11,... | collective-permute-start | bytes 331784 | tf_op jit(solution)/shard_map/ppermute | solution.py:33
  14.1 1.3 %collective-permute-start.2 = (bf16[3,144,128]{2,1,0:T(8,128)(2,1)S(1)}, bf16[3,144,128]{2,1,0:T(8,128)(2,1)S(1)}, u32[]{:S(2)}, u32[]{:S(2)}) collective-permute-start(bf16[3,144,128]{2,1,0:T(8,128)(2,1)S(1)} %pad_maximum_fusion.own_row), channel_id=1, source_target_pairs={{0,1},{1,0},{2,3},{3,2},{4,5},{5,4},{6,7},{7,6},{8,9},{9,8},{10,11... | collective-permute-start | bytes 331784 | tf_op jit(solution)/shard_map/ppermute | solution.py:33
  21.2 5.9 %collective-permute-start.5 = (bf16[3,128,128]{2,1,0:T(8,128)(2,1)S(1)}, bf16[3,128,128]{2,1,0:T(8,128)(2,1)S(1)}, u32[]{:S(2)}, u32[]{:S(2)}) collective-permute-start(bf16[3,128,128]{2,1,0:T(8,128)(2,1)S(1)} %get-tuple-element.55), channel_id=1, source_target_pairs={{1,2},{2,1},{3,4},{4,3},{5,6},{6,5},{7,0},{0,7},{9,10},{10,9},{11,... | collective-permute-start | bytes 294920 | tf_op jit(solution)/shard_map/ppermute | solution.py:33
  25.1 2.1 %collective-permute-start.4 = (bf16[3,128,128]{2,1,0:T(8,128)(2,1)S(1)}, bf16[3,128,128]{2,1,0:T(8,128)(2,1)S(1)}, u32[]{:S(2)}, u32[]{:S(2)}) collective-permute-start(bf16[3,128,128]{2,1,0:T(8,128)(2,1)S(1)} %get-tuple-element.54), channel_id=1, source_target_pairs={{0,1},{1,0},{2,3},{3,2},{4,5},{5,4},{6,7},{7,6},{8,9},{9,8},{10,11... | collective-permute-start | bytes 294920 | tf_op jit(solution)/shard_map/ppermute | solution.py:33
  27.2 4.0 %collective-permute-start.6 = (bf16[128,128]{1,0:T(8,128)(2,1)S(1)}, bf16[128,128]{1,0:T(8,128)(2,1)S(1)}, u32[]{:S(2)}, u32[]{:S(2)}) collective-permute-start(bf16[128,128]{1,0:T(8,128)(2,1)S(1)} %get-tuple-element.62), channel_id=1, source_target_pairs={{0,8},{8,0},{16,24},{24,16},{1,9},{9,1},{17,25},{25,17},{2,10},{10... | collective-permute-start | bytes 98312 | tf_op jit(solution)/shard_map/ppermute | solution.py:33
  28.8 4.8 %collective-permute-start.7 = (bf16[128,128]{1,0:T(8,128)(2,1)S(1)}, bf16[128,128]{1,0:T(8,128)(2,1)S(1)}, u32[]{:S(2)}, u32[]{:S(2)}) collective-permute-start(bf16[128,128]{1,0:T(8,128)(2,1)S(1)} %get-tuple-element.63), channel_id=1, source_target_pairs={{8,16},{16,8},{24,0},{0,24},{9,17},{17,9},{25,1},{1,25},{10,18},{1... | collective-permute-start | bytes 98312 | tf_op jit(solution)/shard_map/ppermute | solution.py:33

commit v2 on v1

--- a/solution.py
+++ b/solution.py
@@ -57,23 +57,23 @@
     copies[1].wait()
 
 
-def own_place(row, rows):
-    pos = row[1, rows:, :].astype(f32)
+def own_place(own_row, rows):
+    pos = own_row[1, rows:, :].astype(f32)
     columns = pos[:8].T
     lines = [pos[m : m + 1] for m in range(3)]
     return lines, [jnp.broadcast_to(columns[:, m : m + 1], (rows, rows)) for m in range(3)]
 
 
-def ghost_place(meta, row, line, column, rows):
-    tail = row[column, rows:, :].astype(f32)
+def ghost_place(meta, block, line, column):
+    tail = block[block.shape[0] - 16 :, :].astype(f32)
     along_x = (meta[0] * (1 - column)).astype(f32)
     along_y = (meta[1] * (0, 1, -1)[line]).astype(f32)
     return [tail[0:1] + along_x, tail[1:2] + along_y, tail[2:3]]
 
 
-def add_tile(row, column, place, recv, weight, basis, stacked, at, degrees):
-    rows, channels = recv[0].shape[0], row.shape[2]
-    feat = row[column, :rows, :]
+def add_tile(source, place, recv, weight, basis, stacked, at, degrees):
+    rows, channels = recv[0].shape[0], source.shape[1]
+    feat = source[:rows, :]
     wide = feat.astype(f32)
     block = slice(at * rows, (at + 1) * rows)
     stacked[block, 0:channels] = feat
@@ -124,20 +124,32 @@
 
 
 def prepare_kernel(
-    cot_ref, radial_ref, mix_ref, square_ref,
-    cot_out, radial_out, mix_out, square_out, cot_t_ref, square_t_ref, first_t_ref, radial_t_ref,
-    sems,
+    ways, counts, senders_ref, cot_ref, radial_ref, mix_ref, square_ref,
+    meta, cot_out, radial_out, mix_out, square_out, cot_t_ref, square_t_ref, first_t_ref,
+    radial_t_ref,
+    senders, sems,
 ):
-    held = (cot_out, radial_out, mix_out, square_out)
+    held = (senders, cot_out, radial_out, mix_out, square_out)
+    given = (senders_ref, cot_ref.at[0, 0], radial_ref, mix_ref, square_ref)
     copies = [
         pltpu.make_async_copy(source, target, sems.at[at])
-        for at, (source, target) in enumerate(
-            zip((cot_ref.at[0, 0], radial_ref, mix_ref, square_ref), held)
-        )
+        for at, (source, target) in enumerate(zip(given, held))
     ]
     for copy in copies:
         copy.start()
-    for copy in copies:
+    dx, dy = ways[0], ways[1]
+    meta[0] = dx
+    meta[1] = dy
+    copies[0].wait()
+    count = counts[0, 0, 0]
+    for line in range(3):
+        for column in range(3):
+            ghost = 3 * (dx * (1 - column) + 1) + dy * (0, 1, -1)[line] + 1
+            live = jnp.int32(0)
+            for t in range(senders.shape[3]):
+                live = live | ((t < count) & (senders[0, 0, 0, t] == ghost)).astype(jnp.int32)
+            meta[2 + line * 3 + column] = live
+    for copy in copies[1:]:
         copy.wait()
     cot_t_ref[...] = cot_out[...].astype(f32).T
     square_t_ref[...] = square_out[...].astype(f32).T.astype(bf16)
@@ -146,6 +158,14 @@
     )
     for path in range(2):
         radial_t_ref[path] = radial_out[path].T
+
+
+EARLY = ((0, 0), (0, 1), (0, 2), (1, 0), (1, 1), (1, 2))
+FAR = ((2, 0), (2, 1), (2, 2))
+
+
+def early_blocks(own_row, near_row):
+    return [own_row.at[c] for c in range(3)] + [near_row.at[c] for c in range(3)]
 
 
 def early_kernel(meta, own_row, near_row, radial_ref, basis, sums_ref, stacked):
@@ -156,30 +176,30 @@
         lax.broadcasted_iota(jnp.int32, (rows, rows), 0)
         != lax.broadcasted_iota(jnp.int32, (rows, rows), 1)
     ).astype(f32)
-    for line, row in enumerate((own_row, near_row)):
-        for column in range(3):
-            at = line * 3 + column
-            live = meta[2 + at]
-
-            @pl.when(live == 1)
-            def _(line=line, row=row, column=column, at=at):
-                place = ghost_place(meta, row, line, column, rows)
-                weight = others if (line, column) == (0, 1) else 1.0
-                add_tile(row, column, place, recv, weight, basis, stacked, at, degrees)
-
-            @pl.when(live == 0)
-            def _(at=at):
-                block = slice(at * rows, (at + 1) * rows)
-                stacked[block, :] = jnp.zeros((rows, 4 * channels), bf16)
-                basis[:, block] = jnp.zeros((degrees * rows, rows), bf16)
+    for at, ((line, column), source) in enumerate(
+        zip(EARLY, early_blocks(own_row, near_row))
+    ):
+        live = meta[2 + line * 3 + column]
+
+        @pl.when(live == 1)
+        def _(line=line, column=column, source=source, at=at):
+            place = ghost_place(meta, source, line, column)
+            weight = others if (line, column) == (0, 1) else 1.0
+            add_tile(source, place, recv, weight, basis, stacked, at, degrees)
+
+        @pl.when(live == 0)
+        def _(at=at):
+            block = slice(at * rows, (at + 1) * rows)
+            stacked[block, :] = jnp.zeros((rows, 4 * channels), bf16)
+            basis[:, block] = jnp.zeros((degrees * rows, rows), bf16)
 
     for at, total in enumerate(gather(basis, stacked, radial_ref, None)):
         sums_ref[at] = total
 
 
 def middle_kernel(
-    meta, far_row, own_row, sums_ref, cot_ref, cot_t_ref, square_ref, square_t_ref, first_t_ref,
-    radial_ref, radial_t_ref,
+    meta, far_row, own_row, sums_ref, cot_ref, cot_t_ref, square_ref,
+    square_t_ref, first_t_ref, radial_ref, radial_t_ref,
     far_out, grads, first_ref, second_ref,
     basis, stacked,
 ):
@@ -187,11 +207,11 @@
     degrees = radial_ref.shape[1]
     lines, recv = own_place(own_row, rows)
     places = []
-    for column in range(3):
-        place = ghost_place(meta, far_row, 2, column, rows)
-        places.append(place)
-        weight = meta[8 + column].astype(f32)
-        add_tile(far_row, column, place, recv, weight, basis, stacked, column, degrees)
+    for at, (line, column) in enumerate(FAR):
+        source = far_row.at[column]
+        places.append(ghost_place(meta, source, line, column))
+        weight = meta[2 + line * 3 + column].astype(f32)
+        add_tile(source, places[at], recv, weight, basis, stacked, at, degrees)
     totals = gather(basis, stacked, radial_ref, [sums_ref[at] for at in range(5)])
     sum_zero, sum_one, moments = totals[0], totals[1], totals[2:]
     first_ref[...] = sum_zero.astype(bf16)
@@ -218,7 +238,7 @@
         grads[0:channels, span] = (zero * first_t + one * one_t).astype(bf16)
         for m in range(3):
             grads[(m + 1) * channels : (m + 2) * channels, span] = (one * second_t[m]).astype(bf16)
-    spread(grads, basis, places, [far_out.at[column] for column in range(3)])
+    spread(grads, basis, places, [far_out.at[column] for _, column in FAR])
 
 
 def late_kernel(
@@ -226,11 +246,9 @@
     near_out, own_out, updated_ref,
 ):
     rows = first_ref.shape[0]
-    places, outs = [], []
-    for line, (row, out) in enumerate(((own_row, own_out), (near_row, near_out))):
-        for column in range(3):
-            places.append(ghost_place(meta, row, line, column, rows))
-            outs.append(out.at[column])
+    sources = early_blocks(own_row, near_row)
+    places = [ghost_place(meta, source, *slot) for slot, source in zip(EARLY, sources)]
+    outs = [own_out.at[c] for c in range(3)] + [near_out.at[c] for c in range(3)]
     spread(grads, basis, places, outs)
     second = second_ref[...]
     quadratic = jnp.dot(second, square_ref[...], preferred_element_type=f32)
@@ -241,46 +259,40 @@
     ).astype(bf16)
 
 
-def local(kernel, name, outs, scratch, meta, *args, flops=0, copies=0):
-    vmem = pl.BlockSpec(memory_space=pltpu.VMEM)
-    smem = pl.BlockSpec(memory_space=pltpu.SMEM)
-    given = pl.BlockSpec(memory_space=pltpu.HBM) if copies else vmem
+def local(kernel, name, outs, scratch, args, flops=0, smem=0, smem_outs=0, copies=0):
+    in_vmem = pl.BlockSpec(memory_space=pltpu.VMEM)
+    in_smem = pl.BlockSpec(memory_space=pltpu.SMEM)
+    given = in_vmem
+    if copies:
+        given = pl.BlockSpec(memory_space=pltpu.HBM)
+        args = args[:smem] + tuple(
+            pltpu.with_memory_space_constraint(arg, pltpu.HBM) for arg in args[smem:]
+        )
     return pl.pallas_call(
         kernel,
         out_shape=tuple(jax.ShapeDtypeStruct(*out) for out in outs),
-        in_specs=([] if meta is None else [smem]) + [given] * len(args),
-        out_specs=(vmem,) * len(outs),
-        scratch_shapes=[pltpu.VMEM(*buffer) for buffer in scratch]
+        in_specs=[in_smem] * smem + [given] * (len(args) - smem),
+        out_specs=(in_smem,) * smem_outs + (in_vmem,) * (len(outs) - smem_outs),
+        scratch_shapes=scratch
         + ([pltpu.SemaphoreType.DMA((copies,))] if copies else []),
         compiler_params=pltpu.CompilerParams(vmem_limit_bytes=32 * 2**20),
         cost_estimate=pl.CostEstimate(flops=flops, bytes_accessed=2**20, transcendentals=0),
         name=name,
-    )(*(() if meta is None else (meta,)), *args)
-
-
-def slot_list(senders, counts):
-    dx = 2 * ahead("gx") - 1
-    dy = 2 * ahead("gy") - 1
-    lines = jnp.stack([jnp.zeros_like(dy), dy, -dy])
-    columns = jnp.stack([dx, jnp.zeros_like(dx), -dx])
-    ghosts = (3 * (columns[None, :] + 1) + lines[:, None] + 1).reshape(9, 1)
-    taken = (senders == ghosts) & (jnp.arange(senders.shape[1]) < counts)
-    live = jnp.any(taken, axis=1).astype(jnp.int32)
-    return jnp.concatenate([jnp.stack([dx, dy]), live])
+    )(*args)
 
 
 def body(positions, features, senders, counts, radial_w, mix_w, square_w, cotangent):
     rows, channels = features.shape[2:]
     degrees = radial_w.shape[1]
     assert senders.shape[2] == 1 and rows == channels
-    meta = slot_list(senders[0, 0], counts[0, 0])
+    ways = jnp.stack([2 * ahead("gx") - 1, 2 * ahead("gy") - 1])
     square = (rows, channels)
     (packed,) = local(
         pack_kernel,
         "pack",
         [((1, rows + 16, channels), bf16)],
-        [(positions.shape, bf16)],
-        None, features, positions,
+        [pltpu.VMEM(positions.shape, bf16)],
+        (features, positions),
         copies=2,
     )
     last, first = swap(packed, "gx", 1), swap(packed, "gx", 0)
@@ -288,6 +300,7 @@
         prepare_kernel,
         "prepare",
         [
+            ((11,), jnp.int32),
             (square, bf16),
             (radial_w.shape, f32),
             (square, bf16),
@@ -297,23 +310,28 @@
             (square, f32),
             ((2, channels, degrees), f32),
         ],
-        [],
-        None, cotangent, radial_w, mix_w, square_w,
+        [pltpu.SMEM(senders.shape, jnp.int32)],
+        (ways, counts, senders, cotangent, radial_w, mix_w, square_w),
         flops=10**8,
-        copies=4,
+        smem=2,
+        smem_outs=1,
+        copies=5,
     )
     last, first, prepared = lax.optimization_barrier((last, first, prepared))
-    cot, radial_w, mix_w, square_w, cot_t, square_t, first_t, radial_t = prepared
+    meta, cot, radial_w, mix_w, square_w, cot_t, square_t, first_t, radial_t = prepared
     own_row = jnp.concatenate([first, packed, last], axis=0)
     far_row, near_row = swap(own_row, "gy", 1), swap(own_row, "gy", 0)
+    slots = len(EARLY) * rows
     basis, sums = local(
         early_kernel,
         "early",
-        [((degrees * rows, 6 * rows), bf16), ((5, rows, channels), f32)],
-        [((6 * rows, 4 * channels), bf16)],
-        meta, own_row, near_row, radial_w,
+        [((degrees * rows, slots), bf16), ((5, rows, channels), f32)],
+        [pltpu.VMEM((slots, 4 * channels), bf16)],
+        (meta, own_row, near_row, radial_w),
         flops=10**9,
-    )
+        smem=1,
+    )
+    slots = len(FAR) * rows
     far_out, grads, first_bf, second_bf = local(
         middle_kernel,
         "middle",
@@ -323,9 +341,13 @@
             (square, bf16),
             ((3 * rows, channels), bf16),
         ],
-        [((degrees * rows, 3 * rows), bf16), ((3 * rows, 4 * channels), bf16)],
-        meta, far_row, own_row, sums, cot, cot_t, square_w, square_t, first_t, radial_w, radial_t,
+        [pltpu.VMEM((degrees * rows, slots), bf16), pltpu.VMEM((slots, 4 * channels), bf16)],
+        (
+            meta, far_row, own_row, sums, cot, cot_t, square_w, square_t, first_t,
+            radial_w, radial_t,
+        ),
         flops=10**9,
+        smem=1,
     )
     far_in = swap_back(far_out, "gy", 1)
     near_out, own_out, updated = local(
@@ -333,8 +355,9 @@
         "late",
         [((3, channels, rows), bf16), ((3, channels, rows), f32), (square, bf16)],
         [],
-        meta, own_row, near_row, basis, grads, first_bf, second_bf, mix_w, square_w,
+        (meta, own_row, near_row, basis, grads, first_bf, second_bf, mix_w, square_w),
         flops=10**9,
+        smem=1,
     )
     near_in = swap_back(near_out, "gy", 0)
     far_in = lax.optimization_barrier(far_in.astype(f32))

time: 34.8 us -> 32.1 us (0.922)
  local copies, waits for them, and re-layouts: 5.21 us -> 0.74 us
  starting transfers between devices: 10.4 us -> 14.4 us
  waiting for transfers between devices: 9 us -> 5.07 us
  Pallas kernels: 7.22 us -> 10.1 us
  other arithmetic: 1.07 us -> 0.15 us
    unnamed x13 -> x1, local copies, waits for them, and re-layouts: 5.12 us -> 0.73 us
    ppermute x8, starting transfers between devices: 10.4 us -> 14.4 us  [swap(): return lax.ppermute(block, axis, pairs)]
    ppermute x8, waiting for transfers between devices: 9 us -> 5.07 us  [swap(): return lax.ppermute(block, axis, pairs)]
    pallas_call x5, Pallas kernels: 7.22 us -> 10.1 us  [local(): pl.pallas_call(kernel, out_shape=tuple((jax.ShapeDtypeStruct(*out) for ou...]
    reduce_or x1 -> x0, other arithmetic: 0.75 us -> none  [slot_list(): live = jnp.any(taken, axis=1).astype(jnp.int32)]
  transfers between devices with their start and end apart: 8 -> 8, of which waited for: 5 -> 6; matrix products, arithmetic and copies ran while one was open for 3% -> 0% of each run, Pallas kernels for 13% -> 21%
where the time goes in v2:
time: 32.1 us; the launch traced here: 31.9 us
  starting transfers between devices  14.4 us (45%)
  Pallas kernels  10.1 us (31%)
  waiting for transfers between devices  5.07 us (16%)
  between operations  1.36 us (4%)
  local copies, waits for them, and re-layouts  0.74 us (2%)
    ppermute x8, starting transfers between devices, swap(): return lax.ppermute(block, axis, pairs)  14.4 us
    pallas_call x5, Pallas kernels, local(): pl.pallas_call(kernel, out_shape=tuple((jax.ShapeDtypeStruct(*out) for ou...  10.1 us
    ppermute x8, waiting for transfers between devices, swap(): return lax.ppermute(block, axis, pairs)  5.07 us
    unnamed x1, local copies, waits for them, and re-layouts  0.73 us
  transfers between devices with their start and end apart: 8, of which 6 were waited for; matrix products, arithmetic and copies ran while one was open for 0% of the time, Pallas kernels for 21%

profile of v2, /device:TPU:0, one launch (start us, length us, event | category | flops | bytes accessed | tf_op | source)
XLA Modules:
  0.0 31.9 jit_solution(7122293306789208583)
XLA Ops:
  0.6 0.8 %pack.1 = bf16[1,144,128]{2,1,0:T(8,128)(2,1)S(1)} custom-call(bf16[1,1,128,128]{3,2,1,0:T(8,128)(2,1)} %feat_ref.1, bf16[1,1,3,128]{3,2,1,0:T(4,128)(2,1)} %pos_ref.1), custom_call_target="tpu_custom_call" | custom-call | bytes 1048576 | tf_op jit(solution)/shard_map/pack/pallas_call | solution.py:271
  1.4 3.0 %collective-permute-start.1 = (bf16[1,144,128]{2,1,0:T(8,128)(2,1)S(1)}, bf16[1,144,128]{2,1,0:T(8,128)(2,1)S(1)}, u32[]{:S(2)}, u32[]{:S(2)}) collective-permute-start(bf16[1,144,128]{2,1,0:T(8,128)(2,1)S(1)} %pack.1), channel_id=1, source_target_pairs={{0,8},{8,0},{16,24},{24,16},{1,9},{9,1},{17,25},{25,17},{2,10},{10... | collective-permute-start | bytes 110600 | tf_op jit(solution)/shard_map/ppermute | solution.py:33
  4.4 1.5 %collective-permute-start = (bf16[1,144,128]{2,1,0:T(8,128)(2,1)S(1)}, bf16[1,144,128]{2,1,0:T(8,128)(2,1)S(1)}, u32[]{:S(2)}, u32[]{:S(2)}) collective-permute-start(bf16[1,144,128]{2,1,0:T(8,128)(2,1)S(1)} %pack.1), channel_id=1, source_target_pairs={{8,16},{16,8},{24,0},{0,24},{9,17},{17,9},{25,1},{1,25},{10,18},{1... | collective-permute-start | bytes 110600 | tf_op jit(solution)/shard_map/ppermute | solution.py:33
  5.9 0.1 pad_add_fusion.ways
  6.7 2.0 %prepare.1 = (s32[11]{0:T(128)S(1)}, bf16[128,128]{1,0:T(8,128)(2,1)S(1)}, f32[2,8,128]{2,1,0:T(8,128)S(1)}, bf16[128,128]{1,0:T(8,128)(2,1)S(1)}, bf16[128,128]...) custom-call(s32[2]{0:T(128)S(1)} %pad_add_fusion.ways, ...), custom_call_target="tpu_custom_call" | custom-call | flops 100000000 | bytes 1048576 | tf_op jit(solution)/shard_map/prepare/pallas_call | solution.py:271
  8.6 0.0 collective-permute-done.1
  8.7 0.6 %collective-permute-done = bf16[1,144,128]{2,1,0:T(8,128)(2,1)S(1)} collective-permute-done((bf16[1,144,128]{2,1,0:T(8,128)(2,1)S(1)}, bf16[1,144,128]{2,1,0:T(8,128)(2,1)S(1)}, u32[]{:S(2)}, u32[]{:S(2)}) %collective-permute-start) | collective-permute-done | bytes 36896 | tf_op jit(solution)/shard_map/ppermute | solution.py:33
  9.3 0.1 collective-permute-start.2
  9.4 3.7 %collective-permute-start.3 = (bf16[3,144,128]{2,1,0:T(8,128)(2,1)S(1)}, bf16[3,144,128]{2,1,0:T(8,128)(2,1)S(1)}, u32[]{:S(2)}, u32[]{:S(2)}) collective-permute-start(bf16[3,144,128]{2,1,0:T(8,128)(2,1)S(1)} %pad_maximum_fusion.own_row), channel_id=1, source_target_pairs={{1,2},{2,1},{3,4},{4,3},{5,6},{6,5},{7,0},{0,7},{9,10},{10,9},{11,... | collective-permute-start | bytes 331784 | tf_op jit(solution)/shard_map/ppermute | solution.py:33
  13.1 0.0 collective-permute-done.2.near_row
  13.1 2.4 %early.1 = (bf16[1024,768]{1,0:T(8,128)(2,1)S(1)}, f32[5,128,128]{2,1,0:T(8,128)S(1)}) custom-call(s32[11]{0:T(128)S(1)} %get-tuple-element.40.meta, bf16[3,144,128]{2,1,0:T(8,128)(2,1)S(1)} %pad_maximum_fusion.own_row, bf16[3,144,128]{2,1,0:T(8,128)(2,1)S(1)} %collective-permute-done.2.near_row, f32[2,8,128]{2,1,0:T(8,128)S(1)} %get-tuple-element.43.radial_ref), custom_call_target="tpu_custom_call" | custom-call | flops 1000000000 | bytes 1048576 | tf_op jit(solution)/shard_map/early/pallas_call | solution.py:271
  15.6 0.5 %collective-permute-done.3.far_row = bf16[3,144,128]{2,1,0:T(8,128)(2,1)S(1)} collective-permute-done((bf16[3,144,128]{2,1,0:T(8,128)(2,1)S(1)}, bf16[3,144,128]{2,1,0:T(8,128)(2,1)S(1)}, u32[]{:S(2)}, u32[]{:S(2)}) %collective-permute-start.3) | collective-permute-done | bytes 110624 | tf_op jit(solution)/shard_map/ppermute | solution.py:33
  16.0 2.7 %middle.1 = (bf16[3,128,128]{2,1,0:T(8,128)(2,1)S(1)}, bf16[512,1024]{1,0:T(8,128)(2,1)S(1)}, bf16[128,128]{1,0:T(8,128)(2,1)S(1)}, bf16[384,128]{1,0:T(8,128)(2,1)S(1)}) custom-call(s32[11]{0:T(128)S(1)} %get-tuple-element.40.meta, bf16[3,144,128]{2,1,0:T(8,128)(2,1)S(1)} %collective-permute-done.3.far_row, ...), custom_call_target="tpu_custom_call" | custom-call | flops 1000000000 | bytes 1048576 | tf_op jit(solution)/shard_map/middle/pallas_call | solution.py:271
  18.7 3.1 %collective-permute-start.5 = (bf16[3,128,128]{2,1,0:T(8,128)(2,1)S(1)}, bf16[3,128,128]{2,1,0:T(8,128)(2,1)S(1)}, u32[]{:S(2)}, u32[]{:S(2)}) collective-permute-start(bf16[3,128,128]{2,1,0:T(8,128)(2,1)S(1)} %get-tuple-element.59), channel_id=1, source_target_pairs={{1,2},{2,1},{3,4},{4,3},{5,6},{6,5},{7,0},{0,7},{9,10},{10,9},{11,... | collective-permute-start | bytes 294920 | tf_op jit(solution)/shard_map/ppermute | solution.py:33
  21.8 2.2 %late.1 = (bf16[3,128,128]{2,1,0:T(8,128)(2,1)S(1)}, f32[3,128,128]{2,1,0:T(8,128)S(1)}, bf16[128,128]{1,0:T(8,128)(2,1)}) custom-call(s32[11]{0:T(128)S(1)} %get-tuple-element.40.meta, bf16[3,144,128]{2,1,0:T(8,128)(2,1)S(1)} %pad_maximum_fusion.own_row, bf16[3,144,128]{2,1,0:T(8,128)(2,1)S(1)} %collective-permute-done.2.near_row, ...), custom_call_target="tpu_custom_call" | custom-call | flops 1000000000 | bytes 1048576 | tf_op jit(solution)/shard_map/late/pallas_call | solution.py:271
  24.0 0.0 collective-permute-start.4
  24.0 0.6 %collective-permute-done.5 = bf16[3,128,128]{2,1,0:T(8,128)(2,1)S(1)} collective-permute-done((bf16[3,128,128]{2,1,0:T(8,128)(2,1)S(1)}, bf16[3,128,128]{2,1,0:T(8,128)(2,1)S(1)}, u32[]{:S(2)}, u32[]{:S(2)}) %collective-permute-start.5) | collective-permute-done | bytes 98336 | tf_op jit(solution)/shard_map/ppermute | solution.py:33
  24.6 0.7 %collective-permute-done.4 = bf16[3,128,128]{2,1,0:T(8,128)(2,1)S(1)} collective-permute-done((bf16[3,128,128]{2,1,0:T(8,128)(2,1)S(1)}, bf16[3,128,128]{2,1,0:T(8,128)(2,1)S(1)}, u32[]{:S(2)}, u32[]{:S(2)}) %collective-permute-start.4) | collective-permute-done | bytes 98336 | tf_op jit(solution)/shard_map/ppermute | solution.py:33
  25.4 0.9 %collective-permute-start.6 = (bf16[128,128]{1,0:T(8,128)(2,1)S(1)}, bf16[128,128]{1,0:T(8,128)(2,1)S(1)}, u32[]{:S(2)}, u32[]{:S(2)}) collective-permute-start(bf16[128,128]{1,0:T(8,128)(2,1)S(1)} %get-tuple-element.64), channel_id=1, source_target_pairs={{0,8},{8,0},{16,24},{24,16},{1,9},{9,1},{17,25},{25,17},{2,10},{10... | collective-permute-start | bytes 98312 | tf_op jit(solution)/shard_map/ppermute | solution.py:33
  26.3 2.1 %collective-permute-start.7 = (bf16[128,128]{1,0:T(8,128)(2,1)S(1)}, bf16[128,128]{1,0:T(8,128)(2,1)S(1)}, u32[]{:S(2)}, u32[]{:S(2)}) collective-permute-start(bf16[128,128]{1,0:T(8,128)(2,1)S(1)} %get-tuple-element.65), channel_id=1, source_target_pairs={{8,16},{16,8},{24,0},{0,24},{9,17},{17,9},{25,1},{1,25},{10,18},{1... | collective-permute-start | bytes 98312 | tf_op jit(solution)/shard_map/ppermute | solution.py:33
  28.4 0.9 %collective-permute-done.6 = bf16[128,128]{1,0:T(8,128)(2,1)S(1)} collective-permute-done((bf16[128,128]{1,0:T(8,128)(2,1)S(1)}, bf16[128,128]{1,0:T(8,128)(2,1)S(1)}, u32[]{:S(2)}, u32[]{:S(2)}) %collective-permute-start.6) | collective-permute-done | bytes 32800 | tf_op jit(solution)/shard_map/ppermute | solution.py:33
  29.4 1.8 %collective-permute-done.7 = bf16[128,128]{1,0:T(8,128)(2,1)S(1)} collective-permute-done((bf16[128,128]{1,0:T(8,128)(2,1)S(1)}, bf16[128,128]{1,0:T(8,128)(2,1)S(1)}, u32[]{:S(2)}, u32[]{:S(2)}) %collective-permute-start.7) | collective-permute-done | bytes 32800 | tf_op jit(solution)/shard_map/ppermute | solution.py:33
  31.1 0.7 %copy.10 = f32[1,1,128,128]{3,2,1,0:T(8,128)} copy(f32[1,1,128,128]{2,3,1,0:T(8,128)S(1)} %fusion.1) | data formatting | bytes 131072
  (5 shorter events, 0.1 us)
Async XLA Ops:
  1.4 7.2 %collective-permute-start.1 = (bf16[1,144,128]{2,1,0:T(8,128)(2,1)S(1)}, bf16[1,144,128]{2,1,0:T(8,128)(2,1)S(1)}, u32[]{:S(2)}, u32[]{:S(2)}) collective-permute-start(bf16[1,144,128]{2,1,0:T(8,128)(2,1)S(1)} %pack.1), channel_id=1, source_target_pairs={{0,8},{8,0},{16,24},{24,16},{1,9},{9,1},{17,25},{25,17},{2,10},{10... | collective-permute-start | bytes 110600 | tf_op jit(solution)/shard_map/ppermute | solution.py:33
  4.4 4.9 %collective-permute-start = (bf16[1,144,128]{2,1,0:T(8,128)(2,1)S(1)}, bf16[1,144,128]{2,1,0:T(8,128)(2,1)S(1)}, u32[]{:S(2)}, u32[]{:S(2)}) collective-permute-start(bf16[1,144,128]{2,1,0:T(8,128)(2,1)S(1)} %pack.1), channel_id=1, source_target_pairs={{8,16},{16,8},{24,0},{0,24},{9,17},{17,9},{25,1},{1,25},{10,18},{1... | collective-permute-start | bytes 110600 | tf_op jit(solution)/shard_map/ppermute | solution.py:33
  9.3 3.8 %collective-permute-start.2 = (bf16[3,144,128]{2,1,0:T(8,128)(2,1)S(1)}, bf16[3,144,128]{2,1,0:T(8,128)(2,1)S(1)}, u32[]{:S(2)}, u32[]{:S(2)}) collective-permute-start(bf16[3,144,128]{2,1,0:T(8,128)(2,1)S(1)} %pad_maximum_fusion.own_row), channel_id=1, source_target_pairs={{0,1},{1,0},{2,3},{3,2},{4,5},{5,4},{6,7},{7,6},{8,9},{9,8},{10,11... | collective-permute-start | bytes 331784 | tf_op jit(solution)/shard_map/ppermute | solution.py:33
  9.4 6.6 %collective-permute-start.3 = (bf16[3,144,128]{2,1,0:T(8,128)(2,1)S(1)}, bf16[3,144,128]{2,1,0:T(8,128)(2,1)S(1)}, u32[]{:S(2)}, u32[]{:S(2)}) collective-permute-start(bf16[3,144,128]{2,1,0:T(8,128)(2,1)S(1)} %pad_maximum_fusion.own_row), channel_id=1, source_target_pairs={{1,2},{2,1},{3,4},{4,3},{5,6},{6,5},{7,0},{0,7},{9,10},{10,9},{11,... | collective-permute-start | bytes 331784 | tf_op jit(solution)/shard_map/ppermute | solution.py:33
  18.7 5.9 %collective-permute-start.5 = (bf16[3,128,128]{2,1,0:T(8,128)(2,1)S(1)}, bf16[3,128,128]{2,1,0:T(8,128)(2,1)S(1)}, u32[]{:S(2)}, u32[]{:S(2)}) collective-permute-start(bf16[3,128,128]{2,1,0:T(8,128)(2,1)S(1)} %get-tuple-element.59), channel_id=1, source_target_pairs={{1,2},{2,1},{3,4},{4,3},{5,6},{6,5},{7,0},{0,7},{9,10},{10,9},{11,... | collective-permute-start | bytes 294920 | tf_op jit(solution)/shard_map/ppermute | solution.py:33
  24.0 1.3 %collective-permute-start.4 = (bf16[3,128,128]{2,1,0:T(8,128)(2,1)S(1)}, bf16[3,128,128]{2,1,0:T(8,128)(2,1)S(1)}, u32[]{:S(2)}, u32[]{:S(2)}) collective-permute-start(bf16[3,128,128]{2,1,0:T(8,128)(2,1)S(1)} %get-tuple-element.58), channel_id=1, source_target_pairs={{0,1},{1,0},{2,3},{3,2},{4,5},{5,4},{6,7},{7,6},{8,9},{9,8},{10,11... | collective-permute-start | bytes 294920 | tf_op jit(solution)/shard_map/ppermute | solution.py:33
  25.4 4.0 %collective-permute-start.6 = (bf16[128,128]{1,0:T(8,128)(2,1)S(1)}, bf16[128,128]{1,0:T(8,128)(2,1)S(1)}, u32[]{:S(2)}, u32[]{:S(2)}) collective-permute-start(bf16[128,128]{1,0:T(8,128)(2,1)S(1)} %get-tuple-element.64), channel_id=1, source_target_pairs={{0,8},{8,0},{16,24},{24,16},{1,9},{9,1},{17,25},{25,17},{2,10},{10... | collective-permute-start | bytes 98312 | tf_op jit(solution)/shard_map/ppermute | solution.py:33
  26.3 4.8 %collective-permute-start.7 = (bf16[128,128]{1,0:T(8,128)(2,1)S(1)}, bf16[128,128]{1,0:T(8,128)(2,1)S(1)}, u32[]{:S(2)}, u32[]{:S(2)}) collective-permute-start(bf16[128,128]{1,0:T(8,128)(2,1)S(1)} %get-tuple-element.65), channel_id=1, source_target_pairs={{8,16},{16,8},{24,0},{0,24},{9,17},{17,9},{25,1},{1,25},{10,18},{1... | collective-permute-start | bytes 98312 | tf_op jit(solution)/shard_map/ppermute | solution.py:33

commit v3 on v2

--- a/solution.py
+++ b/solution.py
@@ -64,10 +64,13 @@
     return lines, [jnp.broadcast_to(columns[:, m : m + 1], (rows, rows)) for m in range(3)]
 
 
-def ghost_place(meta, block, line, column):
+DX, DY, LIVE, FAR_COUNT, FAR_ORDER = 0, 1, 8, 17, 18
+
+
+def ghost_place(table, block, line, column):
     tail = block[block.shape[0] - 16 :, :].astype(f32)
-    along_x = (meta[0] * (1 - column)).astype(f32)
-    along_y = (meta[1] * (0, 1, -1)[line]).astype(f32)
+    along_x = (table[DX : DX + 1, :] * (1 - column)).astype(f32)
+    along_y = (table[DY : DY + 1, :] * (0, 1, -1)[line]).astype(f32)
     return [tail[0:1] + along_x, tail[1:2] + along_y, tail[2:3]]
 
 
@@ -125,7 +128,7 @@
 
 def prepare_kernel(
     ways, counts, senders_ref, cot_ref, radial_ref, mix_ref, square_ref,
-    meta, cot_out, radial_out, mix_out, square_out, cot_t_ref, square_t_ref, first_t_ref,
+    live_ref, cot_out, radial_out, mix_out, square_out, cot_t_ref, square_t_ref, first_t_ref,
     radial_t_ref,
     senders, sems,
 ):
@@ -138,17 +141,21 @@
     for copy in copies:
         copy.start()
     dx, dy = ways[0], ways[1]
-    meta[0] = dx
-    meta[1] = dy
+    count = counts[0, 0, 0]
     copies[0].wait()
-    count = counts[0, 0, 0]
+    live = []
     for line in range(3):
         for column in range(3):
             ghost = 3 * (dx * (1 - column) + 1) + dy * (0, 1, -1)[line] + 1
-            live = jnp.int32(0)
+            found = jnp.int32(0)
             for t in range(senders.shape[3]):
-                live = live | ((t < count) & (senders[0, 0, 0, t] == ghost)).astype(jnp.int32)
-            meta[2 + line * 3 + column] = live
+                found = found | ((t < count) & (senders[0, 0, 0, t] == ghost)).astype(jnp.int32)
+            live.append(found)
+    far = live[6:]
+    begin = jnp.where(far[0] == 1, 0, jnp.where(far[1] == 1, 1, 2))
+    after = jnp.where(begin == 2, 0, jnp.where((begin == 0) & (far[1] == 1), 1, 2))
+    for row, number in enumerate([*live, far[0] + far[1] + far[2], begin, after]):
+        live_ref[row : row + 1, :] = jnp.full((1, live_ref.shape[1]), number, jnp.int32)
     for copy in copies[1:]:
         copy.wait()
     cot_t_ref[...] = cot_out[...].astype(f32).T
@@ -161,14 +168,13 @@
 
 
 EARLY = ((0, 0), (0, 1), (0, 2), (1, 0), (1, 1), (1, 2))
-FAR = ((2, 0), (2, 1), (2, 2))
 
 
 def early_blocks(own_row, near_row):
     return [own_row.at[c] for c in range(3)] + [near_row.at[c] for c in range(3)]
 
 
-def early_kernel(meta, own_row, near_row, radial_ref, basis, sums_ref, stacked):
+def early_kernel(table, own_row, near_row, radial_ref, basis, sums_ref, stacked):
     rows, channels = sums_ref.shape[1:]
     degrees = radial_ref.shape[1]
     _, recv = own_place(own_row, rows)
@@ -179,11 +185,11 @@
     for at, ((line, column), source) in enumerate(
         zip(EARLY, early_blocks(own_row, near_row))
     ):
-        live = meta[2 + line * 3 + column]
+        live = table[LIVE + line * 3 + column, 0]
 
         @pl.when(live == 1)
         def _(line=line, column=column, source=source, at=at):
-            place = ghost_place(meta, source, line, column)
+            place = ghost_place(table, source, line, column)
             weight = others if (line, column) == (0, 1) else 1.0
             add_tile(source, place, recv, weight, basis, stacked, at, degrees)
 
@@ -198,22 +204,33 @@
 
 
 def middle_kernel(
-    meta, far_row, own_row, sums_ref, cot_ref, cot_t_ref, square_ref,
-    square_t_ref, first_t_ref, radial_ref, radial_t_ref,
+    table, far_row, own_row, sums_ref, cot_ref, cot_t_ref, square_ref, square_t_ref, first_t_ref,
+    radial_ref, radial_t_ref,
     far_out, grads, first_ref, second_ref,
-    basis, stacked,
+    basis, stacked, totals,
 ):
     rows, channels = cot_ref.shape
     degrees = radial_ref.shape[1]
     lines, recv = own_place(own_row, rows)
-    places = []
-    for at, (line, column) in enumerate(FAR):
-        source = far_row.at[column]
-        places.append(ghost_place(meta, source, line, column))
-        weight = meta[2 + line * 3 + column].astype(f32)
-        add_tile(source, places[at], recv, weight, basis, stacked, at, degrees)
-    totals = gather(basis, stacked, radial_ref, [sums_ref[at] for at in range(5)])
-    sum_zero, sum_one, moments = totals[0], totals[1], totals[2:]
+    far_count = table[FAR_COUNT, 0]
+    order = [table[FAR_ORDER, 0], table[FAR_ORDER + 1, 0]]
+    few, all_far = (far_count == 1) | (far_count == 2), far_count == 3
+
+    def messages(columns):
+        width = len(columns) * rows
+        for at, column in enumerate(columns):
+            source = far_row.at[column]
+            place = ghost_place(table, source, 2, column)
+            weight = (far_count > at).astype(f32)
+            add_tile(source, place, recv, weight, basis, stacked, at, degrees)
+        parts = gather(basis.at[:, :width], stacked.at[:width], radial_ref, None)
+        for at, part in enumerate(parts):
+            totals[at] += part
+
+    totals[...] = sums_ref[...]
+    pl.when(few)(lambda: messages(order))
+    pl.when(all_far)(lambda: messages([0, 1, 2]))
+    sum_zero, sum_one, moments = totals[0], totals[1], [totals[2 + m] for m in range(3)]
     first_ref[...] = sum_zero.astype(bf16)
     second = jnp.concatenate(
         [(moments[m] - recv[m] * sum_one).astype(bf16) for m in range(3)], axis=0
@@ -238,16 +255,25 @@
         grads[0:channels, span] = (zero * first_t + one * one_t).astype(bf16)
         for m in range(3):
             grads[(m + 1) * channels : (m + 2) * channels, span] = (one * second_t[m]).astype(bf16)
-    spread(grads, basis, places, [far_out.at[column] for _, column in FAR])
+
+    def adjoints(columns):
+        width = len(columns) * rows
+        places = [ghost_place(table, far_row.at[column], 2, column) for column in columns]
+        outs = [far_out.at[column] for column in columns]
+        spread(grads, basis.at[:, :width], places, outs)
+
+    far_out[...] = jnp.zeros(far_out.shape, bf16)
+    pl.when(few)(lambda: adjoints(order))
+    pl.when(all_far)(lambda: adjoints([0, 1, 2]))
 
 
 def late_kernel(
-    meta, own_row, near_row, basis, grads, first_ref, second_ref, mix_ref, square_ref,
+    table, own_row, near_row, basis, grads, first_ref, second_ref, mix_ref, square_ref,
     near_out, own_out, updated_ref,
 ):
     rows = first_ref.shape[0]
     sources = early_blocks(own_row, near_row)
-    places = [ghost_place(meta, source, *slot) for slot, source in zip(EARLY, sources)]
+    places = [ghost_place(table, source, *slot) for slot, source in zip(EARLY, sources)]
     outs = [own_out.at[c] for c in range(3)] + [near_out.at[c] for c in range(3)]
     spread(grads, basis, places, outs)
     second = second_ref[...]
@@ -259,7 +285,7 @@
     ).astype(bf16)
 
 
-def local(kernel, name, outs, scratch, args, flops=0, smem=0, smem_outs=0, copies=0):
+def local(kernel, name, outs, scratch, args, flops=0, smem=0, copies=0):
     in_vmem = pl.BlockSpec(memory_space=pltpu.VMEM)
     in_smem = pl.BlockSpec(memory_space=pltpu.SMEM)
     given = in_vmem
@@ -272,7 +298,7 @@
         kernel,
         out_shape=tuple(jax.ShapeDtypeStruct(*out) for out in outs),
         in_specs=[in_smem] * smem + [given] * (len(args) - smem),
-        out_specs=(in_smem,) * smem_outs + (in_vmem,) * (len(outs) - smem_outs),
+        out_specs=(in_vmem,) * len(outs),
         scratch_shapes=scratch
         + ([pltpu.SemaphoreType.DMA((copies,))] if copies else []),
         compiler_params=pltpu.CompilerParams(vmem_limit_bytes=32 * 2**20),
@@ -300,7 +326,7 @@
         prepare_kernel,
         "prepare",
         [
-            ((11,), jnp.int32),
+            ((16, rows), jnp.int32),
             (square, bf16),
             (radial_w.shape, f32),
             (square, bf16),
@@ -314,11 +340,12 @@
         (ways, counts, senders, cotangent, radial_w, mix_w, square_w),
         flops=10**8,
         smem=2,
-        smem_outs=1,
         copies=5,
     )
-    last, first, prepared = lax.optimization_barrier((last, first, prepared))
-    meta, cot, radial_w, mix_w, square_w, cot_t, square_t, first_t, radial_t = prepared
+    last, first, ways, prepared = lax.optimization_barrier((last, first, ways, prepared))
+    live, cot, radial_w, mix_w, square_w, cot_t, square_t, first_t, radial_t = prepared
+    steps = jnp.broadcast_to(jnp.pad(ways, (0, 6))[:, None], (8, rows))
+    table = jnp.concatenate([steps, live], axis=0)
     own_row = jnp.concatenate([first, packed, last], axis=0)
     far_row, near_row = swap(own_row, "gy", 1), swap(own_row, "gy", 0)
     slots = len(EARLY) * rows
@@ -327,11 +354,10 @@
         "early",
         [((degrees * rows, slots), bf16), ((5, rows, channels), f32)],
         [pltpu.VMEM((slots, 4 * channels), bf16)],
-        (meta, own_row, near_row, radial_w),
+        (table, own_row, near_row, radial_w),
         flops=10**9,
-        smem=1,
-    )
-    slots = len(FAR) * rows
+    )
+    slots = 3 * rows
     far_out, grads, first_bf, second_bf = local(
         middle_kernel,
         "middle",
@@ -341,13 +367,16 @@
             (square, bf16),
             ((3 * rows, channels), bf16),
         ],
-        [pltpu.VMEM((degrees * rows, slots), bf16), pltpu.VMEM((slots, 4 * channels), bf16)],
+        [
+            pltpu.VMEM((degrees * rows, slots), bf16),
+            pltpu.VMEM((slots, 4 * channels), bf16),
+            pltpu.VMEM((5, rows, channels), f32),
+        ],
         (
-            meta, far_row, own_row, sums, cot, cot_t, square_w, square_t, first_t,
+            table, far_row, own_row, sums, cot, cot_t, square_w, square_t, first_t,
             radial_w, radial_t,
         ),
         flops=10**9,
-        smem=1,
     )
     far_in = swap_back(far_out, "gy", 1)
     near_out, own_out, updated = local(
@@ -355,9 +384,8 @@
         "late",
         [((3, channels, rows), bf16), ((3, channels, rows), f32), (square, bf16)],
         [],
-        (meta, own_row, near_row, basis, grads, first_bf, second_bf, mix_w, square_w),
+        (table, own_row, near_row, basis, grads, first_bf, second_bf, mix_w, square_w),
         flops=10**9,
-        smem=1,
     )
     near_in = swap_back(near_out, "gy", 0)
     far_in = lax.optimization_barrier(far_in.astype(f32))

time: 32.1 us -> 30.3 us (0.944)
  waiting for transfers between devices: 5.07 us -> 9.02 us
  Pallas kernels: 10.1 us -> 6.59 us
  starting transfers between devices: 14.4 us -> 12.2 us
    ppermute x8, waiting for transfers between devices: 5.07 us -> 9.02 us  [swap(): return lax.ppermute(block, axis, pairs)]
    pallas_call x5, Pallas kernels: 10.1 us -> 6.59 us  [local(): pl.pallas_call(kernel, out_shape=tuple((jax.ShapeDtypeStruct(*out) for ou...]
    ppermute x8, starting transfers between devices: 14.4 us -> 12.2 us  [swap(): return lax.ppermute(block, axis, pairs)]
  transfers between devices with their start and end apart: 8 -> 8, of which waited for: 6 -> 6; matrix products, arithmetic and copies ran while one was open for 0% -> 1% of each run, Pallas kernels for 21% -> 17%
where the time goes in v3:
time: 30.3 us; the launch traced here: 30.1 us
  starting transfers between devices  12.2 us (40%)
  waiting for transfers between devices  9.02 us (30%)
  Pallas kernels  6.59 us (22%)
  between operations  1.36 us (4%)
  local copies, waits for them, and re-layouts  0.74 us (2%)
    ppermute x8, starting transfers between devices, swap(): return lax.ppermute(block, axis, pairs)  12.2 us
    ppermute x8, waiting for transfers between devices, swap(): return lax.ppermute(block, axis, pairs)  9.02 us
    pallas_call x5, Pallas kernels, local(): pl.pallas_call(kernel, out_shape=tuple((jax.ShapeDtypeStruct(*out) for ou...  6.59 us
    unnamed x1, local copies, waits for them, and re-layouts  0.73 us
  transfers between devices with their start and end apart: 8, of which 6 were waited for; matrix products, arithmetic and copies ran while one was open for 1% of the time, Pallas kernels for 17%

profile of v3, /device:TPU:0, one launch (start us, length us, event | category | flops | bytes accessed | tf_op | source)
XLA Modules:
  0.0 30.1 jit_solution(10594486417840390789)
XLA Ops:
  0.6 0.8 %pack.1 = bf16[1,144,128]{2,1,0:T(8,128)(2,1)S(1)} custom-call(bf16[1,1,128,128]{3,2,1,0:T(8,128)(2,1)} %feat_ref.1, bf16[1,1,3,128]{3,2,1,0:T(4,128)(2,1)} %pos_ref.1), custom_call_target="tpu_custom_call" | custom-call | bytes 1048576 | tf_op jit(solution)/shard_map/pack/pallas_call | solution.py:297
  1.4 3.0 %collective-permute-start.1 = (bf16[1,144,128]{2,1,0:T(8,128)(2,1)S(1)}, bf16[1,144,128]{2,1,0:T(8,128)(2,1)S(1)}, u32[]{:S(2)}, u32[]{:S(2)}) collective-permute-start(bf16[1,144,128]{2,1,0:T(8,128)(2,1)S(1)} %pack.1), channel_id=1, source_target_pairs={{0,8},{8,0},{16,24},{24,16},{1,9},{9,1},{17,25},{25,17},{2,10},{10... | collective-permute-start | bytes 110600 | tf_op jit(solution)/shard_map/ppermute | solution.py:33
  4.4 1.5 %collective-permute-start = (bf16[1,144,128]{2,1,0:T(8,128)(2,1)S(1)}, bf16[1,144,128]{2,1,0:T(8,128)(2,1)S(1)}, u32[]{:S(2)}, u32[]{:S(2)}) collective-permute-start(bf16[1,144,128]{2,1,0:T(8,128)(2,1)S(1)} %pack.1), channel_id=1, source_target_pairs={{8,16},{16,8},{24,0},{0,24},{9,17},{17,9},{25,1},{1,25},{10,18},{1... | collective-permute-start | bytes 110600 | tf_op jit(solution)/shard_map/ppermute | solution.py:33
  5.9 0.1 pad_add_fusion.1.ways
  6.7 1.6 %prepare.1 = (s32[16,128]{1,0:T(8,128)S(1)}, bf16[128,128]{1,0:T(8,128)(2,1)S(1)}, f32[2,8,128]{2,1,0:T(8,128)S(1)}, bf16[128,128]{1,0:T(8,128)(2,1)S(1)}, bf16[...) custom-call(s32[2]{0:T(128)S(1)} %pad_add_fusion.1.ways, ...), custom_call_target="tpu_custom_call" | custom-call | flops 100000000 | bytes 1048576 | tf_op jit(solution)/shard_map/prepare/pallas_call | solution.py:297
  8.2 0.0 collective-permute-done.1
  8.2 1.1 %collective-permute-done = bf16[1,144,128]{2,1,0:T(8,128)(2,1)S(1)} collective-permute-done((bf16[1,144,128]{2,1,0:T(8,128)(2,1)S(1)}, bf16[1,144,128]{2,1,0:T(8,128)(2,1)S(1)}, u32[]{:S(2)}, u32[]{:S(2)}) %collective-permute-start) | collective-permute-done | bytes 36896 | tf_op jit(solution)/shard_map/ppermute | solution.py:33
  9.3 2.1 %collective-permute-start.3 = (bf16[3,144,128]{2,1,0:T(8,128)(2,1)S(1)}, bf16[3,144,128]{2,1,0:T(8,128)(2,1)S(1)}, u32[]{:S(2)}, u32[]{:S(2)}) collective-permute-start(bf16[3,144,128]{2,1,0:T(8,128)(2,1)S(1)} %pad_maximum_fusion.own_row), channel_id=1, source_target_pairs={{1,2},{2,1},{3,4},{4,3},{5,6},{6,5},{7,0},{0,7},{9,10},{10,9},{11,... | collective-permute-start | bytes 331784 | tf_op jit(solution)/shard_map/ppermute | solution.py:33
  11.4 0.0 collective-permute-start.2
  11.4 0.1 pad_add_fusion.table
  11.4 1.2 %collective-permute-done.2.near_row = bf16[3,144,128]{2,1,0:T(8,128)(2,1)S(1)} collective-permute-done((bf16[3,144,128]{2,1,0:T(8,128)(2,1)S(1)}, bf16[3,144,128]{2,1,0:T(8,128)(2,1)S(1)}, u32[]{:S(2)}, u32[]{:S(2)}) %collective-permute-start.2) | collective-permute-done | bytes 110624 | tf_op jit(solution)/shard_map/ppermute | solution.py:33
  12.7 1.8 %early.1 = (bf16[1024,768]{1,0:T(8,128)(2,1)S(1)}, f32[5,128,128]{2,1,0:T(8,128)S(1)}) custom-call(s32[24,128]{1,0:T(8,128)S(1)} %pad_add_fusion.table, bf16[3,144,128]{2,1,0:T(8,128)(2,1)S(1)} %pad_maximum_fusion.own_row, bf16[3,144,128]{2,1,0:T(8,128)(2,1)S(1)} %collective-permute-done.2.near_row, f32[2,8,128]{2,1,0:T(8,128)S(1)} %get-tuple-element.45.radial_ref), custom_call_target="tpu_custom_call" | custom-call | flops 1000000000 | bytes 1048576 | tf_op jit(solution)/shard_map/early/pallas_call | solution.py:297
  14.5 1.7 %collective-permute-done.3.far_row = bf16[3,144,128]{2,1,0:T(8,128)(2,1)S(1)} collective-permute-done((bf16[3,144,128]{2,1,0:T(8,128)(2,1)S(1)}, bf16[3,144,128]{2,1,0:T(8,128)(2,1)S(1)}, u32[]{:S(2)}, u32[]{:S(2)}) %collective-permute-start.3) | collective-permute-done | bytes 110624 | tf_op jit(solution)/shard_map/ppermute | solution.py:33
  16.3 0.7 %middle.1 = (bf16[3,128,128]{2,1,0:T(8,128)(2,1)S(1)}, bf16[512,1024]{1,0:T(8,128)(2,1)S(1)}, bf16[128,128]{1,0:T(8,128)(2,1)S(1)}, bf16[384,128]{1,0:T(8,128)(2,1)S(1)}) custom-call(s32[24,128]{1,0:T(8,128)S(1)} %pad_add_fusion.table, bf16[3,144,128]{2,1,0:T(8,128)(2,1)S(1)} %collective-permute-done.3.far_row, ...), custom_call_target="tpu_custom_call" | custom-call | flops 1000000000 | bytes 1048576 | tf_op jit(solution)/shard_map/middle/pallas_call | solution.py:297
  17.0 2.6 %collective-permute-start.5 = (bf16[3,128,128]{2,1,0:T(8,128)(2,1)S(1)}, bf16[3,128,128]{2,1,0:T(8,128)(2,1)S(1)}, u32[]{:S(2)}, u32[]{:S(2)}) collective-permute-start(bf16[3,128,128]{2,1,0:T(8,128)(2,1)S(1)} %get-tuple-element.61), channel_id=1, source_target_pairs={{1,2},{2,1},{3,4},{4,3},{5,6},{6,5},{7,0},{0,7},{9,10},{10,9},{11,... | collective-permute-start | bytes 294920 | tf_op jit(solution)/shard_map/ppermute | solution.py:33
  19.6 1.7 %late.1 = (bf16[3,128,128]{2,1,0:T(8,128)(2,1)S(1)}, f32[3,128,128]{2,1,0:T(8,128)S(1)}, bf16[128,128]{1,0:T(8,128)(2,1)}) custom-call(s32[24,128]{1,0:T(8,128)S(1)} %pad_add_fusion.table, bf16[3,144,128]{2,1,0:T(8,128)(2,1)S(1)} %pad_maximum_fusion.own_row, bf16[3,144,128]{2,1,0:T(8,128)(2,1)S(1)} %collective-permute-done.2.near_row, ...), custom_call_target="tpu_custom_call" | custom-call | flops 1000000000 | bytes 1048576 | tf_op jit(solution)/shard_map/late/pallas_call | solution.py:297
  21.2 0.0 collective-permute-start.4
  21.2 2.7 %collective-permute-done.5 = bf16[3,128,128]{2,1,0:T(8,128)(2,1)S(1)} collective-permute-done((bf16[3,128,128]{2,1,0:T(8,128)(2,1)S(1)}, bf16[3,128,128]{2,1,0:T(8,128)(2,1)S(1)}, u32[]{:S(2)}, u32[]{:S(2)}) %collective-permute-start.5) | collective-permute-done | bytes 98336 | tf_op jit(solution)/shard_map/ppermute | solution.py:33
  23.9 0.0 collective-permute-done.4
  24.0 0.5 %collective-permute-start.6 = (bf16[128,128]{1,0:T(8,128)(2,1)S(1)}, bf16[128,128]{1,0:T(8,128)(2,1)S(1)}, u32[]{:S(2)}, u32[]{:S(2)}) collective-permute-start(bf16[128,128]{1,0:T(8,128)(2,1)S(1)} %get-tuple-element.66), channel_id=1, source_target_pairs={{0,8},{8,0},{16,24},{24,16},{1,9},{9,1},{17,25},{25,17},{2,10},{10... | collective-permute-start | bytes 98312 | tf_op jit(solution)/shard_map/ppermute | solution.py:33
  24.5 2.5 %collective-permute-start.7 = (bf16[128,128]{1,0:T(8,128)(2,1)S(1)}, bf16[128,128]{1,0:T(8,128)(2,1)S(1)}, u32[]{:S(2)}, u32[]{:S(2)}) collective-permute-start(bf16[128,128]{1,0:T(8,128)(2,1)S(1)} %get-tuple-element.67), channel_id=1, source_target_pairs={{8,16},{16,8},{24,0},{0,24},{9,17},{17,9},{25,1},{1,25},{10,18},{1... | collective-permute-start | bytes 98312 | tf_op jit(solution)/shard_map/ppermute | solution.py:33
  27.0 0.9 %collective-permute-done.6 = bf16[128,128]{1,0:T(8,128)(2,1)S(1)} collective-permute-done((bf16[128,128]{1,0:T(8,128)(2,1)S(1)}, bf16[128,128]{1,0:T(8,128)(2,1)S(1)}, u32[]{:S(2)}, u32[]{:S(2)}) %collective-permute-start.6) | collective-permute-done | bytes 32800 | tf_op jit(solution)/shard_map/ppermute | solution.py:33
  28.0 1.4 %collective-permute-done.7 = bf16[128,128]{1,0:T(8,128)(2,1)S(1)} collective-permute-done((bf16[128,128]{1,0:T(8,128)(2,1)S(1)}, bf16[128,128]{1,0:T(8,128)(2,1)S(1)}, u32[]{:S(2)}, u32[]{:S(2)}) %collective-permute-start.7) | collective-permute-done | bytes 32800 | tf_op jit(solution)/shard_map/ppermute | solution.py:33
  29.4 0.7 %copy.10 = f32[1,1,128,128]{3,2,1,0:T(8,128)} copy(f32[1,1,128,128]{2,3,1,0:T(8,128)S(1)} %fusion.1) | data formatting | bytes 131072
  (6 shorter events, 0.1 us)
Async XLA Ops:
  1.4 6.8 %collective-permute-start.1 = (bf16[1,144,128]{2,1,0:T(8,128)(2,1)S(1)}, bf16[1,144,128]{2,1,0:T(8,128)(2,1)S(1)}, u32[]{:S(2)}, u32[]{:S(2)}) collective-permute-start(bf16[1,144,128]{2,1,0:T(8,128)(2,1)S(1)} %pack.1), channel_id=1, source_target_pairs={{0,8},{8,0},{16,24},{24,16},{1,9},{9,1},{17,25},{25,17},{2,10},{10... | collective-permute-start | bytes 110600 | tf_op jit(solution)/shard_map/ppermute | solution.py:33
  4.4 4.9 %collective-permute-start = (bf16[1,144,128]{2,1,0:T(8,128)(2,1)S(1)}, bf16[1,144,128]{2,1,0:T(8,128)(2,1)S(1)}, u32[]{:S(2)}, u32[]{:S(2)}) collective-permute-start(bf16[1,144,128]{2,1,0:T(8,128)(2,1)S(1)} %pack.1), channel_id=1, source_target_pairs={{8,16},{16,8},{24,0},{0,24},{9,17},{17,9},{25,1},{1,25},{10,18},{1... | collective-permute-start | bytes 110600 | tf_op jit(solution)/shard_map/ppermute | solution.py:33
  9.3 7.0 %collective-permute-start.3 = (bf16[3,144,128]{2,1,0:T(8,128)(2,1)S(1)}, bf16[3,144,128]{2,1,0:T(8,128)(2,1)S(1)}, u32[]{:S(2)}, u32[]{:S(2)}) collective-permute-start(bf16[3,144,128]{2,1,0:T(8,128)(2,1)S(1)} %pad_maximum_fusion.own_row), channel_id=1, source_target_pairs={{1,2},{2,1},{3,4},{4,3},{5,6},{6,5},{7,0},{0,7},{9,10},{10,9},{11,... | collective-permute-start | bytes 331784 | tf_op jit(solution)/shard_map/ppermute | solution.py:33
  11.4 1.3 %collective-permute-start.2 = (bf16[3,144,128]{2,1,0:T(8,128)(2,1)S(1)}, bf16[3,144,128]{2,1,0:T(8,128)(2,1)S(1)}, u32[]{:S(2)}, u32[]{:S(2)}) collective-permute-start(bf16[3,144,128]{2,1,0:T(8,128)(2,1)S(1)} %pad_maximum_fusion.own_row), channel_id=1, source_target_pairs={{0,1},{1,0},{2,3},{3,2},{4,5},{5,4},{6,7},{7,6},{8,9},{9,8},{10,11... | collective-permute-start | bytes 331784 | tf_op jit(solution)/shard_map/ppermute | solution.py:33
  17.0 6.9 %collective-permute-start.5 = (bf16[3,128,128]{2,1,0:T(8,128)(2,1)S(1)}, bf16[3,128,128]{2,1,0:T(8,128)(2,1)S(1)}, u32[]{:S(2)}, u32[]{:S(2)}) collective-permute-start(bf16[3,128,128]{2,1,0:T(8,128)(2,1)S(1)} %get-tuple-element.61), channel_id=1, source_target_pairs={{1,2},{2,1},{3,4},{4,3},{5,6},{6,5},{7,0},{0,7},{9,10},{10,9},{11,... | collective-permute-start | bytes 294920 | tf_op jit(solution)/shard_map/ppermute | solution.py:33
  21.2 2.7 %collective-permute-start.4 = (bf16[3,128,128]{2,1,0:T(8,128)(2,1)S(1)}, bf16[3,128,128]{2,1,0:T(8,128)(2,1)S(1)}, u32[]{:S(2)}, u32[]{:S(2)}) collective-permute-start(bf16[3,128,128]{2,1,0:T(8,128)(2,1)S(1)} %get-tuple-element.60), channel_id=1, source_target_pairs={{0,1},{1,0},{2,3},{3,2},{4,5},{5,4},{6,7},{7,6},{8,9},{9,8},{10,11... | collective-permute-start | bytes 294920 | tf_op jit(solution)/shard_map/ppermute | solution.py:33
  24.0 4.0 %collective-permute-start.6 = (bf16[128,128]{1,0:T(8,128)(2,1)S(1)}, bf16[128,128]{1,0:T(8,128)(2,1)S(1)}, u32[]{:S(2)}, u32[]{:S(2)}) collective-permute-start(bf16[128,128]{1,0:T(8,128)(2,1)S(1)} %get-tuple-element.66), channel_id=1, source_target_pairs={{0,8},{8,0},{16,24},{24,16},{1,9},{9,1},{17,25},{25,17},{2,10},{10... | collective-permute-start | bytes 98312 | tf_op jit(solution)/shard_map/ppermute | solution.py:33
  24.5 4.8 %collective-permute-start.7 = (bf16[128,128]{1,0:T(8,128)(2,1)S(1)}, bf16[128,128]{1,0:T(8,128)(2,1)S(1)}, u32[]{:S(2)}, u32[]{:S(2)}) collective-permute-start(bf16[128,128]{1,0:T(8,128)(2,1)S(1)} %get-tuple-element.67), channel_id=1, source_target_pairs={{8,16},{16,8},{24,0},{0,24},{9,17},{17,9},{25,1},{1,25},{10,18},{1... | collective-permute-start | bytes 98312 | tf_op jit(solution)/shard_map/ppermute | solution.py:33

commit v4 on v3

--- a/solution.py
+++ b/solution.py
@@ -43,18 +43,25 @@
     return 1 - lax.axis_index(axis) % 2 if n % 2 == 0 else jnp.int32(1)
 
 
-def pack_kernel(feat_ref, pos_ref, out_ref, pos, sems):
+def pack_kernel(feat_ref, pos_ref, senders_ref, out_ref, senders, pos, sems):
     rows = feat_ref.shape[2]
+    pairs = ((pos_ref, pos), (feat_ref.at[0, 0], out_ref.at[0, :rows]), (senders_ref, senders))
+    copies = start_copies(pairs, sems)
+    copies[0].wait()
+    tail = jnp.zeros((13, out_ref.shape[2]), f32)
+    out_ref[0, rows:, :] = jnp.concatenate([pos[0, 0].astype(f32), tail], axis=0).astype(bf16)
+    for copy in copies[1:]:
+        copy.wait()
+
+
+def start_copies(pairs, sems):
     copies = [
-        pltpu.make_async_copy(pos_ref, pos, sems.at[0]),
-        pltpu.make_async_copy(feat_ref.at[0, 0], out_ref.at[0, :rows], sems.at[1]),
+        pltpu.make_async_copy(source, target, sems.at[at])
+        for at, (source, target) in enumerate(pairs)
     ]
     for copy in copies:
         copy.start()
-    copies[0].wait()
-    tail = jnp.zeros((13, out_ref.shape[2]), f32)
-    out_ref[0, rows:, :] = jnp.concatenate([pos[0, 0].astype(f32), tail], axis=0).astype(bf16)
-    copies[1].wait()
+    return copies
 
 
 def own_place(own_row, rows):
@@ -126,45 +133,27 @@
         out[...] = total.astype(out.dtype)
 
 
-def prepare_kernel(
-    ways, counts, senders_ref, cot_ref, radial_ref, mix_ref, square_ref,
-    live_ref, cot_out, radial_out, mix_out, square_out, cot_t_ref, square_t_ref, first_t_ref,
-    radial_t_ref,
-    senders, sems,
-):
-    held = (senders, cot_out, radial_out, mix_out, square_out)
-    given = (senders_ref, cot_ref.at[0, 0], radial_ref, mix_ref, square_ref)
-    copies = [
-        pltpu.make_async_copy(source, target, sems.at[at])
-        for at, (source, target) in enumerate(zip(given, held))
+def slots_kernel(info, senders, slots):
+    sender = senders[0, 0].astype(f32)
+    number = sender.shape[1]
+    dx, dy, count = [info[row : row + 1, :number].astype(f32) for row in range(3)]
+    ghosts = [
+        3.0 * (dx * (1 - column) + 1.0) + dy * (0, 1, -1)[line] + 1.0
+        for line in range(3)
+        for column in range(3)
     ]
-    for copy in copies:
-        copy.start()
-    dx, dy = ways[0], ways[1]
-    count = counts[0, 0, 0]
-    copies[0].wait()
-    live = []
-    for line in range(3):
-        for column in range(3):
-            ghost = 3 * (dx * (1 - column) + 1) + dy * (0, 1, -1)[line] + 1
-            found = jnp.int32(0)
-            for t in range(senders.shape[3]):
-                found = found | ((t < count) & (senders[0, 0, 0, t] == ghost)).astype(jnp.int32)
-            live.append(found)
-    far = live[6:]
-    begin = jnp.where(far[0] == 1, 0, jnp.where(far[1] == 1, 1, 2))
-    after = jnp.where(begin == 2, 0, jnp.where((begin == 0) & (far[1] == 1), 1, 2))
-    for row, number in enumerate([*live, far[0] + far[1] + far[2], begin, after]):
-        live_ref[row : row + 1, :] = jnp.full((1, live_ref.shape[1]), number, jnp.int32)
-    for copy in copies[1:]:
-        copy.wait()
-    cot_t_ref[...] = cot_out[...].astype(f32).T
-    square_t_ref[...] = square_out[...].astype(f32).T.astype(bf16)
-    first_t_ref[...] = lax.dot_general(
-        mix_out[...], cot_out[...], NT, preferred_element_type=f32
-    )
-    for path in range(2):
-        radial_t_ref[path] = radial_out[path].T
+    place = lax.broadcasted_iota(jnp.int32, (1, number), 1).astype(f32)
+    hits = [jnp.where((place < count) & (sender == ghost), 1.0, 0.0) for ghost in ghosts]
+    hits = jnp.concatenate(hits + [jnp.zeros((7, number), f32)], axis=0)
+    live = jnp.broadcast_to(jnp.max(hits, axis=1, keepdims=True), slots.shape)
+    far = [live[row : row + 1] for row in (6, 7, 8)]
+    begin = jnp.where(far[0] > 0.5, 0.0, jnp.where(far[1] > 0.5, 1.0, 2.0))
+    second = jnp.where((begin < 0.5) & (far[1] > 0.5), 1.0, 2.0)
+    after = jnp.where(begin > 1.5, 0.0, second)
+    rest = jnp.zeros((4, slots.shape[1]), f32)
+    slots[...] = jnp.concatenate(
+        [live[:9], far[0] + far[1] + far[2], begin, after, rest], axis=0
+    ).astype(jnp.int32)
 
 
 EARLY = ((0, 0), (0, 1), (0, 2), (1, 0), (1, 1), (1, 2))
@@ -174,7 +163,14 @@
     return [own_row.at[c] for c in range(3)] + [near_row.at[c] for c in range(3)]
 
 
-def early_kernel(table, own_row, near_row, radial_ref, basis, sums_ref, stacked):
+def early_kernel(
+    table, own_row, near_row, cot_arg, radial_arg, mix_arg, square_arg,
+    basis, sums_ref, cot_ref, radial_ref, mix_ref, square_ref, cot_t_ref, square_t_ref, first_t_ref,
+    radial_t_ref,
+    stacked, sems,
+):
+    held = (radial_ref, cot_ref, mix_ref, square_ref)
+    copies = start_copies(zip((radial_arg, cot_arg.at[0, 0], mix_arg, square_arg), held), sems)
     rows, channels = sums_ref.shape[1:]
     degrees = radial_ref.shape[1]
     _, recv = own_place(own_row, rows)
@@ -199,15 +195,24 @@
             stacked[block, :] = jnp.zeros((rows, 4 * channels), bf16)
             basis[:, block] = jnp.zeros((degrees * rows, rows), bf16)
 
+    for copy in copies:
+        copy.wait()
     for at, total in enumerate(gather(basis, stacked, radial_ref, None)):
         sums_ref[at] = total
+    cot_t_ref[...] = cot_ref[...].astype(f32).T
+    square_t_ref[...] = square_ref[...].astype(f32).T.astype(bf16)
+    first_t_ref[...] = lax.dot_general(
+        mix_ref[...], cot_ref[...], NT, preferred_element_type=f32
+    )
+    for path in range(2):
+        radial_t_ref[path] = radial_ref[path].T
 
 
 def middle_kernel(
-    table, far_row, own_row, sums_ref, cot_ref, cot_t_ref, square_ref, square_t_ref, first_t_ref,
+    table, far_sides, far_own, own_row, sums_ref, cot_ref, cot_t_ref, square_ref, square_t_ref, first_t_ref,
     radial_ref, radial_t_ref,
     far_out, grads, first_ref, second_ref,
-    basis, stacked, totals,
+    basis, stacked, totals, far_row,
 ):
     rows, channels = cot_ref.shape
     degrees = radial_ref.shape[1]
@@ -228,6 +233,9 @@
             totals[at] += part
 
     totals[...] = sums_ref[...]
+    far_row[0] = far_sides[0]
+    far_row[1] = far_own[0]
+    far_row[2] = far_sides[1]
     pl.when(few)(lambda: messages(order))
     pl.when(all_far)(lambda: messages([0, 1, 2]))
     sum_zero, sum_one, moments = totals[0], totals[1], [totals[2 + m] for m in range(3)]
@@ -285,24 +293,20 @@
     ).astype(bf16)
 
 
-def local(kernel, name, outs, scratch, args, flops=0, smem=0, copies=0):
+def local(kernel, name, outs, scratch, args, fetched=0):
     in_vmem = pl.BlockSpec(memory_space=pltpu.VMEM)
-    in_smem = pl.BlockSpec(memory_space=pltpu.SMEM)
-    given = in_vmem
-    if copies:
-        given = pl.BlockSpec(memory_space=pltpu.HBM)
-        args = args[:smem] + tuple(
-            pltpu.with_memory_space_constraint(arg, pltpu.HBM) for arg in args[smem:]
-        )
+    in_hbm = pl.BlockSpec(memory_space=pltpu.HBM)
+    near = len(args) - fetched
+    args = args[:near] + tuple(
+        pltpu.with_memory_space_constraint(arg, pltpu.HBM) for arg in args[near:]
+    )
     return pl.pallas_call(
         kernel,
         out_shape=tuple(jax.ShapeDtypeStruct(*out) for out in outs),
-        in_specs=[in_smem] * smem + [given] * (len(args) - smem),
+        in_specs=[in_vmem] * near + [in_hbm] * fetched,
         out_specs=(in_vmem,) * len(outs),
-        scratch_shapes=scratch
-        + ([pltpu.SemaphoreType.DMA((copies,))] if copies else []),
+        scratch_shapes=scratch + ([pltpu.SemaphoreType.DMA((fetched,))] if fetched else []),
         compiler_params=pltpu.CompilerParams(vmem_limit_bytes=32 * 2**20),
-        cost_estimate=pl.CostEstimate(flops=flops, bytes_accessed=2**20, transcendentals=0),
         name=name,
     )(*args)
 
@@ -311,22 +315,33 @@
     rows, channels = features.shape[2:]
     degrees = radial_w.shape[1]
     assert senders.shape[2] == 1 and rows == channels
-    ways = jnp.stack([2 * ahead("gx") - 1, 2 * ahead("gy") - 1])
     square = (rows, channels)
-    (packed,) = local(
+    packed, senders = local(
         pack_kernel,
         "pack",
-        [((1, rows + 16, channels), bf16)],
+        [((1, rows + 16, channels), bf16), (senders.shape, jnp.int32)],
         [pltpu.VMEM(positions.shape, bf16)],
-        (features, positions),
-        copies=2,
+        (features, positions, senders),
+        fetched=3,
     )
     last, first = swap(packed, "gx", 1), swap(packed, "gx", 0)
-    prepared = local(
-        prepare_kernel,
-        "prepare",
+    far_own = swap(packed, "gy", 1)
+    info = jnp.stack([2 * ahead("gx") - 1, 2 * ahead("gy") - 1, counts[0, 0, 0]])
+    info = jnp.broadcast_to(jnp.pad(info, (0, 5))[:, None], (8, rows))
+    later = lax.optimization_barrier(jnp.concatenate([packed, last], axis=0))
+    own_row = jnp.concatenate([first, later], axis=0)
+    far_sides = swap(jnp.concatenate([first, last], axis=0), "gy", 1)
+    near_row = swap(own_row, "gy", 0)
+    (live,) = local(slots_kernel, "slots", [((16, rows), jnp.int32)], [], (info, senders))
+    table = jnp.concatenate([info, live], axis=0)
+    table, far_own = lax.optimization_barrier((table, far_own))
+    slots = len(EARLY) * rows
+    basis, sums, cot, radial_w, mix_w, square_w, cot_t, square_t, first_t, radial_t = local(
+        early_kernel,
+        "early",
         [
-            ((16, rows), jnp.int32),
+            ((degrees * rows, slots), bf16),
+            ((5, rows, channels), f32),
             (square, bf16),
             (radial_w.shape, f32),
             (square, bf16),
@@ -336,26 +351,9 @@
             (square, f32),
             ((2, channels, degrees), f32),
         ],
-        [pltpu.SMEM(senders.shape, jnp.int32)],
-        (ways, counts, senders, cotangent, radial_w, mix_w, square_w),
-        flops=10**8,
-        smem=2,
-        copies=5,
-    )
-    last, first, ways, prepared = lax.optimization_barrier((last, first, ways, prepared))
-    live, cot, radial_w, mix_w, square_w, cot_t, square_t, first_t, radial_t = prepared
-    steps = jnp.broadcast_to(jnp.pad(ways, (0, 6))[:, None], (8, rows))
-    table = jnp.concatenate([steps, live], axis=0)
-    own_row = jnp.concatenate([first, packed, last], axis=0)
-    far_row, near_row = swap(own_row, "gy", 1), swap(own_row, "gy", 0)
-    slots = len(EARLY) * rows
-    basis, sums = local(
-        early_kernel,
-        "early",
-        [((degrees * rows, slots), bf16), ((5, rows, channels), f32)],
         [pltpu.VMEM((slots, 4 * channels), bf16)],
-        (table, own_row, near_row, radial_w),
-        flops=10**9,
+        (table, own_row, near_row, cotangent, radial_w, mix_w, square_w),
+        fetched=4,
     )
     slots = 3 * rows
     far_out, grads, first_bf, second_bf = local(
@@ -371,12 +369,12 @@
             pltpu.VMEM((degrees * rows, slots), bf16),
             pltpu.VMEM((slots, 4 * channels), bf16),
             pltpu.VMEM((5, rows, channels), f32),
+            pltpu.VMEM(own_row.shape, bf16),
         ],
         (
-            table, far_row, own_row, sums, cot, cot_t, square_w, square_t, first_t,
+            table, far_sides, far_own, own_row, sums, cot, cot_t, square_w, square_t, first_t,
             radial_w, radial_t,
         ),
-        flops=10**9,
     )
     far_in = swap_back(far_out, "gy", 1)
     near_out, own_out, updated = local(
@@ -385,7 +383,6 @@
         [((3, channels, rows), bf16), ((3, channels, rows), f32), (square, bf16)],
         [],
         (table, own_row, near_row, basis, grads, first_bf, second_bf, mix_w, square_w),
-        flops=10**9,
     )
     near_in = swap_back(near_out, "gy", 0)
     far_in = lax.optimization_barrier(far_in.astype(f32))

time: 30.3 us -> 30.6 us (level)
  starting transfers between devices: 12.2 us -> 14 us
  Pallas kernels: 6.59 us -> 5.07 us
    ppermute x8 -> x9, starting transfers between devices: 12.2 us -> 14 us  [swap(): return lax.ppermute(block, axis, pairs)]
    pallas_call x5, Pallas kernels: 6.59 us -> 5.07 us  [local(): pl.pallas_call(kernel, out_shape=tuple((jax.ShapeDtypeStruct(*out) for ou...]
    ppermute x8 -> x9, waiting for transfers between devices: 9.02 us -> 8.92 us  [swap(): return lax.ppermute(block, axis, pairs)]
  transfers between devices with their start and end apart: 8 -> 9, of which waited for: 6 -> 5; matrix products, arithmetic and copies ran while one was open for 1% -> 1% of each run, Pallas kernels for 17% -> 12%
where the time goes in v4:
time: 30.6 us; the launch traced here: 30.4 us
  starting transfers between devices  14 us (46%)
  waiting for transfers between devices  8.92 us (29%)
  Pallas kernels  5.07 us (17%)
  between operations  1.38 us (5%)
  local copies, waits for them, and re-layouts  0.82 us (3%)
    ppermute x9, starting transfers between devices, swap(): return lax.ppermute(block, axis, pairs)  14 us
    ppermute x9, waiting for transfers between devices, swap(): return lax.ppermute(block, axis, pairs)  8.92 us
    pallas_call x5, Pallas kernels, local(): pl.pallas_call(kernel, out_shape=tuple((jax.ShapeDtypeStruct(*out) for ou...  5.07 us
    unnamed x1, local copies, waits for them, and re-layouts  0.73 us
  transfers between devices with their start and end apart: 9, of which 5 were waited for; matrix products, arithmetic and copies ran while one was open for 1% of the time, Pallas kernels for 12%

profile of v4, /device:TPU:0, one launch (start us, length us, event | category | flops | bytes accessed | tf_op | source)
XLA Modules:
  0.0 30.4 jit_solution(17675989186171116035)
XLA Ops:
  0.6 0.8 %pack.1 = (bf16[1,144,128]{2,1,0:T(8,128)(2,1)S(1)}, s32[1,1,1,8]{3,2,1,0:T(1,128)S(1)}) custom-call(bf16[1,1,128,128]{3,2,1,0:T(8,128)(2,1)} %feat_ref.1, bf16[1,1,3,128]{3,2,1,0:T(4,128)(2,1)} %pos_ref.1, s32[1,1,1,8]{3,2,1,0:T(1,128)} %senders_ref.1), custom_call_target="tpu_custom_call" | custom-call | tf_op jit(solution)/shard_map/pack/pallas_call | solution.py:303
  1.4 4.0 %collective-permute-start.2 = (bf16[1,144,128]{2,1,0:T(8,128)(2,1)S(1)}, bf16[1,144,128]{2,1,0:T(8,128)(2,1)S(1)}, u32[]{:S(2)}, u32[]{:S(2)}) collective-permute-start(bf16[1,144,128]{2,1,0:T(8,128)(2,1)S(1)} %get-tuple-element.24), channel_id=1, source_target_pairs={{8,16},{16,8},{24,0},{0,24},{9,17},{17,9},{25,1},{1,25},{10,18},{1... | collective-permute-start | bytes 110600 | tf_op jit(solution)/shard_map/ppermute | solution.py:33
  5.4 0.5 %collective-permute-start.1 = (bf16[1,144,128]{2,1,0:T(8,128)(2,1)S(1)}, bf16[1,144,128]{2,1,0:T(8,128)(2,1)S(1)}, u32[]{:S(2)}, u32[]{:S(2)}) collective-permute-start(bf16[1,144,128]{2,1,0:T(8,128)(2,1)S(1)} %get-tuple-element.24), channel_id=1, source_target_pairs={{0,8},{8,0},{16,24},{24,16},{1,9},{9,1},{17,25},{25,17},{2,10},{10... | collective-permute-start | bytes 110600 | tf_op jit(solution)/shard_map/ppermute | solution.py:33
  5.9 2.5 %collective-permute-start = (bf16[1,144,128]{2,1,0:T(8,128)(2,1)S(1)}, bf16[1,144,128]{2,1,0:T(8,128)(2,1)S(1)}, u32[]{:S(2)}, u32[]{:S(2)}) collective-permute-start(bf16[1,144,128]{2,1,0:T(8,128)(2,1)S(1)} %get-tuple-element.24), channel_id=1, source_target_pairs={{1,2},{2,1},{3,4},{4,3},{5,6},{6,5},{7,0},{0,7},{9,10},{10,9},{11,... | collective-permute-start | bytes 110600 | tf_op jit(solution)/shard_map/ppermute | solution.py:33
  9.1 0.1 pad_add_fusion.1
  9.2 0.1 broadcast_in_dim.12.info
  9.2 0.1 slots.1
  9.3 0.0 collective-permute-done.2
  9.3 0.0 collective-permute-done.1
  9.4 2.2 %collective-permute-start.4 = (bf16[2,144,128]{2,1,0:T(8,128)(2,1)S(1)}, bf16[2,144,128]{2,1,0:T(8,128)(2,1)S(1)}, u32[]{:S(2)}, u32[]{:S(2)}) collective-permute-start(bf16[2,144,128]{2,1,0:T(8,128)(2,1)S(1)} %get-tuple-element.50), channel_id=1, source_target_pairs={{1,2},{2,1},{3,4},{4,3},{5,6},{6,5},{7,0},{0,7},{9,10},{10,9},{11,... | collective-permute-start | bytes 221192 | tf_op jit(solution)/shard_map/ppermute | solution.py:33
  11.5 0.1 collective-permute-start.3
  11.6 0.0 collective-permute-done.far_own
  11.6 1.3 %collective-permute-done.3.near_row = bf16[3,144,128]{2,1,0:T(8,128)(2,1)S(1)} collective-permute-done((bf16[3,144,128]{2,1,0:T(8,128)(2,1)S(1)}, bf16[3,144,128]{2,1,0:T(8,128)(2,1)S(1)}, u32[]{:S(2)}, u32[]{:S(2)}) %collective-permute-start.3) | collective-permute-done | bytes 110624 | tf_op jit(solution)/shard_map/ppermute | solution.py:33
  12.9 1.8 %early.1 = (bf16[1024,768]{1,0:T(8,128)(2,1)S(1)}, f32[5,128,128]{2,1,0:T(8,128)S(1)}, bf16[128,128]{1,0:T(8,128)(2,1)S(1)}, f32[2,8,128]{2,1,0:T(8,128)S(1)}, b...) custom-call(s32[24,128]{1,0:T(8,128)S(1)} %pad_add_fusion.table, ...), custom_call_target="tpu_custom_call" | custom-call | tf_op jit(solution)/shard_map/early/pallas_call | solution.py:303
  14.8 0.8 %collective-permute-done.4.far_sides = bf16[2,144,128]{2,1,0:T(8,128)(2,1)S(1)} collective-permute-done((bf16[2,144,128]{2,1,0:T(8,128)(2,1)S(1)}, bf16[2,144,128]{2,1,0:T(8,128)(2,1)S(1)}, u32[]{:S(2)}, u32[]{:S(2)}) %collective-permute-start.4) | collective-permute-done | bytes 73760 | tf_op jit(solution)/shard_map/ppermute | solution.py:33
  15.5 0.7 %middle.1 = (bf16[3,128,128]{2,1,0:T(8,128)(2,1)S(1)}, bf16[512,1024]{1,0:T(8,128)(2,1)S(1)}, bf16[128,128]{1,0:T(8,128)(2,1)S(1)}, bf16[384,128]{1,0:T(8,128)(2,1)S(1)}) custom-call(s32[24,128]{1,0:T(8,128)S(1)} %pad_add_fusion.table, bf16[2,144,128]{2,1,0:T(8,128)(2,1)S(1)} %collective-permute-done.4.far_sides, ...), custom_call_target="tpu_custom_call" | custom-call | tf_op jit(solution)/shard_map/middle/pallas_call | solution.py:303
  16.3 2.8 %collective-permute-start.6 = (bf16[3,128,128]{2,1,0:T(8,128)(2,1)S(1)}, bf16[3,128,128]{2,1,0:T(8,128)(2,1)S(1)}, u32[]{:S(2)}, u32[]{:S(2)}) collective-permute-start(bf16[3,128,128]{2,1,0:T(8,128)(2,1)S(1)} %get-tuple-element.43), channel_id=1, source_target_pairs={{1,2},{2,1},{3,4},{4,3},{5,6},{6,5},{7,0},{0,7},{9,10},{10,9},{11,... | collective-permute-start | bytes 294920 | tf_op jit(solution)/shard_map/ppermute | solution.py:33
  19.0 1.6 %late.1 = (bf16[3,128,128]{2,1,0:T(8,128)(2,1)S(1)}, f32[3,128,128]{2,1,0:T(8,128)S(1)}, bf16[128,128]{1,0:T(8,128)(2,1)}) custom-call(s32[24,128]{1,0:T(8,128)S(1)} %pad_add_fusion.table, bf16[3,144,128]{2,1,0:T(8,128)(2,1)S(1)} %pad_maximum_fusion.own_row, bf16[3,144,128]{2,1,0:T(8,128)(2,1)S(1)} %collective-permute-done.3.near_row, ...), custom_call_target="tpu_custom_call" | custom-call | tf_op jit(solution)/shard_map/late/pallas_call | solution.py:303
  20.7 0.0 collective-permute-start.5
  20.7 2.3 %collective-permute-done.6 = bf16[3,128,128]{2,1,0:T(8,128)(2,1)S(1)} collective-permute-done((bf16[3,128,128]{2,1,0:T(8,128)(2,1)S(1)}, bf16[3,128,128]{2,1,0:T(8,128)(2,1)S(1)}, u32[]{:S(2)}, u32[]{:S(2)}) %collective-permute-start.6) | collective-permute-done | bytes 98336 | tf_op jit(solution)/shard_map/ppermute | solution.py:33
  22.9 0.0 collective-permute-done.5
  23.0 1.8 %collective-permute-start.7 = (bf16[128,128]{1,0:T(8,128)(2,1)S(1)}, bf16[128,128]{1,0:T(8,128)(2,1)S(1)}, u32[]{:S(2)}, u32[]{:S(2)}) collective-permute-start(bf16[128,128]{1,0:T(8,128)(2,1)S(1)} %get-tuple-element.48), channel_id=1, source_target_pairs={{0,8},{8,0},{16,24},{24,16},{1,9},{9,1},{17,25},{25,17},{2,10},{10... | collective-permute-start | bytes 98312 | tf_op jit(solution)/shard_map/ppermute | solution.py:33
  24.8 0.2 collective-permute-start.8
  25.0 1.9 %collective-permute-done.7 = bf16[128,128]{1,0:T(8,128)(2,1)S(1)} collective-permute-done((bf16[128,128]{1,0:T(8,128)(2,1)S(1)}, bf16[128,128]{1,0:T(8,128)(2,1)S(1)}, u32[]{:S(2)}, u32[]{:S(2)}) %collective-permute-start.7) | collective-permute-done | bytes 32800 | tf_op jit(solution)/shard_map/ppermute | solution.py:33
  27.0 2.6 %collective-permute-done.8 = bf16[128,128]{1,0:T(8,128)(2,1)S(1)} collective-permute-done((bf16[128,128]{1,0:T(8,128)(2,1)S(1)}, bf16[128,128]{1,0:T(8,128)(2,1)S(1)}, u32[]{:S(2)}, u32[]{:S(2)}) %collective-permute-start.8) | collective-permute-done | bytes 32800 | tf_op jit(solution)/shard_map/ppermute | solution.py:33
  29.6 0.7 %copy.10 = f32[1,1,128,128]{3,2,1,0:T(8,128)} copy(f32[1,1,128,128]{2,3,1,0:T(8,128)S(1)} %fusion.1) | data formatting | bytes 131072
  (8 shorter events, 0.1 us)
Async XLA Ops:
  1.4 7.9 %collective-permute-start.2 = (bf16[1,144,128]{2,1,0:T(8,128)(2,1)S(1)}, bf16[1,144,128]{2,1,0:T(8,128)(2,1)S(1)}, u32[]{:S(2)}, u32[]{:S(2)}) collective-permute-start(bf16[1,144,128]{2,1,0:T(8,128)(2,1)S(1)} %get-tuple-element.24), channel_id=1, source_target_pairs={{8,16},{16,8},{24,0},{0,24},{9,17},{17,9},{25,1},{1,25},{10,18},{1... | collective-permute-start | bytes 110600 | tf_op jit(solution)/shard_map/ppermute | solution.py:33
  5.4 4.0 %collective-permute-start.1 = (bf16[1,144,128]{2,1,0:T(8,128)(2,1)S(1)}, bf16[1,144,128]{2,1,0:T(8,128)(2,1)S(1)}, u32[]{:S(2)}, u32[]{:S(2)}) collective-permute-start(bf16[1,144,128]{2,1,0:T(8,128)(2,1)S(1)} %get-tuple-element.24), channel_id=1, source_target_pairs={{0,8},{8,0},{16,24},{24,16},{1,9},{9,1},{17,25},{25,17},{2,10},{10... | collective-permute-start | bytes 110600 | tf_op jit(solution)/shard_map/ppermute | solution.py:33
  5.9 5.7 %collective-permute-start = (bf16[1,144,128]{2,1,0:T(8,128)(2,1)S(1)}, bf16[1,144,128]{2,1,0:T(8,128)(2,1)S(1)}, u32[]{:S(2)}, u32[]{:S(2)}) collective-permute-start(bf16[1,144,128]{2,1,0:T(8,128)(2,1)S(1)} %get-tuple-element.24), channel_id=1, source_target_pairs={{1,2},{2,1},{3,4},{4,3},{5,6},{6,5},{7,0},{0,7},{9,10},{10,9},{11,... | collective-permute-start | bytes 110600 | tf_op jit(solution)/shard_map/ppermute | solution.py:33
  9.4 6.2 %collective-permute-start.4 = (bf16[2,144,128]{2,1,0:T(8,128)(2,1)S(1)}, bf16[2,144,128]{2,1,0:T(8,128)(2,1)S(1)}, u32[]{:S(2)}, u32[]{:S(2)}) collective-permute-start(bf16[2,144,128]{2,1,0:T(8,128)(2,1)S(1)} %get-tuple-element.50), channel_id=1, source_target_pairs={{1,2},{2,1},{3,4},{4,3},{5,6},{6,5},{7,0},{0,7},{9,10},{10,9},{11,... | collective-permute-start | bytes 221192 | tf_op jit(solution)/shard_map/ppermute | solution.py:33
  11.5 1.4 %collective-permute-start.3 = (bf16[3,144,128]{2,1,0:T(8,128)(2,1)S(1)}, bf16[3,144,128]{2,1,0:T(8,128)(2,1)S(1)}, u32[]{:S(2)}, u32[]{:S(2)}) collective-permute-start(bf16[3,144,128]{2,1,0:T(8,128)(2,1)S(1)} %pad_maximum_fusion.own_row), channel_id=1, source_target_pairs={{0,1},{1,0},{2,3},{3,2},{4,5},{5,4},{6,7},{7,6},{8,9},{9,8},{10,11... | collective-permute-start | bytes 331784 | tf_op jit(solution)/shard_map/ppermute | solution.py:33
  16.3 6.7 %collective-permute-start.6 = (bf16[3,128,128]{2,1,0:T(8,128)(2,1)S(1)}, bf16[3,128,128]{2,1,0:T(8,128)(2,1)S(1)}, u32[]{:S(2)}, u32[]{:S(2)}) collective-permute-start(bf16[3,128,128]{2,1,0:T(8,128)(2,1)S(1)} %get-tuple-element.43), channel_id=1, source_target_pairs={{1,2},{2,1},{3,4},{4,3},{5,6},{6,5},{7,0},{0,7},{9,10},{10,9},{11,... | collective-permute-start | bytes 294920 | tf_op jit(solution)/shard_map/ppermute | solution.py:33
  20.7 2.3 %collective-permute-start.5 = (bf16[3,128,128]{2,1,0:T(8,128)(2,1)S(1)}, bf16[3,128,128]{2,1,0:T(8,128)(2,1)S(1)}, u32[]{:S(2)}, u32[]{:S(2)}) collective-permute-start(bf16[3,128,128]{2,1,0:T(8,128)(2,1)S(1)} %get-tuple-element.42), channel_id=1, source_target_pairs={{0,1},{1,0},{2,3},{3,2},{4,5},{5,4},{6,7},{7,6},{8,9},{9,8},{10,11... | collective-permute-start | bytes 294920 | tf_op jit(solution)/shard_map/ppermute | solution.py:33
  23.0 4.0 %collective-permute-start.7 = (bf16[128,128]{1,0:T(8,128)(2,1)S(1)}, bf16[128,128]{1,0:T(8,128)(2,1)S(1)}, u32[]{:S(2)}, u32[]{:S(2)}) collective-permute-start(bf16[128,128]{1,0:T(8,128)(2,1)S(1)} %get-tuple-element.48), channel_id=1, source_target_pairs={{0,8},{8,0},{16,24},{24,16},{1,9},{9,1},{17,25},{25,17},{2,10},{10... | collective-permute-start | bytes 98312 | tf_op jit(solution)/shard_map/ppermute | solution.py:33
  24.8 4.8 %collective-permute-start.8 = (bf16[128,128]{1,0:T(8,128)(2,1)S(1)}, bf16[128,128]{1,0:T(8,128)(2,1)S(1)}, u32[]{:S(2)}, u32[]{:S(2)}) collective-permute-start(bf16[128,128]{1,0:T(8,128)(2,1)S(1)} %get-tuple-element.49), channel_id=1, source_target_pairs={{8,16},{16,8},{24,0},{0,24},{9,17},{17,9},{25,1},{1,25},{10,18},{1... | collective-permute-start | bytes 98312 | tf_op jit(solution)/shard_map/ppermute | solution.py:33

commit v5 on v4

--- a/solution.py
+++ b/solution.py
@@ -133,10 +133,11 @@
         out[...] = total.astype(out.dtype)
 
 
-def slots_kernel(info, senders, slots):
+def fill_table(steps, count, senders, table):
     sender = senders[0, 0].astype(f32)
     number = sender.shape[1]
-    dx, dy, count = [info[row : row + 1, :number].astype(f32) for row in range(3)]
+    dx, dy = [steps[row : row + 1, :number].astype(f32) for row in range(2)]
+    count = count[:1, :number].astype(f32)
     ghosts = [
         3.0 * (dx * (1 - column) + 1.0) + dy * (0, 1, -1)[line] + 1.0
         for line in range(3)
@@ -145,13 +146,14 @@
     place = lax.broadcasted_iota(jnp.int32, (1, number), 1).astype(f32)
     hits = [jnp.where((place < count) & (sender == ghost), 1.0, 0.0) for ghost in ghosts]
     hits = jnp.concatenate(hits + [jnp.zeros((7, number), f32)], axis=0)
-    live = jnp.broadcast_to(jnp.max(hits, axis=1, keepdims=True), slots.shape)
+    live = jnp.broadcast_to(jnp.max(hits, axis=1, keepdims=True), (16, table.shape[1]))
     far = [live[row : row + 1] for row in (6, 7, 8)]
     begin = jnp.where(far[0] > 0.5, 0.0, jnp.where(far[1] > 0.5, 1.0, 2.0))
     second = jnp.where((begin < 0.5) & (far[1] > 0.5), 1.0, 2.0)
     after = jnp.where(begin > 1.5, 0.0, second)
-    rest = jnp.zeros((4, slots.shape[1]), f32)
-    slots[...] = jnp.concatenate(
+    rest = jnp.zeros((4, table.shape[1]), f32)
+    table[:LIVE, :] = steps[...]
+    table[LIVE:, :] = jnp.concatenate(
         [live[:9], far[0] + far[1] + far[2], begin, after, rest], axis=0
     ).astype(jnp.int32)
 
@@ -164,8 +166,8 @@
 
 
 def early_kernel(
-    table, own_row, near_row, cot_arg, radial_arg, mix_arg, square_arg,
-    basis, sums_ref, cot_ref, radial_ref, mix_ref, square_ref, cot_t_ref, square_t_ref, first_t_ref,
+    steps, number, senders, own_row, near_row, cot_arg, radial_arg, mix_arg, square_arg,
+    table, basis, sums_ref, cot_ref, radial_ref, mix_ref, square_ref, cot_t_ref, square_t_ref, first_t_ref,
     radial_t_ref,
     stacked, sems,
 ):
@@ -173,6 +175,7 @@
     copies = start_copies(zip((radial_arg, cot_arg.at[0, 0], mix_arg, square_arg), held), sems)
     rows, channels = sums_ref.shape[1:]
     degrees = radial_ref.shape[1]
+    fill_table(steps, number, senders, table)
     _, recv = own_place(own_row, rows)
     others = (
         lax.broadcasted_iota(jnp.int32, (rows, rows), 0)
@@ -326,20 +329,19 @@
     )
     last, first = swap(packed, "gx", 1), swap(packed, "gx", 0)
     far_own = swap(packed, "gy", 1)
-    info = jnp.stack([2 * ahead("gx") - 1, 2 * ahead("gy") - 1, counts[0, 0, 0]])
-    info = jnp.broadcast_to(jnp.pad(info, (0, 5))[:, None], (8, rows))
     later = lax.optimization_barrier(jnp.concatenate([packed, last], axis=0))
     own_row = jnp.concatenate([first, later], axis=0)
     far_sides = swap(jnp.concatenate([first, last], axis=0), "gy", 1)
     near_row = swap(own_row, "gy", 0)
-    (live,) = local(slots_kernel, "slots", [((16, rows), jnp.int32)], [], (info, senders))
-    table = jnp.concatenate([info, live], axis=0)
-    table, far_own = lax.optimization_barrier((table, far_own))
+    steps = jnp.stack([2 * ahead("gx") - 1, 2 * ahead("gy") - 1])
+    steps = jnp.broadcast_to(jnp.pad(steps, (0, 6))[:, None], (8, rows))
+    number = jnp.broadcast_to(counts[0], (8, rows))
     slots = len(EARLY) * rows
-    basis, sums, cot, radial_w, mix_w, square_w, cot_t, square_t, first_t, radial_t = local(
+    table, basis, sums, cot, radial_w, mix_w, square_w, cot_t, square_t, first_t, radial_t = local(
         early_kernel,
         "early",
         [
+            ((LIVE + 16, rows), jnp.int32),
             ((degrees * rows, slots), bf16),
             ((5, rows, channels), f32),
             (square, bf16),
@@ -352,7 +354,7 @@
             ((2, channels, degrees), f32),
         ],
         [pltpu.VMEM((slots, 4 * channels), bf16)],
-        (table, own_row, near_row, cotangent, radial_w, mix_w, square_w),
+        (steps, number, senders, own_row, near_row, cotangent, radial_w, mix_w, square_w),
         fetched=4,
     )
     slots = 3 * rows
@@ -389,7 +391,8 @@
     line = own_out + (near_in.astype(f32) + far_in)
     sent = line.astype(bf16)
     last_in, first_in = swap_back(sent[2], "gx", 1), swap_back(sent[0], "gx", 0)
-    collected = (line[1] + (first_in.astype(f32) + last_in.astype(f32))).T
+    partial = lax.optimization_barrier(line[1] + last_in.astype(f32))
+    collected = (partial + first_in.astype(f32)).T
     return (updated[None, None], collected[None, None])
 
 

time: 30.6 us -> 29.5 us (0.964); the launches traced: 30.4 us -> 29.6 us
  starting transfers between devices: 14 us -> 12.9 us
  Pallas kernels: 5.07 us -> 6.1 us
  waiting for transfers between devices: 8.92 us -> 8.25 us
    ppermute x9, starting transfers between devices: 14 us -> 12.9 us  [swap(): return lax.ppermute(block, axis, pairs)]
    pallas_call x5 -> x4, Pallas kernels: 5.07 us -> 6.1 us  [local(): pl.pallas_call(kernel, out_shape=tuple((jax.ShapeDtypeStruct(*out) for ou...]
    ppermute x9, waiting for transfers between devices: 8.92 us -> 8.25 us  [swap(): return lax.ppermute(block, axis, pairs)]
  transfers between devices with their start and end apart: 9 -> 9, of which waited for: 5 -> 6; matrix products, arithmetic and copies ran while one was open for 1% -> 1% of each run, Pallas kernels for 12% -> 12%
where the time goes in v5:
time: 29.5 us; the launch traced here: 29.6 us
  starting transfers between devices  12.9 us (44%)
  waiting for transfers between devices  8.25 us (28%)
  Pallas kernels  6.1 us (21%)
  between operations  1.37 us (5%)
  local copies, waits for them, and re-layouts  0.81 us (3%)
    ppermute x9, starting transfers between devices, swap(): return lax.ppermute(block, axis, pairs)  12.9 us
    ppermute x9, waiting for transfers between devices, swap(): return lax.ppermute(block, axis, pairs)  8.25 us
    pallas_call x4, Pallas kernels, local(): pl.pallas_call(kernel, out_shape=tuple((jax.ShapeDtypeStruct(*out) for ou...  6.1 us
    unnamed x1, local copies, waits for them, and re-layouts  0.73 us
  transfers between devices with their start and end apart: 9, of which 6 were waited for; matrix products, arithmetic and copies ran while one was open for 1% of the time, Pallas kernels for 12%

profile of v5, /device:TPU:0, one launch (start us, length us, event | category | flops | bytes accessed | tf_op | source)
XLA Modules:
  0.0 29.6 jit_solution(9231069602511890254)
XLA Ops:
  0.6 0.8 %pack.1 = (bf16[1,144,128]{2,1,0:T(8,128)(2,1)S(1)}, s32[1,1,1,8]{3,2,1,0:T(1,128)S(1)}) custom-call(bf16[1,1,128,128]{3,2,1,0:T(8,128)(2,1)} %feat_ref.1, bf16[1,1,3,128]{3,2,1,0:T(4,128)(2,1)} %pos_ref.1, s32[1,1,1,8]{3,2,1,0:T(1,128)} %senders_ref.1), custom_call_target="tpu_custom_call" | custom-call | tf_op jit(solution)/shard_map/pack/pallas_call | solution.py:306
  1.4 4.0 %collective-permute-start.1 = (bf16[1,144,128]{2,1,0:T(8,128)(2,1)S(1)}, bf16[1,144,128]{2,1,0:T(8,128)(2,1)S(1)}, u32[]{:S(2)}, u32[]{:S(2)}) collective-permute-start(bf16[1,144,128]{2,1,0:T(8,128)(2,1)S(1)} %get-tuple-element.23), channel_id=1, source_target_pairs={{8,16},{16,8},{24,0},{0,24},{9,17},{17,9},{25,1},{1,25},{10,18},{1... | collective-permute-start | bytes 110600 | tf_op jit(solution)/shard_map/ppermute | solution.py:33
  5.4 0.5 %collective-permute-start = (bf16[1,144,128]{2,1,0:T(8,128)(2,1)S(1)}, bf16[1,144,128]{2,1,0:T(8,128)(2,1)S(1)}, u32[]{:S(2)}, u32[]{:S(2)}) collective-permute-start(bf16[1,144,128]{2,1,0:T(8,128)(2,1)S(1)} %get-tuple-element.23), channel_id=1, source_target_pairs={{0,8},{8,0},{16,24},{24,16},{1,9},{9,1},{17,25},{25,17},{2,10},{10... | collective-permute-start | bytes 110600 | tf_op jit(solution)/shard_map/ppermute | solution.py:33
  5.9 2.5 %collective-permute-start.4 = (bf16[1,144,128]{2,1,0:T(8,128)(2,1)S(1)}, bf16[1,144,128]{2,1,0:T(8,128)(2,1)S(1)}, u32[]{:S(2)}, u32[]{:S(2)}) collective-permute-start(bf16[1,144,128]{2,1,0:T(8,128)(2,1)S(1)} %get-tuple-element.23), channel_id=1, source_target_pairs={{1,2},{2,1},{3,4},{4,3},{5,6},{6,5},{7,0},{0,7},{9,10},{10,9},{11,... | collective-permute-start | bytes 110600 | tf_op jit(solution)/shard_map/ppermute | solution.py:33
  8.4 0.0 collective-permute-done.1
  8.4 0.9 %collective-permute-done = bf16[1,144,128]{2,1,0:T(8,128)(2,1)S(1)} collective-permute-done((bf16[1,144,128]{2,1,0:T(8,128)(2,1)S(1)}, bf16[1,144,128]{2,1,0:T(8,128)(2,1)S(1)}, u32[]{:S(2)}, u32[]{:S(2)}) %collective-permute-start) | collective-permute-done | bytes 36896 | tf_op jit(solution)/shard_map/ppermute | solution.py:33
  9.4 2.2 %collective-permute-start.3 = (bf16[2,144,128]{2,1,0:T(8,128)(2,1)S(1)}, bf16[2,144,128]{2,1,0:T(8,128)(2,1)S(1)}, u32[]{:S(2)}, u32[]{:S(2)}) collective-permute-start(bf16[2,144,128]{2,1,0:T(8,128)(2,1)S(1)} %get-tuple-element.48), channel_id=1, source_target_pairs={{1,2},{2,1},{3,4},{4,3},{5,6},{6,5},{7,0},{0,7},{9,10},{10,9},{11,... | collective-permute-start | bytes 221192 | tf_op jit(solution)/shard_map/ppermute | solution.py:33
  11.5 0.1 collective-permute-start.2
  11.6 0.1 pad_add_fusion
  12.4 0.6 %collective-permute-done.2.near_row = bf16[3,144,128]{2,1,0:T(8,128)(2,1)S(1)} collective-permute-done((bf16[3,144,128]{2,1,0:T(8,128)(2,1)S(1)}, bf16[3,144,128]{2,1,0:T(8,128)(2,1)S(1)}, u32[]{:S(2)}, u32[]{:S(2)}) %collective-permute-start.2) | collective-permute-done | bytes 110624 | tf_op jit(solution)/shard_map/ppermute | solution.py:33
  12.9 0.1 broadcast_in_dim.19.steps
  13.0 1.8 %early.1 = (s32[24,128]{1,0:T(8,128)S(1)}, bf16[1024,768]{1,0:T(8,128)(2,1)S(1)}, f32[5,128,128]{2,1,0:T(8,128)S(1)}, bf16[128,128]{1,0:T(8,128)(2,1)S(1)}, f32[...) custom-call(s32[8,128]{1,0:T(8,128)S(1)} %broadcast_in_dim.19.steps,, ...), custom_call_target="tpu_custom_call" | custom-call | tf_op jit(solution)/shard_map/early/pallas_call | solution.py:306
  14.8 0.0 collective-permute-done.4.far_own
  14.9 0.7 %collective-permute-done.3.far_sides = bf16[2,144,128]{2,1,0:T(8,128)(2,1)S(1)} collective-permute-done((bf16[2,144,128]{2,1,0:T(8,128)(2,1)S(1)}, bf16[2,144,128]{2,1,0:T(8,128)(2,1)S(1)}, u32[]{:S(2)}, u32[]{:S(2)}) %collective-permute-start.3) | collective-permute-done | bytes 73760 | tf_op jit(solution)/shard_map/ppermute | solution.py:33
  15.5 1.8 %middle.1 = (bf16[3,128,128]{2,1,0:T(8,128)(2,1)S(1)}, bf16[512,1024]{1,0:T(8,128)(2,1)S(1)}, bf16[128,128]{1,0:T(8,128)(2,1)S(1)}, bf16[384,128]{1,0:T(8,128)(2,1)S(1)}) custom-call(s32[24,128]{1,0:T(8,128)S(1)} %get-tuple-element.24.table, bf16[2,144,128]{2,1,0:T(8,128)(2,1)S(1)} %collective-permute-done.3.far_sides, ...), custom_call_target="tpu_custom_call" | custom-call | tf_op jit(solution)/shard_map/middle/pallas_call | solution.py:306
  17.4 1.6 %collective-permute-start.6 = (bf16[3,128,128]{2,1,0:T(8,128)(2,1)S(1)}, bf16[3,128,128]{2,1,0:T(8,128)(2,1)S(1)}, u32[]{:S(2)}, u32[]{:S(2)}) collective-permute-start(bf16[3,128,128]{2,1,0:T(8,128)(2,1)S(1)} %get-tuple-element.41), channel_id=1, source_target_pairs={{1,2},{2,1},{3,4},{4,3},{5,6},{6,5},{7,0},{0,7},{9,10},{10,9},{11,... | collective-permute-start | bytes 294920 | tf_op jit(solution)/shard_map/ppermute | solution.py:33
  19.0 1.6 %late.1 = (bf16[3,128,128]{2,1,0:T(8,128)(2,1)S(1)}, f32[3,128,128]{2,1,0:T(8,128)S(1)}, bf16[128,128]{1,0:T(8,128)(2,1)}) custom-call(s32[24,128]{1,0:T(8,128)S(1)} %get-tuple-element.24.table, bf16[3,144,128]{2,1,0:T(8,128)(2,1)S(1)} %pad_maximum_fusion.own_row, bf16[3,144,128]{2,1,0:T(8,128)(2,1)S(1)} %collective-permute-done.2.near_row, ...), custom_call_target="tpu_custom_call" | custom-call | tf_op jit(solution)/shard_map/late/pallas_call | solution.py:306
  20.7 0.0 collective-permute-start.5
  20.7 2.6 %collective-permute-done.6 = bf16[3,128,128]{2,1,0:T(8,128)(2,1)S(1)} collective-permute-done((bf16[3,128,128]{2,1,0:T(8,128)(2,1)S(1)}, bf16[3,128,128]{2,1,0:T(8,128)(2,1)S(1)}, u32[]{:S(2)}, u32[]{:S(2)}) %collective-permute-start.6) | collective-permute-done | bytes 98336 | tf_op jit(solution)/shard_map/ppermute | solution.py:33
  23.3 0.0 collective-permute-done.5
  23.4 1.6 %collective-permute-start.7 = (bf16[128,128]{1,0:T(8,128)(2,1)S(1)}, bf16[128,128]{1,0:T(8,128)(2,1)S(1)}, u32[]{:S(2)}, u32[]{:S(2)}) collective-permute-start(bf16[128,128]{1,0:T(8,128)(2,1)S(1)} %get-tuple-element.47), channel_id=1, source_target_pairs={{8,16},{16,8},{24,0},{0,24},{9,17},{17,9},{25,1},{1,25},{10,18},{1... | collective-permute-start | bytes 98312 | tf_op jit(solution)/shard_map/ppermute | solution.py:33
  24.9 0.5 %collective-permute-start.8 = (bf16[128,128]{1,0:T(8,128)(2,1)S(1)}, bf16[128,128]{1,0:T(8,128)(2,1)S(1)}, u32[]{:S(2)}, u32[]{:S(2)}) collective-permute-start(bf16[128,128]{1,0:T(8,128)(2,1)S(1)} %get-tuple-element.46), channel_id=1, source_target_pairs={{0,8},{8,0},{16,24},{24,16},{1,9},{9,1},{17,25},{25,17},{2,10},{10... | collective-permute-start | bytes 98312 | tf_op jit(solution)/shard_map/ppermute | solution.py:33
  25.4 2.8 %collective-permute-done.7 = bf16[128,128]{1,0:T(8,128)(2,1)S(1)} collective-permute-done((bf16[128,128]{1,0:T(8,128)(2,1)S(1)}, bf16[128,128]{1,0:T(8,128)(2,1)S(1)}, u32[]{:S(2)}, u32[]{:S(2)}) %collective-permute-start.7) | collective-permute-done | bytes 32800 | tf_op jit(solution)/shard_map/ppermute | solution.py:33
  28.3 0.6 %collective-permute-done.8 = bf16[128,128]{1,0:T(8,128)(2,1)S(1)} collective-permute-done((bf16[128,128]{1,0:T(8,128)(2,1)S(1)}, bf16[128,128]{1,0:T(8,128)(2,1)S(1)}, u32[]{:S(2)}, u32[]{:S(2)}) %collective-permute-start.8) | collective-permute-done | bytes 32800 | tf_op jit(solution)/shard_map/ppermute | solution.py:33
  28.9 0.7 %copy.10 = f32[1,1,128,128]{3,2,1,0:T(8,128)} copy(f32[1,1,128,128]{2,3,1,0:T(8,128)S(1)} %add_bitcast_fusion) | data formatting | bytes 131072
  (9 shorter events, 0.1 us)
Async XLA Ops:
  1.4 7.0 %collective-permute-start.1 = (bf16[1,144,128]{2,1,0:T(8,128)(2,1)S(1)}, bf16[1,144,128]{2,1,0:T(8,128)(2,1)S(1)}, u32[]{:S(2)}, u32[]{:S(2)}) collective-permute-start(bf16[1,144,128]{2,1,0:T(8,128)(2,1)S(1)} %get-tuple-element.23), channel_id=1, source_target_pairs={{8,16},{16,8},{24,0},{0,24},{9,17},{17,9},{25,1},{1,25},{10,18},{1... | collective-permute-start | bytes 110600 | tf_op jit(solution)/shard_map/ppermute | solution.py:33
  5.4 4.0 %collective-permute-start = (bf16[1,144,128]{2,1,0:T(8,128)(2,1)S(1)}, bf16[1,144,128]{2,1,0:T(8,128)(2,1)S(1)}, u32[]{:S(2)}, u32[]{:S(2)}) collective-permute-start(bf16[1,144,128]{2,1,0:T(8,128)(2,1)S(1)} %get-tuple-element.23), channel_id=1, source_target_pairs={{0,8},{8,0},{16,24},{24,16},{1,9},{9,1},{17,25},{25,17},{2,10},{10... | collective-permute-start | bytes 110600 | tf_op jit(solution)/shard_map/ppermute | solution.py:33
  5.9 8.9 %collective-permute-start.4 = (bf16[1,144,128]{2,1,0:T(8,128)(2,1)S(1)}, bf16[1,144,128]{2,1,0:T(8,128)(2,1)S(1)}, u32[]{:S(2)}, u32[]{:S(2)}) collective-permute-start(bf16[1,144,128]{2,1,0:T(8,128)(2,1)S(1)} %get-tuple-element.23), channel_id=1, source_target_pairs={{1,2},{2,1},{3,4},{4,3},{5,6},{6,5},{7,0},{0,7},{9,10},{10,9},{11,... | collective-permute-start | bytes 110600 | tf_op jit(solution)/shard_map/ppermute | solution.py:33
  9.4 6.2 %collective-permute-start.3 = (bf16[2,144,128]{2,1,0:T(8,128)(2,1)S(1)}, bf16[2,144,128]{2,1,0:T(8,128)(2,1)S(1)}, u32[]{:S(2)}, u32[]{:S(2)}) collective-permute-start(bf16[2,144,128]{2,1,0:T(8,128)(2,1)S(1)} %get-tuple-element.48), channel_id=1, source_target_pairs={{1,2},{2,1},{3,4},{4,3},{5,6},{6,5},{7,0},{0,7},{9,10},{10,9},{11,... | collective-permute-start | bytes 221192 | tf_op jit(solution)/shard_map/ppermute | solution.py:33
  11.5 1.4 %collective-permute-start.2 = (bf16[3,144,128]{2,1,0:T(8,128)(2,1)S(1)}, bf16[3,144,128]{2,1,0:T(8,128)(2,1)S(1)}, u32[]{:S(2)}, u32[]{:S(2)}) collective-permute-start(bf16[3,144,128]{2,1,0:T(8,128)(2,1)S(1)} %pad_maximum_fusion.own_row), channel_id=1, source_target_pairs={{0,1},{1,0},{2,3},{3,2},{4,5},{5,4},{6,7},{7,6},{8,9},{9,8},{10,11... | collective-permute-start | bytes 331784 | tf_op jit(solution)/shard_map/ppermute | solution.py:33
  17.4 5.9 %collective-permute-start.6 = (bf16[3,128,128]{2,1,0:T(8,128)(2,1)S(1)}, bf16[3,128,128]{2,1,0:T(8,128)(2,1)S(1)}, u32[]{:S(2)}, u32[]{:S(2)}) collective-permute-start(bf16[3,128,128]{2,1,0:T(8,128)(2,1)S(1)} %get-tuple-element.41), channel_id=1, source_target_pairs={{1,2},{2,1},{3,4},{4,3},{5,6},{6,5},{7,0},{0,7},{9,10},{10,9},{11,... | collective-permute-start | bytes 294920 | tf_op jit(solution)/shard_map/ppermute | solution.py:33
  20.7 2.7 %collective-permute-start.5 = (bf16[3,128,128]{2,1,0:T(8,128)(2,1)S(1)}, bf16[3,128,128]{2,1,0:T(8,128)(2,1)S(1)}, u32[]{:S(2)}, u32[]{:S(2)}) collective-permute-start(bf16[3,128,128]{2,1,0:T(8,128)(2,1)S(1)} %get-tuple-element.40), channel_id=1, source_target_pairs={{0,1},{1,0},{2,3},{3,2},{4,5},{5,4},{6,7},{7,6},{8,9},{9,8},{10,11... | collective-permute-start | bytes 294920 | tf_op jit(solution)/shard_map/ppermute | solution.py:33
  23.4 4.9 %collective-permute-start.7 = (bf16[128,128]{1,0:T(8,128)(2,1)S(1)}, bf16[128,128]{1,0:T(8,128)(2,1)S(1)}, u32[]{:S(2)}, u32[]{:S(2)}) collective-permute-start(bf16[128,128]{1,0:T(8,128)(2,1)S(1)} %get-tuple-element.47), channel_id=1, source_target_pairs={{8,16},{16,8},{24,0},{0,24},{9,17},{17,9},{25,1},{1,25},{10,18},{1... | collective-permute-start | bytes 98312 | tf_op jit(solution)/shard_map/ppermute | solution.py:33
  24.9 3.9 %collective-permute-start.8 = (bf16[128,128]{1,0:T(8,128)(2,1)S(1)}, bf16[128,128]{1,0:T(8,128)(2,1)S(1)}, u32[]{:S(2)}, u32[]{:S(2)}) collective-permute-start(bf16[128,128]{1,0:T(8,128)(2,1)S(1)} %get-tuple-element.46), channel_id=1, source_target_pairs={{0,8},{8,0},{16,24},{24,16},{1,9},{9,1},{17,25},{25,17},{2,10},{10... | collective-permute-start | bytes 98312 | tf_op jit(solution)/shard_map/ppermute | solution.py:33

commit v6 on v5

--- a/solution.py
+++ b/solution.py
@@ -168,7 +168,7 @@
 def early_kernel(
     steps, number, senders, own_row, near_row, cot_arg, radial_arg, mix_arg, square_arg,
     table, basis, sums_ref, cot_ref, radial_ref, mix_ref, square_ref, cot_t_ref, square_t_ref, first_t_ref,
-    radial_t_ref,
+    radial_t_ref, recv_ref,
     stacked, sems,
 ):
     held = (radial_ref, cot_ref, mix_ref, square_ref)
@@ -177,6 +177,8 @@
     degrees = radial_ref.shape[1]
     fill_table(steps, number, senders, table)
     _, recv = own_place(own_row, rows)
+    for m in range(3):
+        recv_ref[m] = recv[m]
     others = (
         lax.broadcasted_iota(jnp.int32, (rows, rows), 0)
         != lax.broadcasted_iota(jnp.int32, (rows, rows), 1)
@@ -208,18 +210,21 @@
         mix_ref[...], cot_ref[...], NT, preferred_element_type=f32
     )
     for path in range(2):
-        radial_t_ref[path] = radial_ref[path].T
+        columns = radial_ref[path].T
+        for k in range(degrees):
+            radial_t_ref[path, k] = jnp.broadcast_to(columns[:, k : k + 1], (channels, rows))
 
 
 def middle_kernel(
     table, far_sides, far_own, own_row, sums_ref, cot_ref, cot_t_ref, square_ref, square_t_ref, first_t_ref,
-    radial_ref, radial_t_ref,
+    radial_ref, radial_t_ref, recv_ref,
     far_out, grads, first_ref, second_ref,
     basis, stacked, totals, far_row,
 ):
     rows, channels = cot_ref.shape
     degrees = radial_ref.shape[1]
-    lines, recv = own_place(own_row, rows)
+    pos = own_row[1, rows:, :].astype(f32)
+    lines, recv = [pos[m : m + 1] for m in range(3)], [recv_ref[m] for m in range(3)]
     far_count = table[FAR_COUNT, 0]
     order = [table[FAR_ORDER, 0], table[FAR_ORDER + 1, 0]]
     few, all_far = (far_count == 1) | (far_count == 2), far_count == 3
@@ -233,9 +238,12 @@
             add_tile(source, place, recv, weight, basis, stacked, at, degrees)
         parts = gather(basis.at[:, :width], stacked.at[:width], radial_ref, None)
         for at, part in enumerate(parts):
-            totals[at] += part
-
-    totals[...] = sums_ref[...]
+            totals[at] = sums_ref[at] + part
+
+    @pl.when(far_count == 0)
+    def _():
+        totals[...] = sums_ref[...]
+
     far_row[0] = far_sides[0]
     far_row[1] = far_own[0]
     far_row[2] = far_sides[1]
@@ -261,7 +269,7 @@
     one_t = -(lines[0] * second_t[0] + lines[1] * second_t[1] + lines[2] * second_t[2])
     first_t = first_t_ref[...]
     for k in range(degrees):
-        zero, one = radial_t_ref[0, :, k : k + 1], radial_t_ref[1, :, k : k + 1]
+        zero, one = radial_t_ref[0, k], radial_t_ref[1, k]
         span = slice(k * rows, (k + 1) * rows)
         grads[0:channels, span] = (zero * first_t + one * one_t).astype(bf16)
         for m in range(3):
@@ -337,7 +345,7 @@
     steps = jnp.broadcast_to(jnp.pad(steps, (0, 6))[:, None], (8, rows))
     number = jnp.broadcast_to(counts[0], (8, rows))
     slots = len(EARLY) * rows
-    table, basis, sums, cot, radial_w, mix_w, square_w, cot_t, square_t, first_t, radial_t = local(
+    table, basis, sums, cot, radial_w, mix_w, square_w, cot_t, square_t, first_t, radial_t, recv = local(
         early_kernel,
         "early",
         [
@@ -351,7 +359,8 @@
             (square, f32),
             (square, bf16),
             (square, f32),
-            ((2, channels, degrees), f32),
+            ((2, degrees, channels, rows), f32),
+            ((3, rows, rows), f32),
         ],
         [pltpu.VMEM((slots, 4 * channels), bf16)],
         (steps, number, senders, own_row, near_row, cotangent, radial_w, mix_w, square_w),
@@ -375,7 +384,7 @@
         ],
         (
             table, far_sides, far_own, own_row, sums, cot, cot_t, square_w, square_t, first_t,
-            radial_w, radial_t,
+            radial_w, radial_t, recv,
         ),
     )
     far_in = swap_back(far_out, "gy", 1)

time: 29.5 us -> 29 us (0.983); the launches traced: 29.6 us -> 28.8 us
  starting transfers between devices: 12.9 us -> 15 us
  waiting for transfers between devices: 8.25 us -> 6.6 us
  Pallas kernels: 6.1 us -> 4.85 us
    ppermute x9, starting transfers between devices: 12.9 us -> 15 us  [swap(): return lax.ppermute(block, axis, pairs)]
    ppermute x9, waiting for transfers between devices: 8.25 us -> 6.6 us  [swap(): return lax.ppermute(block, axis, pairs)]
    pallas_call x4, Pallas kernels: 6.1 us -> 4.85 us  [local(): pl.pallas_call(kernel, out_shape=tuple((jax.ShapeDtypeStruct(*out) for ou...]
where the time goes in v6:
time: 29 us; the launch traced here: 28.8 us
  starting transfers between devices  15 us (52%)
  waiting for transfers between devices  6.6 us (23%)
  Pallas kernels  4.85 us (17%)
  between operations  1.38 us (5%)
  local copies, waits for them, and re-layouts  0.81 us (3%)
    ppermute x9, starting transfers between devices, swap(): return lax.ppermute(block, axis, pairs)  15 us
    ppermute x9, waiting for transfers between devices, swap(): return lax.ppermute(block, axis, pairs)  6.6 us
    pallas_call x4, Pallas kernels, local(): pl.pallas_call(kernel, out_shape=tuple((jax.ShapeDtypeStruct(*out) for ou...  4.85 us
    unnamed x1, local copies, waits for them, and re-layouts  0.73 us
  transfers between devices with their start and end apart: 9, of which 6 were waited for; matrix products, arithmetic and copies ran while one was open for 1% of the time, Pallas kernels for 12%

profile of v6, /device:TPU:0, one launch (start us, length us, event | category | flops | bytes accessed | tf_op | source)
XLA Modules:
  0.0 28.8 jit_solution(13707913502023584733)
XLA Ops:
  0.6 0.8 %pack.1 = (bf16[1,144,128]{2,1,0:T(8,128)(2,1)S(1)}, s32[1,1,1,8]{3,2,1,0:T(1,128)S(1)}) custom-call(bf16[1,1,128,128]{3,2,1,0:T(8,128)(2,1)} %feat_ref.1, bf16[1,1,3,128]{3,2,1,0:T(4,128)(2,1)} %pos_ref.1, s32[1,1,1,8]{3,2,1,0:T(1,128)} %senders_ref.1), custom_call_target="tpu_custom_call" | custom-call | tf_op jit(solution)/shard_map/pack/pallas_call | solution.py:314
  1.4 4.0 %collective-permute-start.1 = (bf16[1,144,128]{2,1,0:T(8,128)(2,1)S(1)}, bf16[1,144,128]{2,1,0:T(8,128)(2,1)S(1)}, u32[]{:S(2)}, u32[]{:S(2)}) collective-permute-start(bf16[1,144,128]{2,1,0:T(8,128)(2,1)S(1)} %get-tuple-element.24), channel_id=1, source_target_pairs={{8,16},{16,8},{24,0},{0,24},{9,17},{17,9},{25,1},{1,25},{10,18},{1... | collective-permute-start | bytes 110600 | tf_op jit(solution)/shard_map/ppermute | solution.py:33
  5.4 0.5 %collective-permute-start = (bf16[1,144,128]{2,1,0:T(8,128)(2,1)S(1)}, bf16[1,144,128]{2,1,0:T(8,128)(2,1)S(1)}, u32[]{:S(2)}, u32[]{:S(2)}) collective-permute-start(bf16[1,144,128]{2,1,0:T(8,128)(2,1)S(1)} %get-tuple-element.24), channel_id=1, source_target_pairs={{0,8},{8,0},{16,24},{24,16},{1,9},{9,1},{17,25},{25,17},{2,10},{10... | collective-permute-start | bytes 110600 | tf_op jit(solution)/shard_map/ppermute | solution.py:33
  5.9 2.5 %collective-permute-start.4 = (bf16[1,144,128]{2,1,0:T(8,128)(2,1)S(1)}, bf16[1,144,128]{2,1,0:T(8,128)(2,1)S(1)}, u32[]{:S(2)}, u32[]{:S(2)}) collective-permute-start(bf16[1,144,128]{2,1,0:T(8,128)(2,1)S(1)} %get-tuple-element.24), channel_id=1, source_target_pairs={{1,2},{2,1},{3,4},{4,3},{5,6},{6,5},{7,0},{0,7},{9,10},{10,9},{11,... | collective-permute-start | bytes 110600 | tf_op jit(solution)/shard_map/ppermute | solution.py:33
  8.4 0.0 collective-permute-done.1
  8.4 0.9 %collective-permute-done = bf16[1,144,128]{2,1,0:T(8,128)(2,1)S(1)} collective-permute-done((bf16[1,144,128]{2,1,0:T(8,128)(2,1)S(1)}, bf16[1,144,128]{2,1,0:T(8,128)(2,1)S(1)}, u32[]{:S(2)}, u32[]{:S(2)}) %collective-permute-start) | collective-permute-done | bytes 36896 | tf_op jit(solution)/shard_map/ppermute | solution.py:33
  9.4 2.2 %collective-permute-start.3 = (bf16[2,144,128]{2,1,0:T(8,128)(2,1)S(1)}, bf16[2,144,128]{2,1,0:T(8,128)(2,1)S(1)}, u32[]{:S(2)}, u32[]{:S(2)}) collective-permute-start(bf16[2,144,128]{2,1,0:T(8,128)(2,1)S(1)} %get-tuple-element.50), channel_id=1, source_target_pairs={{1,2},{2,1},{3,4},{4,3},{5,6},{6,5},{7,0},{0,7},{9,10},{10,9},{11,... | collective-permute-start | bytes 221192 | tf_op jit(solution)/shard_map/ppermute | solution.py:33
  11.5 0.1 collective-permute-start.2
  11.6 0.1 pad_add_fusion
  12.4 0.6 %collective-permute-done.2.near_row = bf16[3,144,128]{2,1,0:T(8,128)(2,1)S(1)} collective-permute-done((bf16[3,144,128]{2,1,0:T(8,128)(2,1)S(1)}, bf16[3,144,128]{2,1,0:T(8,128)(2,1)S(1)}, u32[]{:S(2)}, u32[]{:S(2)}) %collective-permute-start.2) | collective-permute-done | bytes 110624 | tf_op jit(solution)/shard_map/ppermute | solution.py:33
  12.9 0.1 broadcast_in_dim.19.steps
  13.0 1.9 %early.1 = (s32[24,128]{1,0:T(8,128)S(1)}, bf16[1024,768]{1,0:T(8,128)(2,1)S(1)}, f32[5,128,128]{2,1,0:T(8,128)S(1)}, bf16[128,128]{1,0:T(8,128)(2,1)S(1)}, f32[...) custom-call(s32[8,128]{1,0:T(8,128)S(1)} %broadcast_in_dim.19.steps,, ...), custom_call_target="tpu_custom_call" | custom-call | tf_op jit(solution)/shard_map/early/pallas_call | solution.py:314
  14.9 0.0 collective-permute-done.4.far_own
  14.9 0.6 %collective-permute-done.3.far_sides = bf16[2,144,128]{2,1,0:T(8,128)(2,1)S(1)} collective-permute-done((bf16[2,144,128]{2,1,0:T(8,128)(2,1)S(1)}, bf16[2,144,128]{2,1,0:T(8,128)(2,1)S(1)}, u32[]{:S(2)}, u32[]{:S(2)}) %collective-permute-start.3) | collective-permute-done | bytes 73760 | tf_op jit(solution)/shard_map/ppermute | solution.py:33
  15.5 0.5 %middle.1 = (bf16[3,128,128]{2,1,0:T(8,128)(2,1)S(1)}, bf16[512,1024]{1,0:T(8,128)(2,1)S(1)}, bf16[128,128]{1,0:T(8,128)(2,1)S(1)}, bf16[384,128]{1,0:T(8,128)(2,1)S(1)}) custom-call(s32[24,128]{1,0:T(8,128)S(1)} %get-tuple-element.25.table, bf16[2,144,128]{2,1,0:T(8,128)(2,1)S(1)} %collective-permute-done.3.far_sides, ...), custom_call_target="tpu_custom_call" | custom-call | tf_op jit(solution)/shard_map/middle/pallas_call | solution.py:314
  16.1 2.7 %collective-permute-start.6 = (bf16[3,128,128]{2,1,0:T(8,128)(2,1)S(1)}, bf16[3,128,128]{2,1,0:T(8,128)(2,1)S(1)}, u32[]{:S(2)}, u32[]{:S(2)}) collective-permute-start(bf16[3,128,128]{2,1,0:T(8,128)(2,1)S(1)} %get-tuple-element.43), channel_id=1, source_target_pairs={{1,2},{2,1},{3,4},{4,3},{5,6},{6,5},{7,0},{0,7},{9,10},{10,9},{11,... | collective-permute-start | bytes 294920 | tf_op jit(solution)/shard_map/ppermute | solution.py:33
  18.8 1.6 %late.1 = (bf16[3,128,128]{2,1,0:T(8,128)(2,1)S(1)}, f32[3,128,128]{2,1,0:T(8,128)S(1)}, bf16[128,128]{1,0:T(8,128)(2,1)}) custom-call(s32[24,128]{1,0:T(8,128)S(1)} %get-tuple-element.25.table, bf16[3,144,128]{2,1,0:T(8,128)(2,1)S(1)} %pad_maximum_fusion.own_row, bf16[3,144,128]{2,1,0:T(8,128)(2,1)S(1)} %collective-permute-done.2.near_row, ...), custom_call_target="tpu_custom_call" | custom-call | tf_op jit(solution)/shard_map/late/pallas_call | solution.py:314
  20.4 0.0 collective-permute-start.5
  20.4 2.1 %collective-permute-done.6 = bf16[3,128,128]{2,1,0:T(8,128)(2,1)S(1)} collective-permute-done((bf16[3,128,128]{2,1,0:T(8,128)(2,1)S(1)}, bf16[3,128,128]{2,1,0:T(8,128)(2,1)S(1)}, u32[]{:S(2)}, u32[]{:S(2)}) %collective-permute-start.6) | collective-permute-done | bytes 98336 | tf_op jit(solution)/shard_map/ppermute | solution.py:33
  22.5 0.0 collective-permute-done.5
  22.6 1.5 %collective-permute-start.7 = (bf16[128,128]{1,0:T(8,128)(2,1)S(1)}, bf16[128,128]{1,0:T(8,128)(2,1)S(1)}, u32[]{:S(2)}, u32[]{:S(2)}) collective-permute-start(bf16[128,128]{1,0:T(8,128)(2,1)S(1)} %get-tuple-element.49), channel_id=1, source_target_pairs={{8,16},{16,8},{24,0},{0,24},{9,17},{17,9},{25,1},{1,25},{10,18},{1... | collective-permute-start | bytes 98312 | tf_op jit(solution)/shard_map/ppermute | solution.py:33
  24.1 1.5 %collective-permute-start.8 = (bf16[128,128]{1,0:T(8,128)(2,1)S(1)}, bf16[128,128]{1,0:T(8,128)(2,1)S(1)}, u32[]{:S(2)}, u32[]{:S(2)}) collective-permute-start(bf16[128,128]{1,0:T(8,128)(2,1)S(1)} %get-tuple-element.48), channel_id=1, source_target_pairs={{0,8},{8,0},{16,24},{24,16},{1,9},{9,1},{17,25},{25,17},{2,10},{10... | collective-permute-start | bytes 98312 | tf_op jit(solution)/shard_map/ppermute | solution.py:33
  25.6 1.9 %collective-permute-done.7 = bf16[128,128]{1,0:T(8,128)(2,1)S(1)} collective-permute-done((bf16[128,128]{1,0:T(8,128)(2,1)S(1)}, bf16[128,128]{1,0:T(8,128)(2,1)S(1)}, u32[]{:S(2)}, u32[]{:S(2)}) %collective-permute-start.7) | collective-permute-done | bytes 32800 | tf_op jit(solution)/shard_map/ppermute | solution.py:33
  27.5 0.5 %collective-permute-done.8 = bf16[128,128]{1,0:T(8,128)(2,1)S(1)} collective-permute-done((bf16[128,128]{1,0:T(8,128)(2,1)S(1)}, bf16[128,128]{1,0:T(8,128)(2,1)S(1)}, u32[]{:S(2)}, u32[]{:S(2)}) %collective-permute-start.8) | collective-permute-done | bytes 32800 | tf_op jit(solution)/shard_map/ppermute | solution.py:33
  28.0 0.7 %copy.10 = f32[1,1,128,128]{3,2,1,0:T(8,128)} copy(f32[1,1,128,128]{2,3,1,0:T(8,128)S(1)} %add_bitcast_fusion) | data formatting | bytes 131072
  (9 shorter events, 0.1 us)
Async XLA Ops:
  1.4 7.0 %collective-permute-start.1 = (bf16[1,144,128]{2,1,0:T(8,128)(2,1)S(1)}, bf16[1,144,128]{2,1,0:T(8,128)(2,1)S(1)}, u32[]{:S(2)}, u32[]{:S(2)}) collective-permute-start(bf16[1,144,128]{2,1,0:T(8,128)(2,1)S(1)} %get-tuple-element.24), channel_id=1, source_target_pairs={{8,16},{16,8},{24,0},{0,24},{9,17},{17,9},{25,1},{1,25},{10,18},{1... | collective-permute-start | bytes 110600 | tf_op jit(solution)/shard_map/ppermute | solution.py:33
  5.4 4.0 %collective-permute-start = (bf16[1,144,128]{2,1,0:T(8,128)(2,1)S(1)}, bf16[1,144,128]{2,1,0:T(8,128)(2,1)S(1)}, u32[]{:S(2)}, u32[]{:S(2)}) collective-permute-start(bf16[1,144,128]{2,1,0:T(8,128)(2,1)S(1)} %get-tuple-element.24), channel_id=1, source_target_pairs={{0,8},{8,0},{16,24},{24,16},{1,9},{9,1},{17,25},{25,17},{2,10},{10... | collective-permute-start | bytes 110600 | tf_op jit(solution)/shard_map/ppermute | solution.py:33
  5.9 9.0 %collective-permute-start.4 = (bf16[1,144,128]{2,1,0:T(8,128)(2,1)S(1)}, bf16[1,144,128]{2,1,0:T(8,128)(2,1)S(1)}, u32[]{:S(2)}, u32[]{:S(2)}) collective-permute-start(bf16[1,144,128]{2,1,0:T(8,128)(2,1)S(1)} %get-tuple-element.24), channel_id=1, source_target_pairs={{1,2},{2,1},{3,4},{4,3},{5,6},{6,5},{7,0},{0,7},{9,10},{10,9},{11,... | collective-permute-start | bytes 110600 | tf_op jit(solution)/shard_map/ppermute | solution.py:33
  9.4 6.2 %collective-permute-start.3 = (bf16[2,144,128]{2,1,0:T(8,128)(2,1)S(1)}, bf16[2,144,128]{2,1,0:T(8,128)(2,1)S(1)}, u32[]{:S(2)}, u32[]{:S(2)}) collective-permute-start(bf16[2,144,128]{2,1,0:T(8,128)(2,1)S(1)} %get-tuple-element.50), channel_id=1, source_target_pairs={{1,2},{2,1},{3,4},{4,3},{5,6},{6,5},{7,0},{0,7},{9,10},{10,9},{11,... | collective-permute-start | bytes 221192 | tf_op jit(solution)/shard_map/ppermute | solution.py:33
  11.5 1.4 %collective-permute-start.2 = (bf16[3,144,128]{2,1,0:T(8,128)(2,1)S(1)}, bf16[3,144,128]{2,1,0:T(8,128)(2,1)S(1)}, u32[]{:S(2)}, u32[]{:S(2)}) collective-permute-start(bf16[3,144,128]{2,1,0:T(8,128)(2,1)S(1)} %pad_maximum_fusion.own_row), channel_id=1, source_target_pairs={{0,1},{1,0},{2,3},{3,2},{4,5},{5,4},{6,7},{7,6},{8,9},{9,8},{10,11... | collective-permute-start | bytes 331784 | tf_op jit(solution)/shard_map/ppermute | solution.py:33
  16.1 6.5 %collective-permute-start.6 = (bf16[3,128,128]{2,1,0:T(8,128)(2,1)S(1)}, bf16[3,128,128]{2,1,0:T(8,128)(2,1)S(1)}, u32[]{:S(2)}, u32[]{:S(2)}) collective-permute-start(bf16[3,128,128]{2,1,0:T(8,128)(2,1)S(1)} %get-tuple-element.43), channel_id=1, source_target_pairs={{1,2},{2,1},{3,4},{4,3},{5,6},{6,5},{7,0},{0,7},{9,10},{10,9},{11,... | collective-permute-start | bytes 294920 | tf_op jit(solution)/shard_map/ppermute | solution.py:33
  20.4 2.1 %collective-permute-start.5 = (bf16[3,128,128]{2,1,0:T(8,128)(2,1)S(1)}, bf16[3,128,128]{2,1,0:T(8,128)(2,1)S(1)}, u32[]{:S(2)}, u32[]{:S(2)}) collective-permute-start(bf16[3,128,128]{2,1,0:T(8,128)(2,1)S(1)} %get-tuple-element.42), channel_id=1, source_target_pairs={{0,1},{1,0},{2,3},{3,2},{4,5},{5,4},{6,7},{7,6},{8,9},{9,8},{10,11... | collective-permute-start | bytes 294920 | tf_op jit(solution)/shard_map/ppermute | solution.py:33
  22.6 4.9 %collective-permute-start.7 = (bf16[128,128]{1,0:T(8,128)(2,1)S(1)}, bf16[128,128]{1,0:T(8,128)(2,1)S(1)}, u32[]{:S(2)}, u32[]{:S(2)}) collective-permute-start(bf16[128,128]{1,0:T(8,128)(2,1)S(1)} %get-tuple-element.49), channel_id=1, source_target_pairs={{8,16},{16,8},{24,0},{0,24},{9,17},{17,9},{25,1},{1,25},{10,18},{1... | collective-permute-start | bytes 98312 | tf_op jit(solution)/shard_map/ppermute | solution.py:33
  24.1 3.9 %collective-permute-start.8 = (bf16[128,128]{1,0:T(8,128)(2,1)S(1)}, bf16[128,128]{1,0:T(8,128)(2,1)S(1)}, u32[]{:S(2)}, u32[]{:S(2)}) collective-permute-start(bf16[128,128]{1,0:T(8,128)(2,1)S(1)} %get-tuple-element.48), channel_id=1, source_target_pairs={{0,8},{8,0},{16,24},{24,16},{1,9},{9,1},{17,25},{25,17},{2,10},{10... | collective-permute-start | bytes 98312 | tf_op jit(solution)/shard_map/ppermute | solution.py:33

commit v7 on v6

--- a/solution.py
+++ b/solution.py
@@ -218,8 +218,8 @@
 def middle_kernel(
     table, far_sides, far_own, own_row, sums_ref, cot_ref, cot_t_ref, square_ref, square_t_ref, first_t_ref,
     radial_ref, radial_t_ref, recv_ref,
-    far_out, grads, first_ref, second_ref,
-    basis, stacked, totals, far_row,
+    sides_out, middle_out, grads, first_ref, second_ref,
+    basis, stacked, totals, far_row, far_out,
 ):
     rows, channels = cot_ref.shape
     degrees = radial_ref.shape[1]
@@ -227,15 +227,14 @@
     lines, recv = [pos[m : m + 1] for m in range(3)], [recv_ref[m] for m in range(3)]
     far_count = table[FAR_COUNT, 0]
     order = [table[FAR_ORDER, 0], table[FAR_ORDER + 1, 0]]
-    few, all_far = (far_count == 1) | (far_count == 2), far_count == 3
+    cases = ((1, order[:1]), (2, order), (3, [0, 1, 2]))
 
     def messages(columns):
         width = len(columns) * rows
         for at, column in enumerate(columns):
             source = far_row.at[column]
             place = ghost_place(table, source, 2, column)
-            weight = (far_count > at).astype(f32)
-            add_tile(source, place, recv, weight, basis, stacked, at, degrees)
+            add_tile(source, place, recv, 1.0, basis, stacked, at, degrees)
         parts = gather(basis.at[:, :width], stacked.at[:width], radial_ref, None)
         for at, part in enumerate(parts):
             totals[at] = sums_ref[at] + part
@@ -247,8 +246,8 @@
     far_row[0] = far_sides[0]
     far_row[1] = far_own[0]
     far_row[2] = far_sides[1]
-    pl.when(few)(lambda: messages(order))
-    pl.when(all_far)(lambda: messages([0, 1, 2]))
+    for live, columns in cases:
+        pl.when(far_count == live)(functools.partial(messages, columns))
     sum_zero, sum_one, moments = totals[0], totals[1], [totals[2 + m] for m in range(3)]
     first_ref[...] = sum_zero.astype(bf16)
     second = jnp.concatenate(
@@ -282,18 +281,22 @@
         spread(grads, basis.at[:, :width], places, outs)
 
     far_out[...] = jnp.zeros(far_out.shape, bf16)
-    pl.when(few)(lambda: adjoints(order))
-    pl.when(all_far)(lambda: adjoints([0, 1, 2]))
+    for live, columns in cases:
+        pl.when(far_count == live)(functools.partial(adjoints, columns))
+    sides_out[0] = far_out[0]
+    sides_out[1] = far_out[2]
+    middle_out[...] = far_out[1]
 
 
 def late_kernel(
     table, own_row, near_row, basis, grads, first_ref, second_ref, mix_ref, square_ref,
-    near_out, own_out, updated_ref,
+    near_out, near_middle, own_out, updated_ref,
 ):
     rows = first_ref.shape[0]
     sources = early_blocks(own_row, near_row)
     places = [ghost_place(table, source, *slot) for slot, source in zip(EARLY, sources)]
-    outs = [own_out.at[c] for c in range(3)] + [near_out.at[c] for c in range(3)]
+    outs = [own_out.at[0], own_out.at[2], own_out.at[1]]
+    outs += [near_out.at[0], near_middle, near_out.at[1]]
     spread(grads, basis, places, outs)
     second = second_ref[...]
     quadratic = jnp.dot(second, square_ref[...], preferred_element_type=f32)
@@ -367,11 +370,12 @@
         fetched=4,
     )
     slots = 3 * rows
-    far_out, grads, first_bf, second_bf = local(
+    far_out, far_middle, grads, first_bf, second_bf = local(
         middle_kernel,
         "middle",
         [
-            ((3, channels, rows), bf16),
+            ((2, channels, rows), bf16),
+            ((channels, rows), bf16),
             ((4 * channels, degrees * rows), bf16),
             (square, bf16),
             ((3 * rows, channels), bf16),
@@ -381,6 +385,7 @@
             pltpu.VMEM((slots, 4 * channels), bf16),
             pltpu.VMEM((5, rows, channels), f32),
             pltpu.VMEM(own_row.shape, bf16),
+            pltpu.VMEM((3, channels, rows), bf16),
         ],
         (
             table, far_sides, far_own, own_row, sums, cot, cot_t, square_w, square_t, first_t,
@@ -388,19 +393,25 @@
         ),
     )
     far_in = swap_back(far_out, "gy", 1)
-    near_out, own_out, updated = local(
+    near_out, near_middle, own_out, updated = local(
         late_kernel,
         "late",
-        [((3, channels, rows), bf16), ((3, channels, rows), f32), (square, bf16)],
+        [
+            ((2, channels, rows), bf16),
+            ((channels, rows), bf16),
+            ((3, channels, rows), f32),
+            (square, bf16),
+        ],
         [],
         (table, own_row, near_row, basis, grads, first_bf, second_bf, mix_w, square_w),
     )
     near_in = swap_back(near_out, "gy", 0)
+    middle_in = [swap_back(far_middle, "gy", 1), swap_back(near_middle, "gy", 0)]
     far_in = lax.optimization_barrier(far_in.astype(f32))
-    line = own_out + (near_in.astype(f32) + far_in)
-    sent = line.astype(bf16)
-    last_in, first_in = swap_back(sent[2], "gx", 1), swap_back(sent[0], "gx", 0)
-    partial = lax.optimization_barrier(line[1] + last_in.astype(f32))
+    sent = (own_out[:2] + (near_in.astype(f32) + far_in)).astype(bf16)
+    last_in, first_in = swap_back(sent[1], "gx", 1), swap_back(sent[0], "gx", 0)
+    middle = own_out[2] + (middle_in[0].astype(f32) + middle_in[1].astype(f32))
+    partial = lax.optimization_barrier(middle + last_in.astype(f32))
     collected = (partial + first_in.astype(f32)).T
     return (updated[None, None], collected[None, None])
 

time: 29 us -> 28.8 us (level)
  waiting for transfers between devices: 6.6 us -> 4.89 us
  Pallas kernels: 4.85 us -> 5.84 us
  starting transfers between devices: 15 us -> 15.5 us
    ppermute x9 -> x11, waiting for transfers between devices: 6.6 us -> 4.89 us  [swap(): return lax.ppermute(block, axis, pairs)]
    pallas_call x4, Pallas kernels: 4.85 us -> 5.84 us  [local(): pl.pallas_call(kernel, out_shape=tuple((jax.ShapeDtypeStruct(*out) for ou...]
    ppermute x9 -> x11, starting transfers between devices: 15 us -> 15.5 us  [swap(): return lax.ppermute(block, axis, pairs)]
  transfers between devices with their start and end apart: 9 -> 11, of which waited for: 6 -> 5; matrix products, arithmetic and copies ran while one was open for 1% -> 1% of each run, Pallas kernels for 12% -> 12%
where the time goes in v7:
time: 28.8 us; the launch traced here: 28.6 us
  starting transfers between devices  15.5 us (54%)
  Pallas kernels  5.84 us (20%)
  waiting for transfers between devices  4.89 us (17%)
  between operations  1.39 us (5%)
  local copies, waits for them, and re-layouts  0.81 us (3%)
    ppermute x11, starting transfers between devices, swap(): return lax.ppermute(block, axis, pairs)  15.5 us
    pallas_call x4, Pallas kernels, local(): pl.pallas_call(kernel, out_shape=tuple((jax.ShapeDtypeStruct(*out) for ou...  5.84 us
    ppermute x11, waiting for transfers between devices, swap(): return lax.ppermute(block, axis, pairs)  4.89 us
    unnamed x1, local copies, waits for them, and re-layouts  0.73 us
  transfers between devices with their start and end apart: 11, of which 5 were waited for; matrix products, arithmetic and copies ran while one was open for 1% of the time, Pallas kernels for 12%

profile of v7, /device:TPU:0, one launch (start us, length us, event | category | flops | bytes accessed | tf_op | source)
XLA Modules:
  0.0 28.6 jit_solution(1357757518064173205)
XLA Ops:
  0.6 0.8 %pack.1 = (bf16[1,144,128]{2,1,0:T(8,128)(2,1)S(1)}, s32[1,1,1,8]{3,2,1,0:T(1,128)S(1)}) custom-call(bf16[1,1,128,128]{3,2,1,0:T(8,128)(2,1)} %feat_ref.1, bf16[1,1,3,128]{3,2,1,0:T(4,128)(2,1)} %pos_ref.1, s32[1,1,1,8]{3,2,1,0:T(1,128)} %senders_ref.1), custom_call_target="tpu_custom_call" | custom-call | tf_op jit(solution)/shard_map/pack/pallas_call | solution.py:317
  1.4 4.0 %collective-permute-start.1 = (bf16[1,144,128]{2,1,0:T(8,128)(2,1)S(1)}, bf16[1,144,128]{2,1,0:T(8,128)(2,1)S(1)}, u32[]{:S(2)}, u32[]{:S(2)}) collective-permute-start(bf16[1,144,128]{2,1,0:T(8,128)(2,1)S(1)} %get-tuple-element.26), channel_id=1, source_target_pairs={{8,16},{16,8},{24,0},{0,24},{9,17},{17,9},{25,1},{1,25},{10,18},{1... | collective-permute-start | bytes 110600 | tf_op jit(solution)/shard_map/ppermute | solution.py:33
  5.4 0.5 %collective-permute-start = (bf16[1,144,128]{2,1,0:T(8,128)(2,1)S(1)}, bf16[1,144,128]{2,1,0:T(8,128)(2,1)S(1)}, u32[]{:S(2)}, u32[]{:S(2)}) collective-permute-start(bf16[1,144,128]{2,1,0:T(8,128)(2,1)S(1)} %get-tuple-element.26), channel_id=1, source_target_pairs={{0,8},{8,0},{16,24},{24,16},{1,9},{9,1},{17,25},{25,17},{2,10},{10... | collective-permute-start | bytes 110600 | tf_op jit(solution)/shard_map/ppermute | solution.py:33
  5.9 2.5 %collective-permute-start.4 = (bf16[1,144,128]{2,1,0:T(8,128)(2,1)S(1)}, bf16[1,144,128]{2,1,0:T(8,128)(2,1)S(1)}, u32[]{:S(2)}, u32[]{:S(2)}) collective-permute-start(bf16[1,144,128]{2,1,0:T(8,128)(2,1)S(1)} %get-tuple-element.26), channel_id=1, source_target_pairs={{1,2},{2,1},{3,4},{4,3},{5,6},{6,5},{7,0},{0,7},{9,10},{10,9},{11,... | collective-permute-start | bytes 110600 | tf_op jit(solution)/shard_map/ppermute | solution.py:33
  8.4 0.0 collective-permute-done.1
  8.4 0.9 %collective-permute-done = bf16[1,144,128]{2,1,0:T(8,128)(2,1)S(1)} collective-permute-done((bf16[1,144,128]{2,1,0:T(8,128)(2,1)S(1)}, bf16[1,144,128]{2,1,0:T(8,128)(2,1)S(1)}, u32[]{:S(2)}, u32[]{:S(2)}) %collective-permute-start) | collective-permute-done | bytes 36896 | tf_op jit(solution)/shard_map/ppermute | solution.py:33
  9.4 2.2 %collective-permute-start.3 = (bf16[2,144,128]{2,1,0:T(8,128)(2,1)S(1)}, bf16[2,144,128]{2,1,0:T(8,128)(2,1)S(1)}, u32[]{:S(2)}, u32[]{:S(2)}) collective-permute-start(bf16[2,144,128]{2,1,0:T(8,128)(2,1)S(1)} %get-tuple-element.52), channel_id=1, source_target_pairs={{1,2},{2,1},{3,4},{4,3},{5,6},{6,5},{7,0},{0,7},{9,10},{10,9},{11,... | collective-permute-start | bytes 221192 | tf_op jit(solution)/shard_map/ppermute | solution.py:33
  11.5 0.1 collective-permute-start.2
  11.6 0.1 pad_add_fusion
  12.4 0.6 %collective-permute-done.2.near_row = bf16[3,144,128]{2,1,0:T(8,128)(2,1)S(1)} collective-permute-done((bf16[3,144,128]{2,1,0:T(8,128)(2,1)S(1)}, bf16[3,144,128]{2,1,0:T(8,128)(2,1)S(1)}, u32[]{:S(2)}, u32[]{:S(2)}) %collective-permute-start.2) | collective-permute-done | bytes 110624 | tf_op jit(solution)/shard_map/ppermute | solution.py:33
  12.9 0.1 broadcast_in_dim.19.steps
  13.0 1.9 %early.1 = (s32[24,128]{1,0:T(8,128)S(1)}, bf16[1024,768]{1,0:T(8,128)(2,1)S(1)}, f32[5,128,128]{2,1,0:T(8,128)S(1)}, bf16[128,128]{1,0:T(8,128)(2,1)S(1)}, f32[...) custom-call(s32[8,128]{1,0:T(8,128)S(1)} %broadcast_in_dim.19.steps,, ...), custom_call_target="tpu_custom_call" | custom-call | tf_op jit(solution)/shard_map/early/pallas_call | solution.py:317
  14.9 0.0 collective-permute-done.4.far_own
  14.9 0.6 %collective-permute-done.3.far_sides = bf16[2,144,128]{2,1,0:T(8,128)(2,1)S(1)} collective-permute-done((bf16[2,144,128]{2,1,0:T(8,128)(2,1)S(1)}, bf16[2,144,128]{2,1,0:T(8,128)(2,1)S(1)}, u32[]{:S(2)}, u32[]{:S(2)}) %collective-permute-start.3) | collective-permute-done | bytes 73760 | tf_op jit(solution)/shard_map/ppermute | solution.py:33
  15.5 1.5 %middle.1 = (bf16[2,128,128]{2,1,0:T(8,128)(2,1)S(1)}, bf16[128,128]{1,0:T(8,128)(2,1)S(1)}, bf16[512,1024]{1,0:T(8,128)(2,1)S(1)}, bf16[128,128]{1,0:T(8,128)(2,1)S(1)}, bf16[384,128]{1,0:T(8,128)(2,1)S(1)}) custom-call(s32[24,128]{1,0:T(8,128)S(1)} %get-tuple-element.27.table, bf16[2,144,128]{2,1,0:T(8,128)(2,1)S(1)} %collective-permute-done.3.far_sides, ...), custom_call_target="tpu_custom_call" | custom-call | tf_op jit(solution)/shard_map/middle/pallas_call | solution.py:317
  17.0 1.6 %collective-permute-start.8 = (bf16[2,128,128]{2,1,0:T(8,128)(2,1)S(1)}, bf16[2,128,128]{2,1,0:T(8,128)(2,1)S(1)}, u32[]{:S(2)}, u32[]{:S(2)}) collective-permute-start(bf16[2,128,128]{2,1,0:T(8,128)(2,1)S(1)} %get-tuple-element.47), channel_id=1, source_target_pairs={{1,2},{2,1},{3,4},{4,3},{5,6},{6,5},{7,0},{0,7},{9,10},{10,9},{11,... | collective-permute-start | bytes 196616 | tf_op jit(solution)/shard_map/ppermute | solution.py:33
  18.7 1.6 %late.1 = (bf16[2,128,128]{2,1,0:T(8,128)(2,1)S(1)}, bf16[128,128]{1,0:T(8,128)(2,1)S(1)}, f32[3,128,128]{2,1,0:T(8,128)S(1)}, bf16[128,128]{1,0:T(8,128)(2,1)}) custom-call(s32[24,128]{1,0:T(8,128)S(1)} %get-tuple-element.27.table, bf16[3,144,128]{2,1,0:T(8,128)(2,1)S(1)} %pad_maximum_fusion.own_row, ...), custom_call_target="tpu_custom_call" | custom-call | tf_op jit(solution)/shard_map/late/pallas_call | solution.py:317
  20.3 0.0 collective-permute-start.7
  20.3 0.5 %collective-permute-start.6 = (bf16[128,128]{1,0:T(8,128)(2,1)S(1)}, bf16[128,128]{1,0:T(8,128)(2,1)S(1)}, u32[]{:S(2)}, u32[]{:S(2)}) collective-permute-start(bf16[128,128]{1,0:T(8,128)(2,1)S(1)} %get-tuple-element.45), channel_id=1, source_target_pairs={{0,1},{1,0},{2,3},{3,2},{4,5},{5,4},{6,7},{7,6},{8,9},{9,8},{10,11... | collective-permute-start | bytes 98312 | tf_op jit(solution)/shard_map/ppermute | solution.py:33
  20.8 2.0 %collective-permute-start.5 = (bf16[128,128]{1,0:T(8,128)(2,1)S(1)}, bf16[128,128]{1,0:T(8,128)(2,1)S(1)}, u32[]{:S(2)}, u32[]{:S(2)}) collective-permute-start(bf16[128,128]{1,0:T(8,128)(2,1)S(1)} %get-tuple-element.44), channel_id=1, source_target_pairs={{1,2},{2,1},{3,4},{4,3},{5,6},{6,5},{7,0},{0,7},{9,10},{10,9},{11,... | collective-permute-start | bytes 98312 | tf_op jit(solution)/shard_map/ppermute | solution.py:33
  22.8 0.0 collective-permute-done.8
  22.8 0.0 collective-permute-done.7
  22.9 1.0 %collective-permute-start.9 = (bf16[128,128]{1,0:T(8,128)(2,1)S(1)}, bf16[128,128]{1,0:T(8,128)(2,1)S(1)}, u32[]{:S(2)}, u32[]{:S(2)}) collective-permute-start(bf16[128,128]{1,0:T(8,128)(2,1)S(1)} %get-tuple-element.51), channel_id=1, source_target_pairs={{8,16},{16,8},{24,0},{0,24},{9,17},{17,9},{25,1},{1,25},{10,18},{1... | collective-permute-start | bytes 98312 | tf_op jit(solution)/shard_map/ppermute | solution.py:33
  23.9 1.2 %collective-permute-start.10 = (bf16[128,128]{1,0:T(8,128)(2,1)S(1)}, bf16[128,128]{1,0:T(8,128)(2,1)S(1)}, u32[]{:S(2)}, u32[]{:S(2)}) collective-permute-start(bf16[128,128]{1,0:T(8,128)(2,1)S(1)} %get-tuple-element.50), channel_id=1, source_target_pairs={{0,8},{8,0},{16,24},{24,16},{1,9},{9,1},{17,25},{25,17},{2,10},{10... | collective-permute-start | bytes 98312 | tf_op jit(solution)/shard_map/ppermute | solution.py:33
  25.0 0.0 collective-permute-done.6
  25.0 1.0 %collective-permute-done.5 = bf16[128,128]{1,0:T(8,128)(2,1)S(1)} collective-permute-done((bf16[128,128]{1,0:T(8,128)(2,1)S(1)}, bf16[128,128]{1,0:T(8,128)(2,1)S(1)}, u32[]{:S(2)}, u32[]{:S(2)}) %collective-permute-start.5) | collective-permute-done | bytes 32800 | tf_op jit(solution)/shard_map/ppermute | solution.py:33
  26.0 1.8 %collective-permute-done.9 = bf16[128,128]{1,0:T(8,128)(2,1)S(1)} collective-permute-done((bf16[128,128]{1,0:T(8,128)(2,1)S(1)}, bf16[128,128]{1,0:T(8,128)(2,1)S(1)}, u32[]{:S(2)}, u32[]{:S(2)}) %collective-permute-start.9) | collective-permute-done | bytes 32800 | tf_op jit(solution)/shard_map/ppermute | solution.py:33
  27.8 0.0 collective-permute-done.10
  27.8 0.7 %copy.10 = f32[1,1,128,128]{3,2,1,0:T(8,128)} copy(f32[1,1,128,128]{2,3,1,0:T(8,128)S(1)} %add_bitcast_fusion) | data formatting | bytes 131072
  (9 shorter events, 0.1 us)
Async XLA Ops:
  1.4 7.0 %collective-permute-start.1 = (bf16[1,144,128]{2,1,0:T(8,128)(2,1)S(1)}, bf16[1,144,128]{2,1,0:T(8,128)(2,1)S(1)}, u32[]{:S(2)}, u32[]{:S(2)}) collective-permute-start(bf16[1,144,128]{2,1,0:T(8,128)(2,1)S(1)} %get-tuple-element.26), channel_id=1, source_target_pairs={{8,16},{16,8},{24,0},{0,24},{9,17},{17,9},{25,1},{1,25},{10,18},{1... | collective-permute-start | bytes 110600 | tf_op jit(solution)/shard_map/ppermute | solution.py:33
  5.4 4.0 %collective-permute-start = (bf16[1,144,128]{2,1,0:T(8,128)(2,1)S(1)}, bf16[1,144,128]{2,1,0:T(8,128)(2,1)S(1)}, u32[]{:S(2)}, u32[]{:S(2)}) collective-permute-start(bf16[1,144,128]{2,1,0:T(8,128)(2,1)S(1)} %get-tuple-element.26), channel_id=1, source_target_pairs={{0,8},{8,0},{16,24},{24,16},{1,9},{9,1},{17,25},{25,17},{2,10},{10... | collective-permute-start | bytes 110600 | tf_op jit(solution)/shard_map/ppermute | solution.py:33
  5.9 9.0 %collective-permute-start.4 = (bf16[1,144,128]{2,1,0:T(8,128)(2,1)S(1)}, bf16[1,144,128]{2,1,0:T(8,128)(2,1)S(1)}, u32[]{:S(2)}, u32[]{:S(2)}) collective-permute-start(bf16[1,144,128]{2,1,0:T(8,128)(2,1)S(1)} %get-tuple-element.26), channel_id=1, source_target_pairs={{1,2},{2,1},{3,4},{4,3},{5,6},{6,5},{7,0},{0,7},{9,10},{10,9},{11,... | collective-permute-start | bytes 110600 | tf_op jit(solution)/shard_map/ppermute | solution.py:33
  9.4 6.2 %collective-permute-start.3 = (bf16[2,144,128]{2,1,0:T(8,128)(2,1)S(1)}, bf16[2,144,128]{2,1,0:T(8,128)(2,1)S(1)}, u32[]{:S(2)}, u32[]{:S(2)}) collective-permute-start(bf16[2,144,128]{2,1,0:T(8,128)(2,1)S(1)} %get-tuple-element.52), channel_id=1, source_target_pairs={{1,2},{2,1},{3,4},{4,3},{5,6},{6,5},{7,0},{0,7},{9,10},{10,9},{11,... | collective-permute-start | bytes 221192 | tf_op jit(solution)/shard_map/ppermute | solution.py:33
  11.5 1.4 %collective-permute-start.2 = (bf16[3,144,128]{2,1,0:T(8,128)(2,1)S(1)}, bf16[3,144,128]{2,1,0:T(8,128)(2,1)S(1)}, u32[]{:S(2)}, u32[]{:S(2)}) collective-permute-start(bf16[3,144,128]{2,1,0:T(8,128)(2,1)S(1)} %pad_maximum_fusion.own_row), channel_id=1, source_target_pairs={{0,1},{1,0},{2,3},{3,2},{4,5},{5,4},{6,7},{7,6},{8,9},{9,8},{10,11... | collective-permute-start | bytes 331784 | tf_op jit(solution)/shard_map/ppermute | solution.py:33
  17.0 5.8 %collective-permute-start.8 = (bf16[2,128,128]{2,1,0:T(8,128)(2,1)S(1)}, bf16[2,128,128]{2,1,0:T(8,128)(2,1)S(1)}, u32[]{:S(2)}, u32[]{:S(2)}) collective-permute-start(bf16[2,128,128]{2,1,0:T(8,128)(2,1)S(1)} %get-tuple-element.47), channel_id=1, source_target_pairs={{1,2},{2,1},{3,4},{4,3},{5,6},{6,5},{7,0},{0,7},{9,10},{10,9},{11,... | collective-permute-start | bytes 196616 | tf_op jit(solution)/shard_map/ppermute | solution.py:33
  20.3 2.5 %collective-permute-start.7 = (bf16[2,128,128]{2,1,0:T(8,128)(2,1)S(1)}, bf16[2,128,128]{2,1,0:T(8,128)(2,1)S(1)}, u32[]{:S(2)}, u32[]{:S(2)}) collective-permute-start(bf16[2,128,128]{2,1,0:T(8,128)(2,1)S(1)} %get-tuple-element.46), channel_id=1, source_target_pairs={{0,1},{1,0},{2,3},{3,2},{4,5},{5,4},{6,7},{7,6},{8,9},{9,8},{10,11... | collective-permute-start | bytes 196616 | tf_op jit(solution)/shard_map/ppermute | solution.py:33
  20.3 4.7 %collective-permute-start.6 = (bf16[128,128]{1,0:T(8,128)(2,1)S(1)}, bf16[128,128]{1,0:T(8,128)(2,1)S(1)}, u32[]{:S(2)}, u32[]{:S(2)}) collective-permute-start(bf16[128,128]{1,0:T(8,128)(2,1)S(1)} %get-tuple-element.45), channel_id=1, source_target_pairs={{0,1},{1,0},{2,3},{3,2},{4,5},{5,4},{6,7},{7,6},{8,9},{9,8},{10,11... | collective-permute-start | bytes 98312 | tf_op jit(solution)/shard_map/ppermute | solution.py:33
  20.8 5.1 %collective-permute-start.5 = (bf16[128,128]{1,0:T(8,128)(2,1)S(1)}, bf16[128,128]{1,0:T(8,128)(2,1)S(1)}, u32[]{:S(2)}, u32[]{:S(2)}) collective-permute-start(bf16[128,128]{1,0:T(8,128)(2,1)S(1)} %get-tuple-element.44), channel_id=1, source_target_pairs={{1,2},{2,1},{3,4},{4,3},{5,6},{6,5},{7,0},{0,7},{9,10},{10,9},{11,... | collective-permute-start | bytes 98312 | tf_op jit(solution)/shard_map/ppermute | solution.py:33
  22.9 4.9 %collective-permute-start.9 = (bf16[128,128]{1,0:T(8,128)(2,1)S(1)}, bf16[128,128]{1,0:T(8,128)(2,1)S(1)}, u32[]{:S(2)}, u32[]{:S(2)}) collective-permute-start(bf16[128,128]{1,0:T(8,128)(2,1)S(1)} %get-tuple-element.51), channel_id=1, source_target_pairs={{8,16},{16,8},{24,0},{0,24},{9,17},{17,9},{25,1},{1,25},{10,18},{1... | collective-permute-start | bytes 98312 | tf_op jit(solution)/shard_map/ppermute | solution.py:33
  23.9 3.9 %collective-permute-start.10 = (bf16[128,128]{1,0:T(8,128)(2,1)S(1)}, bf16[128,128]{1,0:T(8,128)(2,1)S(1)}, u32[]{:S(2)}, u32[]{:S(2)}) collective-permute-start(bf16[128,128]{1,0:T(8,128)(2,1)S(1)} %get-tuple-element.50), channel_id=1, source_target_pairs={{0,8},{8,0},{16,24},{24,16},{1,9},{9,1},{17,25},{25,17},{2,10},{10... | collective-permute-start | bytes 98312 | tf_op jit(solution)/shard_map/ppermute | solution.py:33

commit v8 on v7

--- a/solution.py
+++ b/solution.py
@@ -291,23 +291,40 @@
 def late_kernel(
     table, own_row, near_row, basis, grads, first_ref, second_ref, mix_ref, square_ref,
     near_out, near_middle, own_out, updated_ref,
+    updated, sems,
 ):
     rows = first_ref.shape[0]
+    second = second_ref[...]
+    quadratic = jnp.dot(second, square_ref[...], preferred_element_type=f32)
+    linear = jnp.dot(first_ref[...], mix_ref[...], preferred_element_type=f32)
+    product = quadratic * second.astype(f32)
+    updated[...] = (
+        linear + (product[:rows] + product[rows : 2 * rows] + product[2 * rows :])
+    ).astype(bf16)
+    (copy,) = start_copies([(updated, updated_ref)], sems)
     sources = early_blocks(own_row, near_row)
     places = [ghost_place(table, source, *slot) for slot, source in zip(EARLY, sources)]
     outs = [own_out.at[0], own_out.at[2], own_out.at[1]]
     outs += [near_out.at[0], near_middle, near_out.at[1]]
-    spread(grads, basis, places, outs)
-    second = second_ref[...]
-    quadratic = jnp.dot(second, square_ref[...], preferred_element_type=f32)
-    linear = jnp.dot(first_ref[...], mix_ref[...], preferred_element_type=f32)
-    product = quadratic * second.astype(f32)
-    updated_ref[...] = (
-        linear + (product[:rows] + product[rows : 2 * rows] + product[2 * rows :])
-    ).astype(bf16)
-
-
-def local(kernel, name, outs, scratch, args, fetched=0):
+    width = 2 * rows
+    for pair in range(0, len(EARLY), 2):
+        part = slice(pair, pair + 2)
+        live = sum(table[LIVE + 3 * line + column, 0] for line, column in EARLY[part])
+        span = basis.at[:, pair * rows : pair * rows + width]
+
+        @pl.when(live > 0)
+        def _(span=span, part=part):
+            spread(grads, span, places[part], outs[part])
+
+        @pl.when(live == 0)
+        def _(part=part):
+            for out in outs[part]:
+                out[...] = jnp.zeros(out.shape, out.dtype)
+
+    copy.wait()
+
+
+def local(kernel, name, outs, scratch, args, fetched=0, sent=0):
     in_vmem = pl.BlockSpec(memory_space=pltpu.VMEM)
     in_hbm = pl.BlockSpec(memory_space=pltpu.HBM)
     near = len(args) - fetched
@@ -318,8 +335,9 @@
         kernel,
         out_shape=tuple(jax.ShapeDtypeStruct(*out) for out in outs),
         in_specs=[in_vmem] * near + [in_hbm] * fetched,
-        out_specs=(in_vmem,) * len(outs),
-        scratch_shapes=scratch + ([pltpu.SemaphoreType.DMA((fetched,))] if fetched else []),
+        out_specs=(in_vmem,) * (len(outs) - sent) + (in_hbm,) * sent,
+        scratch_shapes=scratch
+        + ([pltpu.SemaphoreType.DMA((fetched + sent,))] if fetched + sent else []),
         compiler_params=pltpu.CompilerParams(vmem_limit_bytes=32 * 2**20),
         name=name,
     )(*args)
@@ -402,8 +420,9 @@
             ((3, channels, rows), f32),
             (square, bf16),
         ],
-        [],
+        [pltpu.VMEM(square, bf16)],
         (table, own_row, near_row, basis, grads, first_bf, second_bf, mix_w, square_w),
+        sent=1,
     )
     near_in = swap_back(near_out, "gy", 0)
     middle_in = [swap_back(far_middle, "gy", 1), swap_back(near_middle, "gy", 0)]

time: 28.8 us -> 28.6 us (level)
  Pallas kernels: 5.84 us -> 5 us
  waiting for transfers between devices: 4.89 us -> 5.45 us
    pallas_call x4, Pallas kernels: 5.84 us -> 5 us  [local(): pl.pallas_call(kernel, out_shape=tuple((jax.ShapeDtypeStruct(*out) for ou...]
    ppermute x11, waiting for transfers between devices: 4.89 us -> 5.45 us  [swap(): return lax.ppermute(block, axis, pairs)]
  transfers between devices with their start and end apart: 11 -> 11, of which waited for: 5 -> 6; matrix products, arithmetic and copies ran while one was open for 1% -> 1% of each run, Pallas kernels for 12% -> 10%
where the time goes in v8:
time: 28.6 us; the launch traced here: 28.4 us
  starting transfers between devices  15.6 us (55%)
  waiting for transfers between devices  5.45 us (19%)
  Pallas kernels  5 us (17%)
  between operations  1.39 us (5%)
  local copies, waits for them, and re-layouts  0.81 us (3%)
    ppermute x11, starting transfers between devices, swap(): return lax.ppermute(block, axis, pairs)  15.6 us
    ppermute x11, waiting for transfers between devices, swap(): return lax.ppermute(block, axis, pairs)  5.45 us
    pallas_call x4, Pallas kernels, local(): pl.pallas_call(kernel, out_shape=tuple((jax.ShapeDtypeStruct(*out) for ou...  5 us
    unnamed x1, local copies, waits for them, and re-layouts  0.73 us
  transfers between devices with their start and end apart: 11, of which 6 were waited for; matrix products, arithmetic and copies ran while one was open for 1% of the time, Pallas kernels for 10%

profile of v8, /device:TPU:0, one launch (start us, length us, event | category | flops | bytes accessed | tf_op | source)
XLA Modules:
  0.0 28.4 jit_solution(14986401532326401268)
XLA Ops:
  0.6 0.8 %pack.1 = (bf16[1,144,128]{2,1,0:T(8,128)(2,1)S(1)}, s32[1,1,1,8]{3,2,1,0:T(1,128)S(1)}) custom-call(bf16[1,1,128,128]{3,2,1,0:T(8,128)(2,1)} %feat_ref.1, bf16[1,1,3,128]{3,2,1,0:T(4,128)(2,1)} %pos_ref.1, s32[1,1,1,8]{3,2,1,0:T(1,128)} %senders_ref.1), custom_call_target="tpu_custom_call" | custom-call | tf_op jit(solution)/shard_map/pack/pallas_call | solution.py:334
  1.4 4.0 %collective-permute-start.1 = (bf16[1,144,128]{2,1,0:T(8,128)(2,1)S(1)}, bf16[1,144,128]{2,1,0:T(8,128)(2,1)S(1)}, u32[]{:S(2)}, u32[]{:S(2)}) collective-permute-start(bf16[1,144,128]{2,1,0:T(8,128)(2,1)S(1)} %get-tuple-element.26), channel_id=1, source_target_pairs={{8,16},{16,8},{24,0},{0,24},{9,17},{17,9},{25,1},{1,25},{10,18},{1... | collective-permute-start | bytes 110600 | tf_op jit(solution)/shard_map/ppermute | solution.py:33
  5.4 0.5 %collective-permute-start = (bf16[1,144,128]{2,1,0:T(8,128)(2,1)S(1)}, bf16[1,144,128]{2,1,0:T(8,128)(2,1)S(1)}, u32[]{:S(2)}, u32[]{:S(2)}) collective-permute-start(bf16[1,144,128]{2,1,0:T(8,128)(2,1)S(1)} %get-tuple-element.26), channel_id=1, source_target_pairs={{0,8},{8,0},{16,24},{24,16},{1,9},{9,1},{17,25},{25,17},{2,10},{10... | collective-permute-start | bytes 110600 | tf_op jit(solution)/shard_map/ppermute | solution.py:33
  5.9 2.5 %collective-permute-start.4 = (bf16[1,144,128]{2,1,0:T(8,128)(2,1)S(1)}, bf16[1,144,128]{2,1,0:T(8,128)(2,1)S(1)}, u32[]{:S(2)}, u32[]{:S(2)}) collective-permute-start(bf16[1,144,128]{2,1,0:T(8,128)(2,1)S(1)} %get-tuple-element.26), channel_id=1, source_target_pairs={{1,2},{2,1},{3,4},{4,3},{5,6},{6,5},{7,0},{0,7},{9,10},{10,9},{11,... | collective-permute-start | bytes 110600 | tf_op jit(solution)/shard_map/ppermute | solution.py:33
  8.4 0.0 collective-permute-done.1
  8.4 0.9 %collective-permute-done = bf16[1,144,128]{2,1,0:T(8,128)(2,1)S(1)} collective-permute-done((bf16[1,144,128]{2,1,0:T(8,128)(2,1)S(1)}, bf16[1,144,128]{2,1,0:T(8,128)(2,1)S(1)}, u32[]{:S(2)}, u32[]{:S(2)}) %collective-permute-start) | collective-permute-done | bytes 36896 | tf_op jit(solution)/shard_map/ppermute | solution.py:33
  9.4 2.2 %collective-permute-start.3 = (bf16[2,144,128]{2,1,0:T(8,128)(2,1)S(1)}, bf16[2,144,128]{2,1,0:T(8,128)(2,1)S(1)}, u32[]{:S(2)}, u32[]{:S(2)}) collective-permute-start(bf16[2,144,128]{2,1,0:T(8,128)(2,1)S(1)} %get-tuple-element.52), channel_id=1, source_target_pairs={{1,2},{2,1},{3,4},{4,3},{5,6},{6,5},{7,0},{0,7},{9,10},{10,9},{11,... | collective-permute-start | bytes 221192 | tf_op jit(solution)/shard_map/ppermute | solution.py:33
  11.5 0.1 collective-permute-start.2
  11.6 0.1 pad_add_fusion
  12.4 0.6 %collective-permute-done.2.near_row = bf16[3,144,128]{2,1,0:T(8,128)(2,1)S(1)} collective-permute-done((bf16[3,144,128]{2,1,0:T(8,128)(2,1)S(1)}, bf16[3,144,128]{2,1,0:T(8,128)(2,1)S(1)}, u32[]{:S(2)}, u32[]{:S(2)}) %collective-permute-start.2) | collective-permute-done | bytes 110624 | tf_op jit(solution)/shard_map/ppermute | solution.py:33
  12.9 0.1 broadcast_in_dim.19.steps
  13.0 1.9 %early.1 = (s32[24,128]{1,0:T(8,128)S(1)}, bf16[1024,768]{1,0:T(8,128)(2,1)S(1)}, f32[5,128,128]{2,1,0:T(8,128)S(1)}, bf16[128,128]{1,0:T(8,128)(2,1)S(1)}, f32[...) custom-call(s32[8,128]{1,0:T(8,128)S(1)} %broadcast_in_dim.19.steps,, ...), custom_call_target="tpu_custom_call" | custom-call | tf_op jit(solution)/shard_map/early/pallas_call | solution.py:334
  14.9 0.0 collective-permute-done.4.far_own
  14.9 0.6 %collective-permute-done.3.far_sides = bf16[2,144,128]{2,1,0:T(8,128)(2,1)S(1)} collective-permute-done((bf16[2,144,128]{2,1,0:T(8,128)(2,1)S(1)}, bf16[2,144,128]{2,1,0:T(8,128)(2,1)S(1)}, u32[]{:S(2)}, u32[]{:S(2)}) %collective-permute-start.3) | collective-permute-done | bytes 73760 | tf_op jit(solution)/shard_map/ppermute | solution.py:33
  15.5 1.5 %middle.1 = (bf16[2,128,128]{2,1,0:T(8,128)(2,1)S(1)}, bf16[128,128]{1,0:T(8,128)(2,1)S(1)}, bf16[512,1024]{1,0:T(8,128)(2,1)S(1)}, bf16[128,128]{1,0:T(8,128)(2,1)S(1)}, bf16[384,128]{1,0:T(8,128)(2,1)S(1)}) custom-call(s32[24,128]{1,0:T(8,128)S(1)} %get-tuple-element.27.table, bf16[2,144,128]{2,1,0:T(8,128)(2,1)S(1)} %collective-permute-done.3.far_sides, ...), custom_call_target="tpu_custom_call" | custom-call | tf_op jit(solution)/shard_map/middle/pallas_call | solution.py:334
  17.0 0.7 %collective-permute-start.8 = (bf16[2,128,128]{2,1,0:T(8,128)(2,1)S(1)}, bf16[2,128,128]{2,1,0:T(8,128)(2,1)S(1)}, u32[]{:S(2)}, u32[]{:S(2)}) collective-permute-start(bf16[2,128,128]{2,1,0:T(8,128)(2,1)S(1)} %get-tuple-element.47), channel_id=1, source_target_pairs={{1,2},{2,1},{3,4},{4,3},{5,6},{6,5},{7,0},{0,7},{9,10},{10,9},{11,... | collective-permute-start | bytes 196616 | tf_op jit(solution)/shard_map/ppermute | solution.py:33
  17.7 0.8 %late.1 = (bf16[2,128,128]{2,1,0:T(8,128)(2,1)S(1)}, bf16[128,128]{1,0:T(8,128)(2,1)S(1)}, f32[3,128,128]{2,1,0:T(8,128)S(1)}, bf16[128,128]{1,0:T(8,128)(2,1)}) custom-call(s32[24,128]{1,0:T(8,128)S(1)} %get-tuple-element.27.table, bf16[3,144,128]{2,1,0:T(8,128)(2,1)S(1)} %pad_maximum_fusion.own_row, ...), custom_call_target="tpu_custom_call" | custom-call | tf_op jit(solution)/shard_map/late/pallas_call | solution.py:334
  18.5 0.1 collective-permute-start.7
  18.6 0.5 %collective-permute-start.6 = (bf16[128,128]{1,0:T(8,128)(2,1)S(1)}, bf16[128,128]{1,0:T(8,128)(2,1)S(1)}, u32[]{:S(2)}, u32[]{:S(2)}) collective-permute-start(bf16[128,128]{1,0:T(8,128)(2,1)S(1)} %get-tuple-element.45), channel_id=1, source_target_pairs={{0,1},{1,0},{2,3},{3,2},{4,5},{5,4},{6,7},{7,6},{8,9},{9,8},{10,11... | collective-permute-start | bytes 98312 | tf_op jit(solution)/shard_map/ppermute | solution.py:33
  19.1 2.9 %collective-permute-start.5 = (bf16[128,128]{1,0:T(8,128)(2,1)S(1)}, bf16[128,128]{1,0:T(8,128)(2,1)S(1)}, u32[]{:S(2)}, u32[]{:S(2)}) collective-permute-start(bf16[128,128]{1,0:T(8,128)(2,1)S(1)} %get-tuple-element.44), channel_id=1, source_target_pairs={{1,2},{2,1},{3,4},{4,3},{5,6},{6,5},{7,0},{0,7},{9,10},{10,9},{11,... | collective-permute-start | bytes 98312 | tf_op jit(solution)/shard_map/ppermute | solution.py:33
  22.0 0.6 %collective-permute-done.8 = bf16[2,128,128]{2,1,0:T(8,128)(2,1)S(1)} collective-permute-done((bf16[2,128,128]{2,1,0:T(8,128)(2,1)S(1)}, bf16[2,128,128]{2,1,0:T(8,128)(2,1)S(1)}, u32[]{:S(2)}, u32[]{:S(2)}) %collective-permute-start.8) | collective-permute-done | bytes 65568 | tf_op jit(solution)/shard_map/ppermute | solution.py:33
  22.6 0.0 collective-permute-done.7
  22.7 1.1 %collective-permute-start.9 = (bf16[128,128]{1,0:T(8,128)(2,1)S(1)}, bf16[128,128]{1,0:T(8,128)(2,1)S(1)}, u32[]{:S(2)}, u32[]{:S(2)}) collective-permute-start(bf16[128,128]{1,0:T(8,128)(2,1)S(1)} %get-tuple-element.51), channel_id=1, source_target_pairs={{8,16},{16,8},{24,0},{0,24},{9,17},{17,9},{25,1},{1,25},{10,18},{1... | collective-permute-start | bytes 98312 | tf_op jit(solution)/shard_map/ppermute | solution.py:33
  23.7 1.2 %collective-permute-start.10 = (bf16[128,128]{1,0:T(8,128)(2,1)S(1)}, bf16[128,128]{1,0:T(8,128)(2,1)S(1)}, u32[]{:S(2)}, u32[]{:S(2)}) collective-permute-start(bf16[128,128]{1,0:T(8,128)(2,1)S(1)} %get-tuple-element.50), channel_id=1, source_target_pairs={{0,8},{8,0},{16,24},{24,16},{1,9},{9,1},{17,25},{25,17},{2,10},{10... | collective-permute-start | bytes 98312 | tf_op jit(solution)/shard_map/ppermute | solution.py:33
  24.9 0.0 collective-permute-done.6
  24.9 0.0 collective-permute-done.5
  24.9 2.7 %collective-permute-done.9 = bf16[128,128]{1,0:T(8,128)(2,1)S(1)} collective-permute-done((bf16[128,128]{1,0:T(8,128)(2,1)S(1)}, bf16[128,128]{1,0:T(8,128)(2,1)S(1)}, u32[]{:S(2)}, u32[]{:S(2)}) %collective-permute-start.9) | collective-permute-done | bytes 32800 | tf_op jit(solution)/shard_map/ppermute | solution.py:33
  27.6 0.1 collective-permute-done.10
  27.7 0.7 %copy.10 = f32[1,1,128,128]{3,2,1,0:T(8,128)} copy(f32[1,1,128,128]{2,3,1,0:T(8,128)S(1)} %add_bitcast_fusion) | data formatting | bytes 131072
  (9 shorter events, 0.1 us)
Async XLA Ops:
  1.4 7.0 %collective-permute-start.1 = (bf16[1,144,128]{2,1,0:T(8,128)(2,1)S(1)}, bf16[1,144,128]{2,1,0:T(8,128)(2,1)S(1)}, u32[]{:S(2)}, u32[]{:S(2)}) collective-permute-start(bf16[1,144,128]{2,1,0:T(8,128)(2,1)S(1)} %get-tuple-element.26), channel_id=1, source_target_pairs={{8,16},{16,8},{24,0},{0,24},{9,17},{17,9},{25,1},{1,25},{10,18},{1... | collective-permute-start | bytes 110600 | tf_op jit(solution)/shard_map/ppermute | solution.py:33
  5.4 4.0 %collective-permute-start = (bf16[1,144,128]{2,1,0:T(8,128)(2,1)S(1)}, bf16[1,144,128]{2,1,0:T(8,128)(2,1)S(1)}, u32[]{:S(2)}, u32[]{:S(2)}) collective-permute-start(bf16[1,144,128]{2,1,0:T(8,128)(2,1)S(1)} %get-tuple-element.26), channel_id=1, source_target_pairs={{0,8},{8,0},{16,24},{24,16},{1,9},{9,1},{17,25},{25,17},{2,10},{10... | collective-permute-start | bytes 110600 | tf_op jit(solution)/shard_map/ppermute | solution.py:33
  5.9 9.0 %collective-permute-start.4 = (bf16[1,144,128]{2,1,0:T(8,128)(2,1)S(1)}, bf16[1,144,128]{2,1,0:T(8,128)(2,1)S(1)}, u32[]{:S(2)}, u32[]{:S(2)}) collective-permute-start(bf16[1,144,128]{2,1,0:T(8,128)(2,1)S(1)} %get-tuple-element.26), channel_id=1, source_target_pairs={{1,2},{2,1},{3,4},{4,3},{5,6},{6,5},{7,0},{0,7},{9,10},{10,9},{11,... | collective-permute-start | bytes 110600 | tf_op jit(solution)/shard_map/ppermute | solution.py:33
  9.4 6.2 %collective-permute-start.3 = (bf16[2,144,128]{2,1,0:T(8,128)(2,1)S(1)}, bf16[2,144,128]{2,1,0:T(8,128)(2,1)S(1)}, u32[]{:S(2)}, u32[]{:S(2)}) collective-permute-start(bf16[2,144,128]{2,1,0:T(8,128)(2,1)S(1)} %get-tuple-element.52), channel_id=1, source_target_pairs={{1,2},{2,1},{3,4},{4,3},{5,6},{6,5},{7,0},{0,7},{9,10},{10,9},{11,... | collective-permute-start | bytes 221192 | tf_op jit(solution)/shard_map/ppermute | solution.py:33
  11.5 1.4 %collective-permute-start.2 = (bf16[3,144,128]{2,1,0:T(8,128)(2,1)S(1)}, bf16[3,144,128]{2,1,0:T(8,128)(2,1)S(1)}, u32[]{:S(2)}, u32[]{:S(2)}) collective-permute-start(bf16[3,144,128]{2,1,0:T(8,128)(2,1)S(1)} %pad_maximum_fusion.own_row), channel_id=1, source_target_pairs={{0,1},{1,0},{2,3},{3,2},{4,5},{5,4},{6,7},{7,6},{8,9},{9,8},{10,11... | collective-permute-start | bytes 331784 | tf_op jit(solution)/shard_map/ppermute | solution.py:33
  17.0 5.6 %collective-permute-start.8 = (bf16[2,128,128]{2,1,0:T(8,128)(2,1)S(1)}, bf16[2,128,128]{2,1,0:T(8,128)(2,1)S(1)}, u32[]{:S(2)}, u32[]{:S(2)}) collective-permute-start(bf16[2,128,128]{2,1,0:T(8,128)(2,1)S(1)} %get-tuple-element.47), channel_id=1, source_target_pairs={{1,2},{2,1},{3,4},{4,3},{5,6},{6,5},{7,0},{0,7},{9,10},{10,9},{11,... | collective-permute-start | bytes 196616 | tf_op jit(solution)/shard_map/ppermute | solution.py:33
  18.5 4.1 %collective-permute-start.7 = (bf16[2,128,128]{2,1,0:T(8,128)(2,1)S(1)}, bf16[2,128,128]{2,1,0:T(8,128)(2,1)S(1)}, u32[]{:S(2)}, u32[]{:S(2)}) collective-permute-start(bf16[2,128,128]{2,1,0:T(8,128)(2,1)S(1)} %get-tuple-element.46), channel_id=1, source_target_pairs={{0,1},{1,0},{2,3},{3,2},{4,5},{5,4},{6,7},{7,6},{8,9},{9,8},{10,11... | collective-permute-start | bytes 196616 | tf_op jit(solution)/shard_map/ppermute | solution.py:33
  18.6 6.3 %collective-permute-start.6 = (bf16[128,128]{1,0:T(8,128)(2,1)S(1)}, bf16[128,128]{1,0:T(8,128)(2,1)S(1)}, u32[]{:S(2)}, u32[]{:S(2)}) collective-permute-start(bf16[128,128]{1,0:T(8,128)(2,1)S(1)} %get-tuple-element.45), channel_id=1, source_target_pairs={{0,1},{1,0},{2,3},{3,2},{4,5},{5,4},{6,7},{7,6},{8,9},{9,8},{10,11... | collective-permute-start | bytes 98312 | tf_op jit(solution)/shard_map/ppermute | solution.py:33
  19.1 5.8 %collective-permute-start.5 = (bf16[128,128]{1,0:T(8,128)(2,1)S(1)}, bf16[128,128]{1,0:T(8,128)(2,1)S(1)}, u32[]{:S(2)}, u32[]{:S(2)}) collective-permute-start(bf16[128,128]{1,0:T(8,128)(2,1)S(1)} %get-tuple-element.44), channel_id=1, source_target_pairs={{1,2},{2,1},{3,4},{4,3},{5,6},{6,5},{7,0},{0,7},{9,10},{10,9},{11,... | collective-permute-start | bytes 98312 | tf_op jit(solution)/shard_map/ppermute | solution.py:33
  22.7 4.9 %collective-permute-start.9 = (bf16[128,128]{1,0:T(8,128)(2,1)S(1)}, bf16[128,128]{1,0:T(8,128)(2,1)S(1)}, u32[]{:S(2)}, u32[]{:S(2)}) collective-permute-start(bf16[128,128]{1,0:T(8,128)(2,1)S(1)} %get-tuple-element.51), channel_id=1, source_target_pairs={{8,16},{16,8},{24,0},{0,24},{9,17},{17,9},{25,1},{1,25},{10,18},{1... | collective-permute-start | bytes 98312 | tf_op jit(solution)/shard_map/ppermute | solution.py:33
  23.7 3.9 %collective-permute-start.10 = (bf16[128,128]{1,0:T(8,128)(2,1)S(1)}, bf16[128,128]{1,0:T(8,128)(2,1)S(1)}, u32[]{:S(2)}, u32[]{:S(2)}) collective-permute-start(bf16[128,128]{1,0:T(8,128)(2,1)S(1)} %get-tuple-element.50), channel_id=1, source_target_pairs={{0,8},{8,0},{16,24},{24,16},{1,9},{9,1},{17,25},{25,17},{2,10},{10... | collective-permute-start | bytes 98312 | tf_op jit(solution)/shard_map/ppermute | solution.py:33

commit v9 on v8

--- a/solution.py
+++ b/solution.py
@@ -289,11 +289,12 @@
 
 
 def late_kernel(
-    table, own_row, near_row, basis, grads, first_ref, second_ref, mix_ref, square_ref,
-    near_out, near_middle, own_out, updated_ref,
+    far_middle, table, own_row, near_row, basis, grads, first_ref, second_ref, mix_ref, square_ref,
+    near_out, near_middle, far_held, own_out, updated_ref,
     updated, sems,
 ):
     rows = first_ref.shape[0]
+    far_held[...] = far_middle[...]
     second = second_ref[...]
     quadratic = jnp.dot(second, square_ref[...], preferred_element_type=f32)
     linear = jnp.dot(first_ref[...], mix_ref[...], preferred_element_type=f32)
@@ -411,17 +412,18 @@
         ),
     )
     far_in = swap_back(far_out, "gy", 1)
-    near_out, near_middle, own_out, updated = local(
+    near_out, near_middle, far_middle, own_out, updated = local(
         late_kernel,
         "late",
         [
             ((2, channels, rows), bf16),
             ((channels, rows), bf16),
+            ((channels, rows), bf16),
             ((3, channels, rows), f32),
             (square, bf16),
         ],
         [pltpu.VMEM(square, bf16)],
-        (table, own_row, near_row, basis, grads, first_bf, second_bf, mix_w, square_w),
+        (far_middle, table, own_row, near_row, basis, grads, first_bf, second_bf, mix_w, square_w),
         sent=1,
     )
     near_in = swap_back(near_out, "gy", 0)

time: 28.6 us -> 28.9 us (1.010)
  Pallas kernels: 5 us -> 5.45 us
    pallas_call x4, Pallas kernels: 5 us -> 5.45 us  [local(): pl.pallas_call(kernel, out_shape=tuple((jax.ShapeDtypeStruct(*out) for ou...]
  transfers between devices with their start and end apart: 11 -> 11, of which waited for: 6 -> 6; matrix products, arithmetic and copies ran while one was open for 1% -> 1% of each run, Pallas kernels for 10% -> 11%
where the time goes in v9:
time: 28.9 us; the launch traced here: 28.8 us
  starting transfers between devices  15.4 us (53%)
  waiting for transfers between devices  5.59 us (19%)
  Pallas kernels  5.45 us (19%)
  between operations  1.39 us (5%)
  local copies, waits for them, and re-layouts  0.81 us (3%)
    ppermute x11, starting transfers between devices, swap(): return lax.ppermute(block, axis, pairs)  15.4 us
    ppermute x11, waiting for transfers between devices, swap(): return lax.ppermute(block, axis, pairs)  5.59 us
    pallas_call x4, Pallas kernels, local(): pl.pallas_call(kernel, out_shape=tuple((jax.ShapeDtypeStruct(*out) for ou...  5.45 us
    unnamed x1, local copies, waits for them, and re-layouts  0.73 us
  transfers between devices with their start and end apart: 11, of which 6 were waited for; matrix products, arithmetic and copies ran while one was open for 1% of the time, Pallas kernels for 11%

profile of v9, /device:TPU:0, one launch (start us, length us, event | category | flops | bytes accessed | tf_op | source)
XLA Modules:
  0.0 28.8 jit_solution(3190756579965811356)
XLA Ops:
  0.6 0.8 %pack.1 = (bf16[1,144,128]{2,1,0:T(8,128)(2,1)S(1)}, s32[1,1,1,8]{3,2,1,0:T(1,128)S(1)}) custom-call(bf16[1,1,128,128]{3,2,1,0:T(8,128)(2,1)} %feat_ref.1, bf16[1,1,3,128]{3,2,1,0:T(4,128)(2,1)} %pos_ref.1, s32[1,1,1,8]{3,2,1,0:T(1,128)} %senders_ref.1), custom_call_target="tpu_custom_call" | custom-call | tf_op jit(solution)/shard_map/pack/pallas_call | solution.py:335
  1.4 4.0 %collective-permute-start.1 = (bf16[1,144,128]{2,1,0:T(8,128)(2,1)S(1)}, bf16[1,144,128]{2,1,0:T(8,128)(2,1)S(1)}, u32[]{:S(2)}, u32[]{:S(2)}) collective-permute-start(bf16[1,144,128]{2,1,0:T(8,128)(2,1)S(1)} %get-tuple-element.27), channel_id=1, source_target_pairs={{8,16},{16,8},{24,0},{0,24},{9,17},{17,9},{25,1},{1,25},{10,18},{1... | collective-permute-start | bytes 110600 | tf_op jit(solution)/shard_map/ppermute | solution.py:33
  5.4 0.5 %collective-permute-start = (bf16[1,144,128]{2,1,0:T(8,128)(2,1)S(1)}, bf16[1,144,128]{2,1,0:T(8,128)(2,1)S(1)}, u32[]{:S(2)}, u32[]{:S(2)}) collective-permute-start(bf16[1,144,128]{2,1,0:T(8,128)(2,1)S(1)} %get-tuple-element.27), channel_id=1, source_target_pairs={{0,8},{8,0},{16,24},{24,16},{1,9},{9,1},{17,25},{25,17},{2,10},{10... | collective-permute-start | bytes 110600 | tf_op jit(solution)/shard_map/ppermute | solution.py:33
  5.9 2.5 %collective-permute-start.4 = (bf16[1,144,128]{2,1,0:T(8,128)(2,1)S(1)}, bf16[1,144,128]{2,1,0:T(8,128)(2,1)S(1)}, u32[]{:S(2)}, u32[]{:S(2)}) collective-permute-start(bf16[1,144,128]{2,1,0:T(8,128)(2,1)S(1)} %get-tuple-element.27), channel_id=1, source_target_pairs={{1,2},{2,1},{3,4},{4,3},{5,6},{6,5},{7,0},{0,7},{9,10},{10,9},{11,... | collective-permute-start | bytes 110600 | tf_op jit(solution)/shard_map/ppermute | solution.py:33
  8.4 0.0 collective-permute-done.1
  8.4 0.9 %collective-permute-done = bf16[1,144,128]{2,1,0:T(8,128)(2,1)S(1)} collective-permute-done((bf16[1,144,128]{2,1,0:T(8,128)(2,1)S(1)}, bf16[1,144,128]{2,1,0:T(8,128)(2,1)S(1)}, u32[]{:S(2)}, u32[]{:S(2)}) %collective-permute-start) | collective-permute-done | bytes 36896 | tf_op jit(solution)/shard_map/ppermute | solution.py:33
  9.4 2.2 %collective-permute-start.3 = (bf16[2,144,128]{2,1,0:T(8,128)(2,1)S(1)}, bf16[2,144,128]{2,1,0:T(8,128)(2,1)S(1)}, u32[]{:S(2)}, u32[]{:S(2)}) collective-permute-start(bf16[2,144,128]{2,1,0:T(8,128)(2,1)S(1)} %get-tuple-element.54), channel_id=1, source_target_pairs={{1,2},{2,1},{3,4},{4,3},{5,6},{6,5},{7,0},{0,7},{9,10},{10,9},{11,... | collective-permute-start | bytes 221192 | tf_op jit(solution)/shard_map/ppermute | solution.py:33
  11.5 0.1 collective-permute-start.2
  11.6 0.1 pad_add_fusion
  12.4 0.6 %collective-permute-done.2.near_row = bf16[3,144,128]{2,1,0:T(8,128)(2,1)S(1)} collective-permute-done((bf16[3,144,128]{2,1,0:T(8,128)(2,1)S(1)}, bf16[3,144,128]{2,1,0:T(8,128)(2,1)S(1)}, u32[]{:S(2)}, u32[]{:S(2)}) %collective-permute-start.2) | collective-permute-done | bytes 110624 | tf_op jit(solution)/shard_map/ppermute | solution.py:33
  12.9 0.1 broadcast_in_dim.19.steps
  13.0 2.0 %early.1 = (s32[24,128]{1,0:T(8,128)S(1)}, bf16[1024,768]{1,0:T(8,128)(2,1)S(1)}, f32[5,128,128]{2,1,0:T(8,128)S(1)}, bf16[128,128]{1,0:T(8,128)(2,1)S(1)}, f32[...) custom-call(s32[8,128]{1,0:T(8,128)S(1)} %broadcast_in_dim.19.steps,, ...), custom_call_target="tpu_custom_call" | custom-call | tf_op jit(solution)/shard_map/early/pallas_call | solution.py:335
  15.0 0.0 collective-permute-done.4.far_own
  15.0 0.5 %collective-permute-done.3.far_sides = bf16[2,144,128]{2,1,0:T(8,128)(2,1)S(1)} collective-permute-done((bf16[2,144,128]{2,1,0:T(8,128)(2,1)S(1)}, bf16[2,144,128]{2,1,0:T(8,128)(2,1)S(1)}, u32[]{:S(2)}, u32[]{:S(2)}) %collective-permute-start.3) | collective-permute-done | bytes 73760 | tf_op jit(solution)/shard_map/ppermute | solution.py:33
  15.5 1.5 %middle.1 = (bf16[2,128,128]{2,1,0:T(8,128)(2,1)S(1)}, bf16[128,128]{1,0:T(8,128)(2,1)S(1)}, bf16[512,1024]{1,0:T(8,128)(2,1)S(1)}, bf16[128,128]{1,0:T(8,128)(2,1)S(1)}, bf16[384,128]{1,0:T(8,128)(2,1)S(1)}) custom-call(s32[24,128]{1,0:T(8,128)S(1)} %get-tuple-element.28.table, bf16[2,144,128]{2,1,0:T(8,128)(2,1)S(1)} %collective-permute-done.3.far_sides, ...), custom_call_target="tpu_custom_call" | custom-call | tf_op jit(solution)/shard_map/middle/pallas_call | solution.py:335
  17.1 0.7 %collective-permute-start.8 = (bf16[2,128,128]{2,1,0:T(8,128)(2,1)S(1)}, bf16[2,128,128]{2,1,0:T(8,128)(2,1)S(1)}, u32[]{:S(2)}, u32[]{:S(2)}) collective-permute-start(bf16[2,128,128]{2,1,0:T(8,128)(2,1)S(1)} %get-tuple-element.49), channel_id=1, source_target_pairs={{1,2},{2,1},{3,4},{4,3},{5,6},{6,5},{7,0},{0,7},{9,10},{10,9},{11,... | collective-permute-start | bytes 196616 | tf_op jit(solution)/shard_map/ppermute | solution.py:33
  17.7 1.2 %late.1 = (bf16[2,128,128]{2,1,0:T(8,128)(2,1)S(1)}, bf16[128,128]{1,0:T(8,128)(2,1)S(1)}, bf16[128,128]{1,0:T(8,128)(2,1)S(1)}, f32[3,128,128]{2,1,0:T(8,128)S(1)}, bf16[128,128]{1,0:T(8,128)(2,1)}) custom-call(bf16[128,128]{1,0:T(8,128)(2,1)S(1)} %get-tuple-element.38.far_middle, s32[24,128]{1,0:T(8,128)S(1)} %get-tuple-element.28.table, ...), custom_call_target="tpu_custom_call" | custom-call | tf_op jit(solution)/shard_map/late/pallas_call | solution.py:335
  18.9 0.1 collective-permute-start.7
  18.9 3.4 %collective-permute-start.5 = (bf16[128,128]{1,0:T(8,128)(2,1)S(1)}, bf16[128,128]{1,0:T(8,128)(2,1)S(1)}, u32[]{:S(2)}, u32[]{:S(2)}) collective-permute-start(bf16[128,128]{1,0:T(8,128)(2,1)S(1)} %get-tuple-element.46), channel_id=1, source_target_pairs={{1,2},{2,1},{3,4},{4,3},{5,6},{6,5},{7,0},{0,7},{9,10},{10,9},{11,... | collective-permute-start | bytes 98312 | tf_op jit(solution)/shard_map/ppermute | solution.py:33
  22.4 0.0 collective-permute-start.6
  22.4 0.2 collective-permute-done.8
  22.6 0.0 collective-permute-done.7
  22.7 1.5 %collective-permute-start.9 = (bf16[128,128]{1,0:T(8,128)(2,1)S(1)}, bf16[128,128]{1,0:T(8,128)(2,1)S(1)}, u32[]{:S(2)}, u32[]{:S(2)}) collective-permute-start(bf16[128,128]{1,0:T(8,128)(2,1)S(1)} %get-tuple-element.53), channel_id=1, source_target_pairs={{8,16},{16,8},{24,0},{0,24},{9,17},{17,9},{25,1},{1,25},{10,18},{1... | collective-permute-start | bytes 98312 | tf_op jit(solution)/shard_map/ppermute | solution.py:33
  24.2 0.5 %collective-permute-start.10 = (bf16[128,128]{1,0:T(8,128)(2,1)S(1)}, bf16[128,128]{1,0:T(8,128)(2,1)S(1)}, u32[]{:S(2)}, u32[]{:S(2)}) collective-permute-start(bf16[128,128]{1,0:T(8,128)(2,1)S(1)} %get-tuple-element.52), channel_id=1, source_target_pairs={{0,8},{8,0},{16,24},{24,16},{1,9},{9,1},{17,25},{25,17},{2,10},{10... | collective-permute-start | bytes 98312 | tf_op jit(solution)/shard_map/ppermute | solution.py:33
  24.7 0.0 collective-permute-done.5
  24.7 0.0 collective-permute-done.6
  24.7 2.9 %collective-permute-done.9 = bf16[128,128]{1,0:T(8,128)(2,1)S(1)} collective-permute-done((bf16[128,128]{1,0:T(8,128)(2,1)S(1)}, bf16[128,128]{1,0:T(8,128)(2,1)S(1)}, u32[]{:S(2)}, u32[]{:S(2)}) %collective-permute-start.9) | collective-permute-done | bytes 32800 | tf_op jit(solution)/shard_map/ppermute | solution.py:33
  27.6 0.5 %collective-permute-done.10 = bf16[128,128]{1,0:T(8,128)(2,1)S(1)} collective-permute-done((bf16[128,128]{1,0:T(8,128)(2,1)S(1)}, bf16[128,128]{1,0:T(8,128)(2,1)S(1)}, u32[]{:S(2)}, u32[]{:S(2)}) %collective-permute-start.10) | collective-permute-done | bytes 32800 | tf_op jit(solution)/shard_map/ppermute | solution.py:33
  28.1 0.7 %copy.10 = f32[1,1,128,128]{3,2,1,0:T(8,128)} copy(f32[1,1,128,128]{2,3,1,0:T(8,128)S(1)} %add_bitcast_fusion) | data formatting | bytes 131072
  (9 shorter events, 0.1 us)
Async XLA Ops:
  1.4 7.0 %collective-permute-start.1 = (bf16[1,144,128]{2,1,0:T(8,128)(2,1)S(1)}, bf16[1,144,128]{2,1,0:T(8,128)(2,1)S(1)}, u32[]{:S(2)}, u32[]{:S(2)}) collective-permute-start(bf16[1,144,128]{2,1,0:T(8,128)(2,1)S(1)} %get-tuple-element.27), channel_id=1, source_target_pairs={{8,16},{16,8},{24,0},{0,24},{9,17},{17,9},{25,1},{1,25},{10,18},{1... | collective-permute-start | bytes 110600 | tf_op jit(solution)/shard_map/ppermute | solution.py:33
  5.4 4.0 %collective-permute-start = (bf16[1,144,128]{2,1,0:T(8,128)(2,1)S(1)}, bf16[1,144,128]{2,1,0:T(8,128)(2,1)S(1)}, u32[]{:S(2)}, u32[]{:S(2)}) collective-permute-start(bf16[1,144,128]{2,1,0:T(8,128)(2,1)S(1)} %get-tuple-element.27), channel_id=1, source_target_pairs={{0,8},{8,0},{16,24},{24,16},{1,9},{9,1},{17,25},{25,17},{2,10},{10... | collective-permute-start | bytes 110600 | tf_op jit(solution)/shard_map/ppermute | solution.py:33
  5.9 9.1 %collective-permute-start.4 = (bf16[1,144,128]{2,1,0:T(8,128)(2,1)S(1)}, bf16[1,144,128]{2,1,0:T(8,128)(2,1)S(1)}, u32[]{:S(2)}, u32[]{:S(2)}) collective-permute-start(bf16[1,144,128]{2,1,0:T(8,128)(2,1)S(1)} %get-tuple-element.27), channel_id=1, source_target_pairs={{1,2},{2,1},{3,4},{4,3},{5,6},{6,5},{7,0},{0,7},{9,10},{10,9},{11,... | collective-permute-start | bytes 110600 | tf_op jit(solution)/shard_map/ppermute | solution.py:33
  9.4 6.2 %collective-permute-start.3 = (bf16[2,144,128]{2,1,0:T(8,128)(2,1)S(1)}, bf16[2,144,128]{2,1,0:T(8,128)(2,1)S(1)}, u32[]{:S(2)}, u32[]{:S(2)}) collective-permute-start(bf16[2,144,128]{2,1,0:T(8,128)(2,1)S(1)} %get-tuple-element.54), channel_id=1, source_target_pairs={{1,2},{2,1},{3,4},{4,3},{5,6},{6,5},{7,0},{0,7},{9,10},{10,9},{11,... | collective-permute-start | bytes 221192 | tf_op jit(solution)/shard_map/ppermute | solution.py:33
  11.5 1.4 %collective-permute-start.2 = (bf16[3,144,128]{2,1,0:T(8,128)(2,1)S(1)}, bf16[3,144,128]{2,1,0:T(8,128)(2,1)S(1)}, u32[]{:S(2)}, u32[]{:S(2)}) collective-permute-start(bf16[3,144,128]{2,1,0:T(8,128)(2,1)S(1)} %pad_maximum_fusion.own_row), channel_id=1, source_target_pairs={{0,1},{1,0},{2,3},{3,2},{4,5},{5,4},{6,7},{7,6},{8,9},{9,8},{10,11... | collective-permute-start | bytes 331784 | tf_op jit(solution)/shard_map/ppermute | solution.py:33
  17.1 5.6 %collective-permute-start.8 = (bf16[2,128,128]{2,1,0:T(8,128)(2,1)S(1)}, bf16[2,128,128]{2,1,0:T(8,128)(2,1)S(1)}, u32[]{:S(2)}, u32[]{:S(2)}) collective-permute-start(bf16[2,128,128]{2,1,0:T(8,128)(2,1)S(1)} %get-tuple-element.49), channel_id=1, source_target_pairs={{1,2},{2,1},{3,4},{4,3},{5,6},{6,5},{7,0},{0,7},{9,10},{10,9},{11,... | collective-permute-start | bytes 196616 | tf_op jit(solution)/shard_map/ppermute | solution.py:33
  18.9 3.8 %collective-permute-start.7 = (bf16[2,128,128]{2,1,0:T(8,128)(2,1)S(1)}, bf16[2,128,128]{2,1,0:T(8,128)(2,1)S(1)}, u32[]{:S(2)}, u32[]{:S(2)}) collective-permute-start(bf16[2,128,128]{2,1,0:T(8,128)(2,1)S(1)} %get-tuple-element.48), channel_id=1, source_target_pairs={{0,1},{1,0},{2,3},{3,2},{4,5},{5,4},{6,7},{7,6},{8,9},{9,8},{10,11... | collective-permute-start | bytes 196616 | tf_op jit(solution)/shard_map/ppermute | solution.py:33
  18.9 5.8 %collective-permute-start.5 = (bf16[128,128]{1,0:T(8,128)(2,1)S(1)}, bf16[128,128]{1,0:T(8,128)(2,1)S(1)}, u32[]{:S(2)}, u32[]{:S(2)}) collective-permute-start(bf16[128,128]{1,0:T(8,128)(2,1)S(1)} %get-tuple-element.46), channel_id=1, source_target_pairs={{1,2},{2,1},{3,4},{4,3},{5,6},{6,5},{7,0},{0,7},{9,10},{10,9},{11,... | collective-permute-start | bytes 98312 | tf_op jit(solution)/shard_map/ppermute | solution.py:33
  22.4 2.3 %collective-permute-start.6 = (bf16[128,128]{1,0:T(8,128)(2,1)S(1)}, bf16[128,128]{1,0:T(8,128)(2,1)S(1)}, u32[]{:S(2)}, u32[]{:S(2)}) collective-permute-start(bf16[128,128]{1,0:T(8,128)(2,1)S(1)} %get-tuple-element.47), channel_id=1, source_target_pairs={{0,1},{1,0},{2,3},{3,2},{4,5},{5,4},{6,7},{7,6},{8,9},{9,8},{10,11... | collective-permute-start | bytes 98312 | tf_op jit(solution)/shard_map/ppermute | solution.py:33
  22.7 4.9 %collective-permute-start.9 = (bf16[128,128]{1,0:T(8,128)(2,1)S(1)}, bf16[128,128]{1,0:T(8,128)(2,1)S(1)}, u32[]{:S(2)}, u32[]{:S(2)}) collective-permute-start(bf16[128,128]{1,0:T(8,128)(2,1)S(1)} %get-tuple-element.53), channel_id=1, source_target_pairs={{8,16},{16,8},{24,0},{0,24},{9,17},{17,9},{25,1},{1,25},{10,18},{1... | collective-permute-start | bytes 98312 | tf_op jit(solution)/shard_map/ppermute | solution.py:33
  24.2 3.9 %collective-permute-start.10 = (bf16[128,128]{1,0:T(8,128)(2,1)S(1)}, bf16[128,128]{1,0:T(8,128)(2,1)S(1)}, u32[]{:S(2)}, u32[]{:S(2)}) collective-permute-start(bf16[128,128]{1,0:T(8,128)(2,1)S(1)} %get-tuple-element.52), channel_id=1, source_target_pairs={{0,8},{8,0},{16,24},{24,16},{1,9},{9,1},{17,25},{25,17},{2,10},{10... | collective-permute-start | bytes 98312 | tf_op jit(solution)/shard_map/ppermute | solution.py:33

commit v10 on v8

--- a/solution.py
+++ b/solution.py
@@ -45,13 +45,13 @@
 
 def pack_kernel(feat_ref, pos_ref, senders_ref, out_ref, senders, pos, sems):
     rows = feat_ref.shape[2]
-    pairs = ((pos_ref, pos), (feat_ref.at[0, 0], out_ref.at[0, :rows]), (senders_ref, senders))
+    pairs = ((feat_ref.at[0, 0], out_ref.at[0, :rows]), (pos_ref, pos), (senders_ref, senders))
     copies = start_copies(pairs, sems)
-    copies[0].wait()
+    copies[1].wait()
     tail = jnp.zeros((13, out_ref.shape[2]), f32)
     out_ref[0, rows:, :] = jnp.concatenate([pos[0, 0].astype(f32), tail], axis=0).astype(bf16)
-    for copy in copies[1:]:
-        copy.wait()
+    copies[2].wait()
+    copies[0].wait()
 
 
 def start_copies(pairs, sems):

time: 28.6 us -> 28.8 us (level)
  starting transfers between devices: 15.6 us -> 14.9 us
  waiting for transfers between devices: 5.45 us -> 6.03 us
    ppermute x11, starting transfers between devices: 15.6 us -> 14.9 us  [swap(): return lax.ppermute(block, axis, pairs)]
    ppermute x11, waiting for transfers between devices: 5.45 us -> 6.03 us  [swap(): return lax.ppermute(block, axis, pairs)]
  transfers between devices with their start and end apart: 11 -> 11, of which waited for: 6 -> 7; matrix products, arithmetic and copies ran while one was open for 1% -> 1% of each run, Pallas kernels for 10% -> 14%
where the time goes in v10:
time: 28.8 us; the launch traced here: 28.5 us
  starting transfers between devices  14.9 us (52%)
  waiting for transfers between devices  6.03 us (21%)
  Pallas kernels  5.2 us (18%)
  between operations  1.39 us (5%)
  local copies, waits for them, and re-layouts  0.81 us (3%)
    ppermute x11, starting transfers between devices, swap(): return lax.ppermute(block, axis, pairs)  14.9 us
    ppermute x11, waiting for transfers between devices, swap(): return lax.ppermute(block, axis, pairs)  6.03 us
    pallas_call x4, Pallas kernels, local(): pl.pallas_call(kernel, out_shape=tuple((jax.ShapeDtypeStruct(*out) for ou...  5.2 us
    unnamed x1, local copies, waits for them, and re-layouts  0.73 us
  transfers between devices with their start and end apart: 11, of which 7 were waited for; matrix products, arithmetic and copies ran while one was open for 1% of the time, Pallas kernels for 14%

profile of v10, /device:TPU:0, one launch (start us, length us, event | category | flops | bytes accessed | tf_op | source)
XLA Modules:
  0.0 28.5 jit_solution(1790785268794470102)
XLA Ops:
  0.6 0.8 %pack.1 = (bf16[1,144,128]{2,1,0:T(8,128)(2,1)S(1)}, s32[1,1,1,8]{3,2,1,0:T(1,128)S(1)}) custom-call(bf16[1,1,128,128]{3,2,1,0:T(8,128)(2,1)} %feat_ref.1, bf16[1,1,3,128]{3,2,1,0:T(4,128)(2,1)} %pos_ref.1, s32[1,1,1,8]{3,2,1,0:T(1,128)} %senders_ref.1), custom_call_target="tpu_custom_call" | custom-call | tf_op jit(solution)/shard_map/pack/pallas_call | solution.py:334
  1.4 4.0 %collective-permute-start.1 = (bf16[1,144,128]{2,1,0:T(8,128)(2,1)S(1)}, bf16[1,144,128]{2,1,0:T(8,128)(2,1)S(1)}, u32[]{:S(2)}, u32[]{:S(2)}) collective-permute-start(bf16[1,144,128]{2,1,0:T(8,128)(2,1)S(1)} %get-tuple-element.26), channel_id=1, source_target_pairs={{8,16},{16,8},{24,0},{0,24},{9,17},{17,9},{25,1},{1,25},{10,18},{1... | collective-permute-start | bytes 110600 | tf_op jit(solution)/shard_map/ppermute | solution.py:33
  5.4 0.5 %collective-permute-start = (bf16[1,144,128]{2,1,0:T(8,128)(2,1)S(1)}, bf16[1,144,128]{2,1,0:T(8,128)(2,1)S(1)}, u32[]{:S(2)}, u32[]{:S(2)}) collective-permute-start(bf16[1,144,128]{2,1,0:T(8,128)(2,1)S(1)} %get-tuple-element.26), channel_id=1, source_target_pairs={{0,8},{8,0},{16,24},{24,16},{1,9},{9,1},{17,25},{25,17},{2,10},{10... | collective-permute-start | bytes 110600 | tf_op jit(solution)/shard_map/ppermute | solution.py:33
  5.9 2.5 %collective-permute-start.4 = (bf16[1,144,128]{2,1,0:T(8,128)(2,1)S(1)}, bf16[1,144,128]{2,1,0:T(8,128)(2,1)S(1)}, u32[]{:S(2)}, u32[]{:S(2)}) collective-permute-start(bf16[1,144,128]{2,1,0:T(8,128)(2,1)S(1)} %get-tuple-element.26), channel_id=1, source_target_pairs={{1,2},{2,1},{3,4},{4,3},{5,6},{6,5},{7,0},{0,7},{9,10},{10,9},{11,... | collective-permute-start | bytes 110600 | tf_op jit(solution)/shard_map/ppermute | solution.py:33
  8.4 0.0 collective-permute-done.1
  8.4 0.9 %collective-permute-done = bf16[1,144,128]{2,1,0:T(8,128)(2,1)S(1)} collective-permute-done((bf16[1,144,128]{2,1,0:T(8,128)(2,1)S(1)}, bf16[1,144,128]{2,1,0:T(8,128)(2,1)S(1)}, u32[]{:S(2)}, u32[]{:S(2)}) %collective-permute-start) | collective-permute-done | bytes 36896 | tf_op jit(solution)/shard_map/ppermute | solution.py:33
  9.4 2.2 %collective-permute-start.3 = (bf16[2,144,128]{2,1,0:T(8,128)(2,1)S(1)}, bf16[2,144,128]{2,1,0:T(8,128)(2,1)S(1)}, u32[]{:S(2)}, u32[]{:S(2)}) collective-permute-start(bf16[2,144,128]{2,1,0:T(8,128)(2,1)S(1)} %get-tuple-element.52), channel_id=1, source_target_pairs={{1,2},{2,1},{3,4},{4,3},{5,6},{6,5},{7,0},{0,7},{9,10},{10,9},{11,... | collective-permute-start | bytes 221192 | tf_op jit(solution)/shard_map/ppermute | solution.py:33
  11.5 0.1 collective-permute-start.2
  11.6 0.1 pad_add_fusion
  12.4 0.6 %collective-permute-done.2.near_row = bf16[3,144,128]{2,1,0:T(8,128)(2,1)S(1)} collective-permute-done((bf16[3,144,128]{2,1,0:T(8,128)(2,1)S(1)}, bf16[3,144,128]{2,1,0:T(8,128)(2,1)S(1)}, u32[]{:S(2)}, u32[]{:S(2)}) %collective-permute-start.2) | collective-permute-done | bytes 110624 | tf_op jit(solution)/shard_map/ppermute | solution.py:33
  12.9 0.1 broadcast_in_dim.19.steps
  13.0 2.3 %early.1 = (s32[24,128]{1,0:T(8,128)S(1)}, bf16[1024,768]{1,0:T(8,128)(2,1)S(1)}, f32[5,128,128]{2,1,0:T(8,128)S(1)}, bf16[128,128]{1,0:T(8,128)(2,1)S(1)}, f32[...) custom-call(s32[8,128]{1,0:T(8,128)S(1)} %broadcast_in_dim.19.steps,, ...), custom_call_target="tpu_custom_call" | custom-call | tf_op jit(solution)/shard_map/early/pallas_call | solution.py:334
  15.3 0.0 collective-permute-done.4.far_own
  15.3 0.2 collective-permute-done.3.far_sides
  15.5 0.5 %middle.1 = (bf16[2,128,128]{2,1,0:T(8,128)(2,1)S(1)}, bf16[128,128]{1,0:T(8,128)(2,1)S(1)}, bf16[512,1024]{1,0:T(8,128)(2,1)S(1)}, bf16[128,128]{1,0:T(8,128)(2,1)S(1)}, bf16[384,128]{1,0:T(8,128)(2,1)S(1)}) custom-call(s32[24,128]{1,0:T(8,128)S(1)} %get-tuple-element.27.table, bf16[2,144,128]{2,1,0:T(8,128)(2,1)S(1)} %collective-permute-done.3.far_sides, ...), custom_call_target="tpu_custom_call" | custom-call | tf_op jit(solution)/shard_map/middle/pallas_call | solution.py:334
  16.1 2.6 %collective-permute-start.8 = (bf16[2,128,128]{2,1,0:T(8,128)(2,1)S(1)}, bf16[2,128,128]{2,1,0:T(8,128)(2,1)S(1)}, u32[]{:S(2)}, u32[]{:S(2)}) collective-permute-start(bf16[2,128,128]{2,1,0:T(8,128)(2,1)S(1)} %get-tuple-element.47), channel_id=1, source_target_pairs={{1,2},{2,1},{3,4},{4,3},{5,6},{6,5},{7,0},{0,7},{9,10},{10,9},{11,... | collective-permute-start | bytes 196616 | tf_op jit(solution)/shard_map/ppermute | solution.py:33
  18.7 1.6 %late.1 = (bf16[2,128,128]{2,1,0:T(8,128)(2,1)S(1)}, bf16[128,128]{1,0:T(8,128)(2,1)S(1)}, f32[3,128,128]{2,1,0:T(8,128)S(1)}, bf16[128,128]{1,0:T(8,128)(2,1)}) custom-call(s32[24,128]{1,0:T(8,128)S(1)} %get-tuple-element.27.table, bf16[3,144,128]{2,1,0:T(8,128)(2,1)S(1)} %pad_maximum_fusion.own_row, ...), custom_call_target="tpu_custom_call" | custom-call | tf_op jit(solution)/shard_map/late/pallas_call | solution.py:334
  20.3 0.1 collective-permute-start.7
  20.3 0.5 %collective-permute-start.6 = (bf16[128,128]{1,0:T(8,128)(2,1)S(1)}, bf16[128,128]{1,0:T(8,128)(2,1)S(1)}, u32[]{:S(2)}, u32[]{:S(2)}) collective-permute-start(bf16[128,128]{1,0:T(8,128)(2,1)S(1)} %get-tuple-element.45), channel_id=1, source_target_pairs={{0,1},{1,0},{2,3},{3,2},{4,5},{5,4},{6,7},{7,6},{8,9},{9,8},{10,11... | collective-permute-start | bytes 98312 | tf_op jit(solution)/shard_map/ppermute | solution.py:33
  20.8 0.6 %collective-permute-start.5 = (bf16[128,128]{1,0:T(8,128)(2,1)S(1)}, bf16[128,128]{1,0:T(8,128)(2,1)S(1)}, u32[]{:S(2)}, u32[]{:S(2)}) collective-permute-start(bf16[128,128]{1,0:T(8,128)(2,1)S(1)} %get-tuple-element.44), channel_id=1, source_target_pairs={{1,2},{2,1},{3,4},{4,3},{5,6},{6,5},{7,0},{0,7},{9,10},{10,9},{11,... | collective-permute-start | bytes 98312 | tf_op jit(solution)/shard_map/ppermute | solution.py:33
  21.4 0.6 %collective-permute-done.8 = bf16[2,128,128]{2,1,0:T(8,128)(2,1)S(1)} collective-permute-done((bf16[2,128,128]{2,1,0:T(8,128)(2,1)S(1)}, bf16[2,128,128]{2,1,0:T(8,128)(2,1)S(1)}, u32[]{:S(2)}, u32[]{:S(2)}) %collective-permute-start.8) | collective-permute-done | bytes 65568 | tf_op jit(solution)/shard_map/ppermute | solution.py:33
  22.0 0.0 collective-permute-done.7
  22.1 1.7 %collective-permute-start.9 = (bf16[128,128]{1,0:T(8,128)(2,1)S(1)}, bf16[128,128]{1,0:T(8,128)(2,1)S(1)}, u32[]{:S(2)}, u32[]{:S(2)}) collective-permute-start(bf16[128,128]{1,0:T(8,128)(2,1)S(1)} %get-tuple-element.51), channel_id=1, source_target_pairs={{8,16},{16,8},{24,0},{0,24},{9,17},{17,9},{25,1},{1,25},{10,18},{1... | collective-permute-start | bytes 98312 | tf_op jit(solution)/shard_map/ppermute | solution.py:33
  23.8 0.2 collective-permute-start.10
  24.0 0.0 collective-permute-done.6
  24.0 2.0 %collective-permute-done.5 = bf16[128,128]{1,0:T(8,128)(2,1)S(1)} collective-permute-done((bf16[128,128]{1,0:T(8,128)(2,1)S(1)}, bf16[128,128]{1,0:T(8,128)(2,1)S(1)}, u32[]{:S(2)}, u32[]{:S(2)}) %collective-permute-start.5) | collective-permute-done | bytes 32800 | tf_op jit(solution)/shard_map/ppermute | solution.py:33
  26.0 1.0 %collective-permute-done.9 = bf16[128,128]{1,0:T(8,128)(2,1)S(1)} collective-permute-done((bf16[128,128]{1,0:T(8,128)(2,1)S(1)}, bf16[128,128]{1,0:T(8,128)(2,1)S(1)}, u32[]{:S(2)}, u32[]{:S(2)}) %collective-permute-start.9) | collective-permute-done | bytes 32800 | tf_op jit(solution)/shard_map/ppermute | solution.py:33
  27.0 0.7 %collective-permute-done.10 = bf16[128,128]{1,0:T(8,128)(2,1)S(1)} collective-permute-done((bf16[128,128]{1,0:T(8,128)(2,1)S(1)}, bf16[128,128]{1,0:T(8,128)(2,1)S(1)}, u32[]{:S(2)}, u32[]{:S(2)}) %collective-permute-start.10) | collective-permute-done | bytes 32800 | tf_op jit(solution)/shard_map/ppermute | solution.py:33
  27.7 0.7 %copy.10 = f32[1,1,128,128]{3,2,1,0:T(8,128)} copy(f32[1,1,128,128]{2,3,1,0:T(8,128)S(1)} %add_bitcast_fusion) | data formatting | bytes 131072
  (9 shorter events, 0.1 us)
Async XLA Ops:
  1.4 7.0 %collective-permute-start.1 = (bf16[1,144,128]{2,1,0:T(8,128)(2,1)S(1)}, bf16[1,144,128]{2,1,0:T(8,128)(2,1)S(1)}, u32[]{:S(2)}, u32[]{:S(2)}) collective-permute-start(bf16[1,144,128]{2,1,0:T(8,128)(2,1)S(1)} %get-tuple-element.26), channel_id=1, source_target_pairs={{8,16},{16,8},{24,0},{0,24},{9,17},{17,9},{25,1},{1,25},{10,18},{1... | collective-permute-start | bytes 110600 | tf_op jit(solution)/shard_map/ppermute | solution.py:33
  5.4 4.0 %collective-permute-start = (bf16[1,144,128]{2,1,0:T(8,128)(2,1)S(1)}, bf16[1,144,128]{2,1,0:T(8,128)(2,1)S(1)}, u32[]{:S(2)}, u32[]{:S(2)}) collective-permute-start(bf16[1,144,128]{2,1,0:T(8,128)(2,1)S(1)} %get-tuple-element.26), channel_id=1, source_target_pairs={{0,8},{8,0},{16,24},{24,16},{1,9},{9,1},{17,25},{25,17},{2,10},{10... | collective-permute-start | bytes 110600 | tf_op jit(solution)/shard_map/ppermute | solution.py:33
  5.9 9.4 %collective-permute-start.4 = (bf16[1,144,128]{2,1,0:T(8,128)(2,1)S(1)}, bf16[1,144,128]{2,1,0:T(8,128)(2,1)S(1)}, u32[]{:S(2)}, u32[]{:S(2)}) collective-permute-start(bf16[1,144,128]{2,1,0:T(8,128)(2,1)S(1)} %get-tuple-element.26), channel_id=1, source_target_pairs={{1,2},{2,1},{3,4},{4,3},{5,6},{6,5},{7,0},{0,7},{9,10},{10,9},{11,... | collective-permute-start | bytes 110600 | tf_op jit(solution)/shard_map/ppermute | solution.py:33
  9.4 6.2 %collective-permute-start.3 = (bf16[2,144,128]{2,1,0:T(8,128)(2,1)S(1)}, bf16[2,144,128]{2,1,0:T(8,128)(2,1)S(1)}, u32[]{:S(2)}, u32[]{:S(2)}) collective-permute-start(bf16[2,144,128]{2,1,0:T(8,128)(2,1)S(1)} %get-tuple-element.52), channel_id=1, source_target_pairs={{1,2},{2,1},{3,4},{4,3},{5,6},{6,5},{7,0},{0,7},{9,10},{10,9},{11,... | collective-permute-start | bytes 221192 | tf_op jit(solution)/shard_map/ppermute | solution.py:33
  11.5 1.4 %collective-permute-start.2 = (bf16[3,144,128]{2,1,0:T(8,128)(2,1)S(1)}, bf16[3,144,128]{2,1,0:T(8,128)(2,1)S(1)}, u32[]{:S(2)}, u32[]{:S(2)}) collective-permute-start(bf16[3,144,128]{2,1,0:T(8,128)(2,1)S(1)} %pad_maximum_fusion.own_row), channel_id=1, source_target_pairs={{0,1},{1,0},{2,3},{3,2},{4,5},{5,4},{6,7},{7,6},{8,9},{9,8},{10,11... | collective-permute-start | bytes 331784 | tf_op jit(solution)/shard_map/ppermute | solution.py:33
  16.1 6.0 %collective-permute-start.8 = (bf16[2,128,128]{2,1,0:T(8,128)(2,1)S(1)}, bf16[2,128,128]{2,1,0:T(8,128)(2,1)S(1)}, u32[]{:S(2)}, u32[]{:S(2)}) collective-permute-start(bf16[2,128,128]{2,1,0:T(8,128)(2,1)S(1)} %get-tuple-element.47), channel_id=1, source_target_pairs={{1,2},{2,1},{3,4},{4,3},{5,6},{6,5},{7,0},{0,7},{9,10},{10,9},{11,... | collective-permute-start | bytes 196616 | tf_op jit(solution)/shard_map/ppermute | solution.py:33
  20.3 1.8 %collective-permute-start.7 = (bf16[2,128,128]{2,1,0:T(8,128)(2,1)S(1)}, bf16[2,128,128]{2,1,0:T(8,128)(2,1)S(1)}, u32[]{:S(2)}, u32[]{:S(2)}) collective-permute-start(bf16[2,128,128]{2,1,0:T(8,128)(2,1)S(1)} %get-tuple-element.46), channel_id=1, source_target_pairs={{0,1},{1,0},{2,3},{3,2},{4,5},{5,4},{6,7},{7,6},{8,9},{9,8},{10,11... | collective-permute-start | bytes 196616 | tf_op jit(solution)/shard_map/ppermute | solution.py:33
  20.3 3.7 %collective-permute-start.6 = (bf16[128,128]{1,0:T(8,128)(2,1)S(1)}, bf16[128,128]{1,0:T(8,128)(2,1)S(1)}, u32[]{:S(2)}, u32[]{:S(2)}) collective-permute-start(bf16[128,128]{1,0:T(8,128)(2,1)S(1)} %get-tuple-element.45), channel_id=1, source_target_pairs={{0,1},{1,0},{2,3},{3,2},{4,5},{5,4},{6,7},{7,6},{8,9},{9,8},{10,11... | collective-permute-start | bytes 98312 | tf_op jit(solution)/shard_map/ppermute | solution.py:33
  20.8 5.1 %collective-permute-start.5 = (bf16[128,128]{1,0:T(8,128)(2,1)S(1)}, bf16[128,128]{1,0:T(8,128)(2,1)S(1)}, u32[]{:S(2)}, u32[]{:S(2)}) collective-permute-start(bf16[128,128]{1,0:T(8,128)(2,1)S(1)} %get-tuple-element.44), channel_id=1, source_target_pairs={{1,2},{2,1},{3,4},{4,3},{5,6},{6,5},{7,0},{0,7},{9,10},{10,9},{11,... | collective-permute-start | bytes 98312 | tf_op jit(solution)/shard_map/ppermute | solution.py:33
  22.1 4.9 %collective-permute-start.9 = (bf16[128,128]{1,0:T(8,128)(2,1)S(1)}, bf16[128,128]{1,0:T(8,128)(2,1)S(1)}, u32[]{:S(2)}, u32[]{:S(2)}) collective-permute-start(bf16[128,128]{1,0:T(8,128)(2,1)S(1)} %get-tuple-element.51), channel_id=1, source_target_pairs={{8,16},{16,8},{24,0},{0,24},{9,17},{17,9},{25,1},{1,25},{10,18},{1... | collective-permute-start | bytes 98312 | tf_op jit(solution)/shard_map/ppermute | solution.py:33
  23.8 3.9 %collective-permute-start.10 = (bf16[128,128]{1,0:T(8,128)(2,1)S(1)}, bf16[128,128]{1,0:T(8,128)(2,1)S(1)}, u32[]{:S(2)}, u32[]{:S(2)}) collective-permute-start(bf16[128,128]{1,0:T(8,128)(2,1)S(1)} %get-tuple-element.50), channel_id=1, source_target_pairs={{0,8},{8,0},{16,24},{24,16},{1,9},{9,1},{17,25},{25,17},{2,10},{10... | collective-permute-start | bytes 98312 | tf_op jit(solution)/shard_map/ppermute | solution.py:33

commit v11 on v10

--- a/solution.py
+++ b/solution.py
@@ -95,10 +95,10 @@
     envelope = (1.0 - scaled) * (1.0 - scaled) * weight
     shifted = scaled - 0.5
     power = shifted * shifted
-    sine = jnp.full_like(power, SINE[-1])
+    sine = jnp.full_like(power, -SINE[-1])
     for factor in SINE[-2::-1]:
-        sine = sine * power + factor
-    cosine = -(shifted * sine)
+        sine = sine * power - factor
+    cosine = shifted * sine
     twice = cosine + cosine
     before, now = envelope, envelope * cosine
     for k in range(degrees):

time: 28.8 us -> 28.5 us (0.990); the launches traced: 28.5 us -> 28.8 us
  starting transfers between devices: 14.9 us -> 16 us
  waiting for transfers between devices: 6.03 us -> 5.48 us
    ppermute x11, starting transfers between devices: 14.9 us -> 16 us  [swap(): return lax.ppermute(block, axis, pairs)]
    ppermute x11, waiting for transfers between devices: 6.03 us -> 5.48 us  [swap(): return lax.ppermute(block, axis, pairs)]
  transfers between devices with their start and end apart: 11 -> 11, of which waited for: 7 -> 7; matrix products, arithmetic and copies ran while one was open for 1% -> 1% of each run, Pallas kernels for 14% -> 13%
where the time goes in v11:
time: 28.5 us; the launch traced here: 28.8 us
  starting transfers between devices  16 us (56%)
  waiting for transfers between devices  5.48 us (19%)
  Pallas kernels  4.99 us (18%)
  between operations  1.39 us (5%)
  local copies, waits for them, and re-layouts  0.81 us (3%)
    ppermute x11, starting transfers between devices, swap(): return lax.ppermute(block, axis, pairs)  16 us
    ppermute x11, waiting for transfers between devices, swap(): return lax.ppermute(block, axis, pairs)  5.48 us
    pallas_call x4, Pallas kernels, local(): pl.pallas_call(kernel, out_shape=tuple((jax.ShapeDtypeStruct(*out) for ou...  4.99 us
    unnamed x1, local copies, waits for them, and re-layouts  0.73 us
  transfers between devices with their start and end apart: 11, of which 7 were waited for; matrix products, arithmetic and copies ran while one was open for 1% of the time, Pallas kernels for 13%

profile of v11, /device:TPU:0, one launch (start us, length us, event | category | flops | bytes accessed | tf_op | source)
XLA Modules:
  0.0 28.8 jit_solution(9951499587928899313)
XLA Ops:
  0.6 0.8 %pack.1 = (bf16[1,144,128]{2,1,0:T(8,128)(2,1)S(1)}, s32[1,1,1,8]{3,2,1,0:T(1,128)S(1)}) custom-call(bf16[1,1,128,128]{3,2,1,0:T(8,128)(2,1)} %feat_ref.1, bf16[1,1,3,128]{3,2,1,0:T(4,128)(2,1)} %pos_ref.1, s32[1,1,1,8]{3,2,1,0:T(1,128)} %senders_ref.1), custom_call_target="tpu_custom_call" | custom-call | tf_op jit(solution)/shard_map/pack/pallas_call | solution.py:334
  1.4 4.0 %collective-permute-start.1 = (bf16[1,144,128]{2,1,0:T(8,128)(2,1)S(1)}, bf16[1,144,128]{2,1,0:T(8,128)(2,1)S(1)}, u32[]{:S(2)}, u32[]{:S(2)}) collective-permute-start(bf16[1,144,128]{2,1,0:T(8,128)(2,1)S(1)} %get-tuple-element.26), channel_id=1, source_target_pairs={{8,16},{16,8},{24,0},{0,24},{9,17},{17,9},{25,1},{1,25},{10,18},{1... | collective-permute-start | bytes 110600 | tf_op jit(solution)/shard_map/ppermute | solution.py:33
  5.4 0.5 %collective-permute-start = (bf16[1,144,128]{2,1,0:T(8,128)(2,1)S(1)}, bf16[1,144,128]{2,1,0:T(8,128)(2,1)S(1)}, u32[]{:S(2)}, u32[]{:S(2)}) collective-permute-start(bf16[1,144,128]{2,1,0:T(8,128)(2,1)S(1)} %get-tuple-element.26), channel_id=1, source_target_pairs={{0,8},{8,0},{16,24},{24,16},{1,9},{9,1},{17,25},{25,17},{2,10},{10... | collective-permute-start | bytes 110600 | tf_op jit(solution)/shard_map/ppermute | solution.py:33
  5.9 2.5 %collective-permute-start.4 = (bf16[1,144,128]{2,1,0:T(8,128)(2,1)S(1)}, bf16[1,144,128]{2,1,0:T(8,128)(2,1)S(1)}, u32[]{:S(2)}, u32[]{:S(2)}) collective-permute-start(bf16[1,144,128]{2,1,0:T(8,128)(2,1)S(1)} %get-tuple-element.26), channel_id=1, source_target_pairs={{1,2},{2,1},{3,4},{4,3},{5,6},{6,5},{7,0},{0,7},{9,10},{10,9},{11,... | collective-permute-start | bytes 110600 | tf_op jit(solution)/shard_map/ppermute | solution.py:33
  8.4 0.0 collective-permute-done.1
  8.4 0.9 %collective-permute-done = bf16[1,144,128]{2,1,0:T(8,128)(2,1)S(1)} collective-permute-done((bf16[1,144,128]{2,1,0:T(8,128)(2,1)S(1)}, bf16[1,144,128]{2,1,0:T(8,128)(2,1)S(1)}, u32[]{:S(2)}, u32[]{:S(2)}) %collective-permute-start) | collective-permute-done | bytes 36896 | tf_op jit(solution)/shard_map/ppermute | solution.py:33
  9.4 2.2 %collective-permute-start.3 = (bf16[2,144,128]{2,1,0:T(8,128)(2,1)S(1)}, bf16[2,144,128]{2,1,0:T(8,128)(2,1)S(1)}, u32[]{:S(2)}, u32[]{:S(2)}) collective-permute-start(bf16[2,144,128]{2,1,0:T(8,128)(2,1)S(1)} %get-tuple-element.52), channel_id=1, source_target_pairs={{1,2},{2,1},{3,4},{4,3},{5,6},{6,5},{7,0},{0,7},{9,10},{10,9},{11,... | collective-permute-start | bytes 221192 | tf_op jit(solution)/shard_map/ppermute | solution.py:33
  11.5 0.1 collective-permute-start.2
  11.6 0.1 pad_add_fusion
  12.4 0.6 %collective-permute-done.2.near_row = bf16[3,144,128]{2,1,0:T(8,128)(2,1)S(1)} collective-permute-done((bf16[3,144,128]{2,1,0:T(8,128)(2,1)S(1)}, bf16[3,144,128]{2,1,0:T(8,128)(2,1)S(1)}, u32[]{:S(2)}, u32[]{:S(2)}) %collective-permute-start.2) | collective-permute-done | bytes 110624 | tf_op jit(solution)/shard_map/ppermute | solution.py:33
  12.9 0.1 broadcast_in_dim.19.steps
  13.0 2.1 %early.1 = (s32[24,128]{1,0:T(8,128)S(1)}, bf16[1024,768]{1,0:T(8,128)(2,1)S(1)}, f32[5,128,128]{2,1,0:T(8,128)S(1)}, bf16[128,128]{1,0:T(8,128)(2,1)S(1)}, f32[...) custom-call(s32[8,128]{1,0:T(8,128)S(1)} %broadcast_in_dim.19.steps,, ...), custom_call_target="tpu_custom_call" | custom-call | tf_op jit(solution)/shard_map/early/pallas_call | solution.py:334
  15.1 0.0 collective-permute-done.4.far_own
  15.1 0.4 %collective-permute-done.3.far_sides = bf16[2,144,128]{2,1,0:T(8,128)(2,1)S(1)} collective-permute-done((bf16[2,144,128]{2,1,0:T(8,128)(2,1)S(1)}, bf16[2,144,128]{2,1,0:T(8,128)(2,1)S(1)}, u32[]{:S(2)}, u32[]{:S(2)}) %collective-permute-start.3) | collective-permute-done | bytes 73760 | tf_op jit(solution)/shard_map/ppermute | solution.py:33
  15.5 0.5 %middle.1 = (bf16[2,128,128]{2,1,0:T(8,128)(2,1)S(1)}, bf16[128,128]{1,0:T(8,128)(2,1)S(1)}, bf16[512,1024]{1,0:T(8,128)(2,1)S(1)}, bf16[128,128]{1,0:T(8,128)(2,1)S(1)}, bf16[384,128]{1,0:T(8,128)(2,1)S(1)}) custom-call(s32[24,128]{1,0:T(8,128)S(1)} %get-tuple-element.27.table, bf16[2,144,128]{2,1,0:T(8,128)(2,1)S(1)} %collective-permute-done.3.far_sides, ...), custom_call_target="tpu_custom_call" | custom-call | tf_op jit(solution)/shard_map/middle/pallas_call | solution.py:334
  16.1 1.6 %collective-permute-start.8 = (bf16[2,128,128]{2,1,0:T(8,128)(2,1)S(1)}, bf16[2,128,128]{2,1,0:T(8,128)(2,1)S(1)}, u32[]{:S(2)}, u32[]{:S(2)}) collective-permute-start(bf16[2,128,128]{2,1,0:T(8,128)(2,1)S(1)} %get-tuple-element.47), channel_id=1, source_target_pairs={{1,2},{2,1},{3,4},{4,3},{5,6},{6,5},{7,0},{0,7},{9,10},{10,9},{11,... | collective-permute-start | bytes 196616 | tf_op jit(solution)/shard_map/ppermute | solution.py:33
  17.7 1.6 %late.1 = (bf16[2,128,128]{2,1,0:T(8,128)(2,1)S(1)}, bf16[128,128]{1,0:T(8,128)(2,1)S(1)}, f32[3,128,128]{2,1,0:T(8,128)S(1)}, bf16[128,128]{1,0:T(8,128)(2,1)}) custom-call(s32[24,128]{1,0:T(8,128)S(1)} %get-tuple-element.27.table, bf16[3,144,128]{2,1,0:T(8,128)(2,1)S(1)} %pad_maximum_fusion.own_row, ...), custom_call_target="tpu_custom_call" | custom-call | tf_op jit(solution)/shard_map/late/pallas_call | solution.py:334
  19.3 0.1 collective-permute-start.7
  19.4 0.5 %collective-permute-start.6 = (bf16[128,128]{1,0:T(8,128)(2,1)S(1)}, bf16[128,128]{1,0:T(8,128)(2,1)S(1)}, u32[]{:S(2)}, u32[]{:S(2)}) collective-permute-start(bf16[128,128]{1,0:T(8,128)(2,1)S(1)} %get-tuple-element.45), channel_id=1, source_target_pairs={{0,1},{1,0},{2,3},{3,2},{4,5},{5,4},{6,7},{7,6},{8,9},{9,8},{10,11... | collective-permute-start | bytes 98312 | tf_op jit(solution)/shard_map/ppermute | solution.py:33
  19.9 1.5 %collective-permute-start.5 = (bf16[128,128]{1,0:T(8,128)(2,1)S(1)}, bf16[128,128]{1,0:T(8,128)(2,1)S(1)}, u32[]{:S(2)}, u32[]{:S(2)}) collective-permute-start(bf16[128,128]{1,0:T(8,128)(2,1)S(1)} %get-tuple-element.44), channel_id=1, source_target_pairs={{1,2},{2,1},{3,4},{4,3},{5,6},{6,5},{7,0},{0,7},{9,10},{10,9},{11,... | collective-permute-start | bytes 98312 | tf_op jit(solution)/shard_map/ppermute | solution.py:33
  21.4 0.4 %collective-permute-done.8 = bf16[2,128,128]{2,1,0:T(8,128)(2,1)S(1)} collective-permute-done((bf16[2,128,128]{2,1,0:T(8,128)(2,1)S(1)}, bf16[2,128,128]{2,1,0:T(8,128)(2,1)S(1)}, u32[]{:S(2)}, u32[]{:S(2)}) %collective-permute-start.8) | collective-permute-done | bytes 65568 | tf_op jit(solution)/shard_map/ppermute | solution.py:33
  21.8 0.0 collective-permute-done.7
  21.9 2.3 %collective-permute-start.9 = (bf16[128,128]{1,0:T(8,128)(2,1)S(1)}, bf16[128,128]{1,0:T(8,128)(2,1)S(1)}, u32[]{:S(2)}, u32[]{:S(2)}) collective-permute-start(bf16[128,128]{1,0:T(8,128)(2,1)S(1)} %get-tuple-element.51), channel_id=1, source_target_pairs={{8,16},{16,8},{24,0},{0,24},{9,17},{17,9},{25,1},{1,25},{10,18},{1... | collective-permute-start | bytes 98312 | tf_op jit(solution)/shard_map/ppermute | solution.py:33
  24.2 0.8 %collective-permute-start.10 = (bf16[128,128]{1,0:T(8,128)(2,1)S(1)}, bf16[128,128]{1,0:T(8,128)(2,1)S(1)}, u32[]{:S(2)}, u32[]{:S(2)}) collective-permute-start(bf16[128,128]{1,0:T(8,128)(2,1)S(1)} %get-tuple-element.50), channel_id=1, source_target_pairs={{0,8},{8,0},{16,24},{24,16},{1,9},{9,1},{17,25},{25,17},{2,10},{10... | collective-permute-start | bytes 98312 | tf_op jit(solution)/shard_map/ppermute | solution.py:33
  24.9 0.0 collective-permute-done.6
  24.9 0.1 collective-permute-done.5
  25.0 1.7 %collective-permute-done.9 = bf16[128,128]{1,0:T(8,128)(2,1)S(1)} collective-permute-done((bf16[128,128]{1,0:T(8,128)(2,1)S(1)}, bf16[128,128]{1,0:T(8,128)(2,1)S(1)}, u32[]{:S(2)}, u32[]{:S(2)}) %collective-permute-start.9) | collective-permute-done | bytes 32800 | tf_op jit(solution)/shard_map/ppermute | solution.py:33
  26.8 1.3 %collective-permute-done.10 = bf16[128,128]{1,0:T(8,128)(2,1)S(1)} collective-permute-done((bf16[128,128]{1,0:T(8,128)(2,1)S(1)}, bf16[128,128]{1,0:T(8,128)(2,1)S(1)}, u32[]{:S(2)}, u32[]{:S(2)}) %collective-permute-start.10) | collective-permute-done | bytes 32800 | tf_op jit(solution)/shard_map/ppermute | solution.py:33
  28.1 0.7 %copy.10 = f32[1,1,128,128]{3,2,1,0:T(8,128)} copy(f32[1,1,128,128]{2,3,1,0:T(8,128)S(1)} %add_bitcast_fusion) | data formatting | bytes 131072
  (9 shorter events, 0.1 us)
Async XLA Ops:
  1.4 7.0 %collective-permute-start.1 = (bf16[1,144,128]{2,1,0:T(8,128)(2,1)S(1)}, bf16[1,144,128]{2,1,0:T(8,128)(2,1)S(1)}, u32[]{:S(2)}, u32[]{:S(2)}) collective-permute-start(bf16[1,144,128]{2,1,0:T(8,128)(2,1)S(1)} %get-tuple-element.26), channel_id=1, source_target_pairs={{8,16},{16,8},{24,0},{0,24},{9,17},{17,9},{25,1},{1,25},{10,18},{1... | collective-permute-start | bytes 110600 | tf_op jit(solution)/shard_map/ppermute | solution.py:33
  5.4 4.0 %collective-permute-start = (bf16[1,144,128]{2,1,0:T(8,128)(2,1)S(1)}, bf16[1,144,128]{2,1,0:T(8,128)(2,1)S(1)}, u32[]{:S(2)}, u32[]{:S(2)}) collective-permute-start(bf16[1,144,128]{2,1,0:T(8,128)(2,1)S(1)} %get-tuple-element.26), channel_id=1, source_target_pairs={{0,8},{8,0},{16,24},{24,16},{1,9},{9,1},{17,25},{25,17},{2,10},{10... | collective-permute-start | bytes 110600 | tf_op jit(solution)/shard_map/ppermute | solution.py:33
  5.9 9.2 %collective-permute-start.4 = (bf16[1,144,128]{2,1,0:T(8,128)(2,1)S(1)}, bf16[1,144,128]{2,1,0:T(8,128)(2,1)S(1)}, u32[]{:S(2)}, u32[]{:S(2)}) collective-permute-start(bf16[1,144,128]{2,1,0:T(8,128)(2,1)S(1)} %get-tuple-element.26), channel_id=1, source_target_pairs={{1,2},{2,1},{3,4},{4,3},{5,6},{6,5},{7,0},{0,7},{9,10},{10,9},{11,... | collective-permute-start | bytes 110600 | tf_op jit(solution)/shard_map/ppermute | solution.py:33
  9.4 6.2 %collective-permute-start.3 = (bf16[2,144,128]{2,1,0:T(8,128)(2,1)S(1)}, bf16[2,144,128]{2,1,0:T(8,128)(2,1)S(1)}, u32[]{:S(2)}, u32[]{:S(2)}) collective-permute-start(bf16[2,144,128]{2,1,0:T(8,128)(2,1)S(1)} %get-tuple-element.52), channel_id=1, source_target_pairs={{1,2},{2,1},{3,4},{4,3},{5,6},{6,5},{7,0},{0,7},{9,10},{10,9},{11,... | collective-permute-start | bytes 221192 | tf_op jit(solution)/shard_map/ppermute | solution.py:33
  11.5 1.4 %collective-permute-start.2 = (bf16[3,144,128]{2,1,0:T(8,128)(2,1)S(1)}, bf16[3,144,128]{2,1,0:T(8,128)(2,1)S(1)}, u32[]{:S(2)}, u32[]{:S(2)}) collective-permute-start(bf16[3,144,128]{2,1,0:T(8,128)(2,1)S(1)} %pad_maximum_fusion.own_row), channel_id=1, source_target_pairs={{0,1},{1,0},{2,3},{3,2},{4,5},{5,4},{6,7},{7,6},{8,9},{9,8},{10,11... | collective-permute-start | bytes 331784 | tf_op jit(solution)/shard_map/ppermute | solution.py:33
  16.1 5.7 %collective-permute-start.8 = (bf16[2,128,128]{2,1,0:T(8,128)(2,1)S(1)}, bf16[2,128,128]{2,1,0:T(8,128)(2,1)S(1)}, u32[]{:S(2)}, u32[]{:S(2)}) collective-permute-start(bf16[2,128,128]{2,1,0:T(8,128)(2,1)S(1)} %get-tuple-element.47), channel_id=1, source_target_pairs={{1,2},{2,1},{3,4},{4,3},{5,6},{6,5},{7,0},{0,7},{9,10},{10,9},{11,... | collective-permute-start | bytes 196616 | tf_op jit(solution)/shard_map/ppermute | solution.py:33
  19.3 2.5 %collective-permute-start.7 = (bf16[2,128,128]{2,1,0:T(8,128)(2,1)S(1)}, bf16[2,128,128]{2,1,0:T(8,128)(2,1)S(1)}, u32[]{:S(2)}, u32[]{:S(2)}) collective-permute-start(bf16[2,128,128]{2,1,0:T(8,128)(2,1)S(1)} %get-tuple-element.46), channel_id=1, source_target_pairs={{0,1},{1,0},{2,3},{3,2},{4,5},{5,4},{6,7},{7,6},{8,9},{9,8},{10,11... | collective-permute-start | bytes 196616 | tf_op jit(solution)/shard_map/ppermute | solution.py:33
  19.4 5.6 %collective-permute-start.6 = (bf16[128,128]{1,0:T(8,128)(2,1)S(1)}, bf16[128,128]{1,0:T(8,128)(2,1)S(1)}, u32[]{:S(2)}, u32[]{:S(2)}) collective-permute-start(bf16[128,128]{1,0:T(8,128)(2,1)S(1)} %get-tuple-element.45), channel_id=1, source_target_pairs={{0,1},{1,0},{2,3},{3,2},{4,5},{5,4},{6,7},{7,6},{8,9},{9,8},{10,11... | collective-permute-start | bytes 98312 | tf_op jit(solution)/shard_map/ppermute | solution.py:33
  19.9 5.1 %collective-permute-start.5 = (bf16[128,128]{1,0:T(8,128)(2,1)S(1)}, bf16[128,128]{1,0:T(8,128)(2,1)S(1)}, u32[]{:S(2)}, u32[]{:S(2)}) collective-permute-start(bf16[128,128]{1,0:T(8,128)(2,1)S(1)} %get-tuple-element.44), channel_id=1, source_target_pairs={{1,2},{2,1},{3,4},{4,3},{5,6},{6,5},{7,0},{0,7},{9,10},{10,9},{11,... | collective-permute-start | bytes 98312 | tf_op jit(solution)/shard_map/ppermute | solution.py:33
  21.9 4.9 %collective-permute-start.9 = (bf16[128,128]{1,0:T(8,128)(2,1)S(1)}, bf16[128,128]{1,0:T(8,128)(2,1)S(1)}, u32[]{:S(2)}, u32[]{:S(2)}) collective-permute-start(bf16[128,128]{1,0:T(8,128)(2,1)S(1)} %get-tuple-element.51), channel_id=1, source_target_pairs={{8,16},{16,8},{24,0},{0,24},{9,17},{17,9},{25,1},{1,25},{10,18},{1... | collective-permute-start | bytes 98312 | tf_op jit(solution)/shard_map/ppermute | solution.py:33
  24.2 3.9 %collective-permute-start.10 = (bf16[128,128]{1,0:T(8,128)(2,1)S(1)}, bf16[128,128]{1,0:T(8,128)(2,1)S(1)}, u32[]{:S(2)}, u32[]{:S(2)}) collective-permute-start(bf16[128,128]{1,0:T(8,128)(2,1)S(1)} %get-tuple-element.50), channel_id=1, source_target_pairs={{0,8},{8,0},{16,24},{24,16},{1,9},{9,1},{17,25},{25,17},{2,10},{10... | collective-permute-start | bytes 98312 | tf_op jit(solution)/shard_map/ppermute | solution.py:33
